TPU v7x, 32 devices: a whole 2x2x4 slice. The times are simulated.
32 devices in a mesh: rows: 8 (over z, x), lev: 4 (over y, core).
Axes of the slice: x: 2, y: 2, z: 4, core: 2. Of those that a mesh axis runs over, the one named last changes fastest.
Arguments:
- source: float32 [2048, 16, 2048], P('rows', 'lev'), may hold values from -40 to 40
- solid: int32 [256, 16, 32], P('rows', 'lev'), may hold values 0 or 1
- couplings: float32 [17], replicated, may hold values from 2 to 8
Outputs:
- pressure: float32 [2048, 16, 2048], P('rows', 'lev')
Inputs may be any that keep to these rules, and one draw needn't show every extreme that they name: Each entry is 0 or 1; 1 marks a block of 8 x 64 cells of one level inside a solid.
All inputs are finite; a program needn't handle non-finite values.
Results may differ from a plain program's by a relative error of at most 0.0001.
Values sent between devices are 32-bit elements; how exact they have to be, the bound alone decides.
A program may use at most 192 MiB of HBM per device.

v0:
```python
import math

import jax
import jax.numpy as jnp
from jax import lax
from jax.sharding import PartitionSpec as P

BY = 8
BX = 64


full_turn = 2.0 * math.pi
highest = lax.Precision.HIGHEST


def shifted(value, axis, steps):
    count = lax.axis_size(axis)
    first, last = (max(0, -steps), min(count, count - steps))
    return lax.ppermute(value, axis, [(source, source + steps) for source in range(first, last)])


def product(form, left, right):
    return jnp.einsum(form, left, right, precision=highest, preferred_element_type=jnp.float32)


def tables(length):
    fine_size = 32
    coarse_size = length // fine_size
    coarse = jnp.arange(coarse_size, dtype=jnp.int32)
    fine = jnp.arange(fine_size, dtype=jnp.int32)
    angle_first = jnp.mod(coarse[:, None] * coarse[None, :], coarse_size).astype(jnp.float32) * (
        full_turn / coarse_size
    )
    first_table = jnp.concatenate([jnp.cos(angle_first), jnp.sin(angle_first)], 0)
    upper_rows = jnp.arange(fine_size // 2, dtype=jnp.int32)
    angle_last = jnp.mod(upper_rows[:, None] * fine[None, :], fine_size).astype(jnp.float32) * (
        full_turn / fine_size
    )
    cos_table = jnp.cos(angle_last)
    sin_table = jnp.sin(angle_last)
    angle_twist = jnp.mod(coarse[:, None] * fine[None, :], length).astype(jnp.float32) * (
        full_turn / length
    )
    twist_cos = jnp.cos(angle_twist)[:, :, None]
    twist_sin = jnp.sin(angle_twist)[:, :, None]
    alternating = (1 - 2 * jnp.mod(fine, 2)).astype(jnp.float32)
    nyquist_row = jnp.where(coarse[:, None] == 0, alternating[None, :], 0.0)[:, :, None]
    slots = jnp.arange(length, dtype=jnp.int32)
    edge = (slots == 0) | (slots == length // 2)
    weights = jnp.where(edge, math.sqrt(1.0 / length), math.sqrt(2.0 / length)).astype(jnp.float32)
    return (
        fine_size,
        coarse_size,
        first_table,
        cos_table,
        sin_table,
        twist_cos,
        twist_sin,
        alternating,
        nyquist_row,
        weights,
    )


def finish(segment_one, lookup):
    (
        fine_size,
        coarse_size,
        first_table,
        cos_table,
        sin_table,
        twist_cos,
        twist_sin,
        alternating,
        nyquist_row,
        weights,
    ) = lookup
    batch_size = segment_one.shape[2]
    real_first = segment_one[:coarse_size]
    imag_first = -segment_one[coarse_size:]
    nyquist = jnp.sum(real_first[0] * alternating[:, None], axis=0)
    real_twisted = real_first * twist_cos + imag_first * twist_sin
    imag_twisted = imag_first * twist_cos - real_first * twist_sin
    real_final = (
        product("fjb,gj->bgf", real_twisted, cos_table)
        + product("fjb,gj->bgf", imag_twisted, sin_table)
    ).reshape(batch_size, -1)
    imag_final = (
        product("fjb,gj->bgf", imag_twisted, cos_table)
        - product("fjb,gj->bgf", real_twisted, sin_table)
    ).reshape(batch_size, -1)
    leading = jnp.arange(real_final.shape[1]) == 0
    sine_half = jnp.where(leading[None, :], nyquist[:, None], -imag_final)
    return jnp.concatenate([real_final, sine_half], 1) * weights


def unfinish(packed, lookup):
    (
        fine_size,
        coarse_size,
        first_table,
        cos_table,
        sin_table,
        twist_cos,
        twist_sin,
        alternating,
        nyquist_row,
        weights,
    ) = lookup
    batch_size, length = packed.shape
    half_len = length // 2
    half_fine = fine_size // 2
    scaled = packed * weights
    cosine_half = scaled[:, :half_len]
    sine_half = scaled[:, half_len:]
    leading = jnp.arange(half_len) == 0
    back_real = cosine_half.reshape(batch_size, half_fine, coarse_size)
    back_imag = jnp.where(leading[None, :], 0.0, -sine_half).reshape(
        batch_size, half_fine, coarse_size
    )
    back_nyquist = sine_half[:, 0]
    twisted_real = product("bgf,gj->fjb", back_real, cos_table) - product(
        "bgf,gj->fjb", back_imag, sin_table
    )
    twisted_imag = product("bgf,gj->fjb", back_imag, cos_table) + product(
        "bgf,gj->fjb", back_real, sin_table
    )
    real_first = (
        twisted_real * twist_cos
        - twisted_imag * twist_sin
        + back_nyquist[None, None, :] * nyquist_row
    )
    imag_first = twisted_real * twist_sin + twisted_imag * twist_cos
    return jnp.concatenate([real_first, -imag_first], 0)


def forward_last(values, lookup):
    batch_size = values.shape[0]
    segment_one = product(
        "bkj,fk->fjb", values.reshape(batch_size, lookup[1], lookup[0]), lookup[2]
    )
    return finish(segment_one, lookup)


def inverse_last(packed, lookup):
    return product("fjb,fk->bkj", unfinish(packed, lookup), lookup[2]).reshape(packed.shape)


def forward_lead(pencil, lookup):
    length, levels, slab_width = pencil.shape
    segment_one = product(
        "kjr,fk->fjr", pencil.reshape(lookup[1], lookup[0], levels * slab_width), lookup[2]
    )
    return finish(segment_one, lookup).reshape(levels, slab_width, length)


def inverse_lead(packed, lookup):
    levels, slab_width, length = packed.shape
    segments = unfinish(packed.reshape(levels * slab_width, length), lookup)
    return product("fjr,fk->kjr", segments, lookup[2]).reshape(length, levels, slab_width)


def eigenvalue(slots, length):
    frequency = jnp.where(slots <= length // 2, slots, slots - length // 2)
    return 2.0 - 2.0 * jnp.cos(frequency.astype(jnp.float32) * (full_turn / length))


def section_solve(horizontal, part_couplings, spectrum):
    level_count = part_couplings.shape[0] - 1
    level_index = jnp.arange(level_count, dtype=jnp.int32)
    at_bottom = (level_index == 0).astype(jnp.float32)
    at_top = (level_index == level_count - 1).astype(jnp.float32)
    zero_plane = jnp.zeros(horizontal.shape, jnp.float32)
    has_source = spectrum is not None
    system_count = int(has_source) + 2 * int(True)

    def forward(carry, slices):
        pivot_ratio, partial_value = carry
        lower_w, upper_w, bottom_flag, top_flag, source_level = slices
        inverse = 1.0 / (horizontal + lower_w + upper_w - lower_w * pivot_ratio)
        updated = []
        updated.append((source_level + lower_w * partial_value[0]) * inverse)
        shift_pos = len(updated)
        updated.append(lower_w * (bottom_flag + partial_value[shift_pos]) * inverse)
        updated.append((upper_w * top_flag + lower_w * partial_value[shift_pos + 1]) * inverse)
        ratio = upper_w * inverse
        return ((ratio, tuple(updated)), (ratio, tuple(updated)))

    sweep_in = (part_couplings[:-1], part_couplings[1:], at_bottom, at_top, spectrum)
    unused, (ratios, partials) = lax.scan(
        forward, (zero_plane, (zero_plane,) * system_count), sweep_in
    )

    def backward(upper_values, slices):
        ratio, partial_value = slices
        current = tuple(
            (value + ratio * above for value, above in zip(partial_value, upper_values))
        )
        return (current, current)

    unused, solutions = lax.scan(
        backward, (zero_plane,) * system_count, (ratios, partials), reverse=True
    )
    return solutions


def chain_ends(particular, lower_part, upper_part, lev_devices):
    first_u = particular[0]
    top_u = particular[-1]
    first_a = lower_part[0]
    top_a = lower_part[-1]
    first_b = upper_part[0]
    top_b = upper_part[-1]

    def relation(incoming):
        offset_in = incoming[0]
        factor_in = incoming[1]
        scale_inv = 1.0 / (1.0 - first_a * factor_in)
        first_offset = (first_u + first_a * offset_in) * scale_inv
        first_factor = first_b * scale_inv
        offset_out = top_u + top_a * (offset_in + factor_in * first_offset)
        factor_out = top_a * factor_in * first_factor + top_b
        return (first_offset, first_factor, jnp.stack([offset_out, factor_out]))

    incoming = jnp.zeros((2,) + first_u.shape, jnp.float32)
    for round_index in range(lev_devices - 1):
        outgoing = relation(incoming)[2]
        incoming = shifted(outgoing, "lev", 1)
    first_offset, first_factor, unused = relation(incoming)
    above_value = jnp.zeros_like(first_u)
    for round_index in range(lev_devices - 1):
        above_value = shifted(first_offset + first_factor * above_value, "lev", -1)
    first_value = first_offset + first_factor * above_value
    below_value = incoming[0] + incoming[1] * first_value
    return (below_value, above_value)


def body(source, solid, couplings):
    row_count, level_count, cell_count = source.shape
    keep_cells = (1 - solid).astype(jnp.float32)
    masked_cells = (
        source.reshape(row_count // BY, BY, level_count, cell_count // BX, BX)
        * keep_cells[:, None, :, :, None]
    ).reshape(row_count * level_count, cell_count)
    lookup_x = tables(cell_count)
    spectral = forward_last(masked_cells, lookup_x).reshape(row_count, level_count, cell_count)
    row_devices = lax.axis_size("rows")
    lev_devices = lax.axis_size("lev")
    total_rows = row_count * row_devices
    lookup_y = tables(total_rows)
    row_eigen = eigenvalue(jnp.arange(total_rows, dtype=jnp.int32), total_rows)
    spectrum = forward_lead(
        lax.all_to_all(spectral, "rows", split_axis=2, concat_axis=0, tiled=True), lookup_y
    )
    slab_width = cell_count // row_devices
    slots = lax.axis_index("rows") * slab_width + jnp.arange(slab_width, dtype=jnp.int32)
    horizontal = eigenvalue(slots, cell_count)[:, None] + row_eigen[None, :]
    own_section = lax.axis_index("lev")
    local_couplings = lax.dynamic_slice_in_dim(
        couplings, own_section * level_count, level_count + 1
    )
    particular, lower_part, upper_part = section_solve(horizontal, local_couplings, spectrum)
    below_value, above_value = chain_ends(particular, lower_part, upper_part, lev_devices)
    pressure_spectrum = particular + lower_part * below_value + upper_part * above_value
    physical = inverse_lead(pressure_spectrum, lookup_y)
    pencil = lax.all_to_all(physical, "rows", split_axis=0, concat_axis=2, tiled=True)
    rows_here, levels_here, cells_here = pencil.shape
    return inverse_last(pencil.reshape(rows_here * levels_here, cells_here), lookup_x).reshape(
        pencil.shape
    )


def solution(mesh):
    return jax.shard_map(
        body,
        mesh=mesh,
        in_specs=(P("rows", "lev", None), P("rows", "lev", None), P()),
        out_specs=P("rows", "lev", None),
        check_vma=False,
    )
```

profile of v0, /device:TPU:0, one launch (start us, length us, event | category | flops | bytes accessed | tf_op | source)
XLA Modules:
  0.0 1420.4 jit_solution(7903789285727864139)
XLA Ops:
  0.3 22.2 %reshape.209 = f32[1024,64,32]{2,1,0:T(8,128)} reshape(f32[256,4,2048]{2,1,0:T(4,128)} %param.7) | data formatting | bytes 16777216 | tf_op jit(solution)/shard_map/reshape | solution.py:242
  27.6 8.4 mul.826
  36.1 23.1 %broadcast_multiply_fusion.1 = f32[1024,64,32]{2,1,0:T(8,128)} fusion(f32[1024,64,32]{2,1,0:T(8,128)} %reshape.209, f32[1024,64]{1,0:T(8,128)S(1)} %copy.189), kind=kLoop, calls=%fused_computation.38 | loop fusion | flops 2097152 | bytes 17039360 | tf_op jit(solution)/shard_map/mul | solution.py:242
  59.2 22.8 %copy.190 = f32[1024,64,32]{0,1,2:T(8,128)} copy(f32[1024,64,32]{2,1,0:T(8,128)} %broadcast_multiply_fusion.1) | data formatting | bytes 16777216 | tf_op jit(solution)/shard_map/mul | solution.py:242
  82.1 20.7 %convolution_bitcast_fusion = f32[128,32,1024]{2,0,1:T(8,128)S(1)} fusion(f32[128,64,1]{0,1,2:T(8,128)S(1)} %maximum_bitcast_fusion, f32[1024,64,32]{0,1,2:T(8,128)} %copy.190), kind=kOutput, calls=%fused_computation.39 | convolution fusion | flops 3221225472 | bytes 25198592 | tf_op jit(solution)/shard_map/bkj,fk->fjb/dot_general | solution.py:23
  108.6 7.2 multiply_add_fusion.2
  115.9 9.4 fusion.37
  125.2 9.7 fusion.39
  134.9 9.5 negate_bitcast_fusion.1
  144.5 8.7 copy.197
  153.1 8.2 neg.41
  161.6 14.5 %add_bitcast_fusion.1 = f32[1024,16,64]{0,1,2:T(8,128)} fusion(f32[16,64,1024]{2,0,1:T(8,128)} %fusion.39, f32[64,32,1024]{2,0,1:T(8,128)} %copy-done.1), kind=kOutput, calls=%fused_computation.100 | convolution fusion | flops 403708928 | bytes 16777216 | tf_op jit(solution)/shard_map/fjb,gj->bgf/dot_general | solution.py:23
  176.1 8.7 copy.193
  184.8 8.1 concatenate.23
  204.7 9.9 copy.200
  214.5 7.8 all-to-all-start
  222.7 182.7 %all-to-all-done = f32[256,4,2048]{0,1,2:T(4,128)} async-done(((f32[256,4,2048]{0,1,2:T(4,128)}), f32[256,4,2048]{0,1,2:T(4,128)}, u32[]{:S(2)}, u32[]{:S(2)}) %all-to-all-start) | async-done | bytes 8388640 | tf_op jit(solution)/shard_map/all_to_all | solution.py:253
  405.5 12.1 copy.201
  417.6 10.8 reshape.210
  428.3 24.4 %fusion.27 = f32[128,32,1024]{2,0,1:T(8,128)} fusion(f32[128,64,1]{0,1,2:T(8,128)S(1)} %maximum_bitcast_fusion, f32[64,32,1024]{2,1,0:T(8,128)} %reshape.210), kind=kOutput, calls=%fused_computation.64 | convolution fusion | flops 3221225472 | bytes 25198592 | tf_op jit(solution)/shard_map/kjr,fk->fjr/dot_general | solution.py:23
  452.7 7.2 multiply_add_fusion.1
  462.0 9.4 fusion.29
  471.3 9.5 fusion.31
  480.8 9.9 negate_bitcast_fusion
  501.3 13.5 add_bitcast_fusion
  530.8 14.6 %maximum_multiply_fusion.1 = f32[4,256,2048]{1,0,2:T(4,128)} fusion(f32[4,256,1024]{1,0,2:T(4,128)S(1)} %broadcast_select_fusion, f32[4,256,1024]{1,0,2:T(4,128)S(1)} %copy-done.6, f32[2048]{0:T(1024)S(1)} %fusion.125), kind=kLoop, calls=%fused_computation.43 | loop fusion | flops 4194304 | bytes 16785408 | tf_op jit(solution)/shard_map/mul | solution.py:94
  562.7 94.2 %while.50 = (s32[]{:T(128)}, f32[256,2048]{1,0:T(8,128)}, f32[256,2048]{1,0:T(8,128)}, f32[256,2048]{1,0:T(8,128)}, f32[256,2048]{1,0:T(8,128)}, /*index=5*/f32[...) while((s32[]{:T(128)}, f32[256,2048]{1,0:T(8,128)}, ...), condition=%wide.region_3.4_spmd.clone, body=%wide.region_2.3_spmd.clone.sunk | while | flops 10485764 | bytes 35663088 | solution.py:190
  575.9 9.4 bitcast_dynamic-update-slice_fusion.9
  598.5 10.6 bitcast_dynamic-update-slice_fusion.9
  622.3 10.6 bitcast_dynamic-update-slice_fusion.9
  646.2 10.7 bitcast_dynamic-update-slice_fusion.9
  669.9 37.2 %while.51 = (s32[]{:T(128)}, f32[256,2048]{1,0:T(8,128)S(1)}, f32[256,2048]{1,0:T(8,128)}, f32[256,2048]{1,0:T(8,128)}, f32[4,256,2048]{2,1,0:T(8,128)}, /*index...) while((s32[]{:T(128)}, f32[256,2048]{1,0:T(8,128)S(1)}, ...), condition=%wide.region_5.6_spmd.clone, body=%wide.region_4.5_spmd.clone.sunk | while | flops 4718596 | bytes 27263132 | solution.py:201
  669.9 8.4 bitcast_dynamic-update-slice_fusion.10
  678.3 9.6 bitcast_dynamic-update-slice_fusion.10
  687.9 9.6 bitcast_dynamic-update-slice_fusion.10
  697.4 9.6 bitcast_dynamic-update-slice_fusion.10
  715.6 6.5 collective-permute-done
  726.7 43.2 %collective-permute-start.1 = (f32[2,256,2048]{2,1,0:T(8,128)S(1)}, f32[2,256,2048]{2,1,0:T(8,128)S(1)}, u32[]{:S(2)}, u32[]{:S(2)}) collective-permute-start(f32[2,256,2048]{2,1,0:T(8,128)S(1)} %pad_maximum_fusion.1), channel_id=1, source_target_pairs={{0,1},{1,2},{2,3},{4,5},{5,6},{6,7},{8,9},{9,10},{10,11},{12,13},{... | collective-permute-start | bytes 12582920 | tf_op jit(solution)/shard_map/ppermute | solution.py:19
  769.9 6.5 collective-permute-done.1
  778.5 43.3 %collective-permute-start.2 = (f32[2,256,2048]{2,1,0:T(8,128)S(1)}, f32[2,256,2048]{2,1,0:T(8,128)S(1)}, u32[]{:S(2)}, u32[]{:S(2)}) collective-permute-start(f32[2,256,2048]{2,1,0:T(8,128)S(1)} %pad_maximum_fusion.2), channel_id=1, source_target_pairs={{0,1},{1,2},{2,3},{4,5},{5,6},{6,7},{8,9},{9,10},{10,11},{12,13},{... | collective-permute-start | bytes 12582920 | tf_op jit(solution)/shard_map/ppermute | solution.py:19
  833.0 45.4 %collective-permute-done.3 = f32[256,2048]{1,0:T(8,128)S(1)} collective-permute-done((f32[256,2048]{1,0:T(8,128)S(1)}, f32[256,2048]{1,0:T(8,128)S(1)}, u32[]{:S(2)}, u32[]{:S(2)}) %collective-permute-start.3) | collective-permute-done | bytes 2097184 | tf_op jit(solution)/shard_map/ppermute | solution.py:19
  880.3 26.8 %collective-permute-done.4 = f32[256,2048]{1,0:T(8,128)S(1)} collective-permute-done((f32[256,2048]{1,0:T(8,128)S(1)}, f32[256,2048]{1,0:T(8,128)S(1)}, u32[]{:S(2)}, u32[]{:S(2)}) %collective-permute-start.4) | collective-permute-done | bytes 2097184 | tf_op jit(solution)/shard_map/ppermute | solution.py:19
  909.0 26.0 %collective-permute-done.5 = f32[256,2048]{1,0:T(8,128)S(1)} collective-permute-done((f32[256,2048]{1,0:T(8,128)S(1)}, f32[256,2048]{1,0:T(8,128)S(1)}, u32[]{:S(2)}, u32[]{:S(2)}) %collective-permute-start.5) | collective-permute-done | bytes 2097184 | tf_op jit(solution)/shard_map/ppermute | solution.py:19
  937.4 10.6 multiply_add_fusion
  948.0 9.3 copy.233
  962.4 10.3 fusion.55
  972.7 10.4 fusion.57
  983.1 10.2 fusion.59
  993.3 10.3 fusion.61
  1003.6 35.6 %fusion.24 = (f32[64,32,1024]{2,0,1:T(8,128)}, f32[64,32,1024]{2,0,1:T(8,128)}) fusion(f32[64,32]{0,1:T(8,128)S(1)} %broadcast_select_fusion.1, f32[1024]{0:T(1024)S(1)} %bitcast.239, f32[64,32]{0,1:T(8,128)S(1)} %copy-done.10, f32[64,32]{0,1:T(8,128)S(1)} %copy-done.12, f32[32,1024,64]{1,0,2:T(8,128)} %fusion.57, f32[32,1024,64]{1,0,2:T(8,128)} %fusion.61, ...), kind=kLoop, calls=%fused_computation.55 | loop fusion | flops 23068672 | bytes 50360320 | tf_op jit(solution)/shard_map/add | solution.py:129
  1039.2 12.3 fusion.11
  1051.5 8.3 copy.220
  1059.7 10.6 reshape.214
  1070.3 180.4 %all_to_all.30 = f32[2048,4,256]{2,1,0:T(4,128)S(1)} all-to-all(f32[2048,4,256]{2,1,0:T(4,128)} %reshape.214), channel_id=1, replica_groups=mesh['rows'=8,'lev'=4] {'rows'}, dimensions={0} | all-to-all | bytes 16777216 | tf_op jit(solution)/shard_map/all_to_all | solution.py:266
  1257.2 7.5 copy.237
  1264.7 9.5 copy.223
  1279.3 10.3 fusion.47
  1289.6 10.2 fusion.49
  1299.8 10.6 fusion.51
  1310.4 10.3 fusion.53
  1320.7 34.4 %fusion.20 = (f32[64,32,1024]{2,0,1:T(8,128)S(1)}, f32[64,32,1024]{2,0,1:T(8,128)}) fusion(f32[1024]{0:T(1024)S(1)} %bitcast.238, f32[64,32]{0,1:T(8,128)S(1)} %broadcast_select_fusion.1, f32[64,32]{0,1:T(8,128)S(1)} %copy-done.10, f32[64,32]{0,1:T(8,128)S(1)} %copy-done.12, f32[32,1024,64]{1,0,2:T(8,128)} %fusion.49, f32[32,1024,64]{1,0,2:T(8,128)} %fusion.53, ...), kind=kLoop, calls=%fused_computation.47 | loop fusion | flops 23068672 | bytes 50360320 | tf_op jit(solution)/shard_map/add | solution.py:129
  1355.0 12.2 fusion.63
  1367.3 26.7 %copy.232 = f32[1024,64,32]{2,1,0:T(8,128)} copy(f32[1024,64,32]{0,1,2:T(8,128)} %fusion.63) | data formatting | bytes 16777216 | tf_op jit(solution)/shard_map/fjb,fk->bkj/transpose | solution.py:23
  1394.0 26.2 %reshape_reshape.4 = f32[256,4,2048]{2,1,0:T(4,128)} reshape(f32[1024,64,32]{2,1,0:T(8,128)} %copy.232) | data formatting | bytes 16777216 | tf_op jit(solution)/shard_map/reshape;reshape | solution.py:268
  (145 shorter events, 179.2 us)
Async XLA Ops:
  0.2 452.5 %copy-start.9 = (f32[64,32]{0,1:T(8,128)}, f32[64,32]{0,1:T(8,128)S(1)}, u32[]{:S(2)}) copy-start(f32[64,32]{0,1:T(8,128)S(1)} %get-tuple-element.585) | copy-start | bytes 24580
  0.2 452.5 %copy-start.11 = (f32[64,32]{0,1:T(8,128)}, f32[64,32]{0,1:T(8,128)S(1)}, u32[]{:S(2)}) copy-start(f32[64,32]{0,1:T(8,128)S(1)} %get-tuple-element.586) | copy-start | bytes 24580
  0.3 501.0 %copy-start.18 = (f32[32]{0:T(128)}, f32[32]{0:T(128)S(1)}, u32[]{:S(2)}) copy-start(f32[32]{0:T(128)S(1)} %fusion.151) | copy-start | bytes 388
  0.3 524.7 %copy-start.16 = (pred[1024]{0:T(1024)(128)(4,1)}, pred[1024]{0:T(1024)(128)(4,1)S(1)}, u32[]{:S(2)}) copy-start(pred[1024]{0:T(1024)(128)(4,1)S(1)} %iota_compare_fusion.2) | copy-start | bytes 3076
  0.3 22.2 %copy-start.15 = (s32[32,4,32]{2,1,0:T(4,128)S(1)}, s32[32,4,32]{2,1,0:T(4,128)}, u32[]{:S(2)}) copy-start(s32[32,4,32]{2,1,0:T(4,128)} %param.8) | copy-start | bytes 49156
  82.1 346.2 %copy-start.7 = (f32[128,64,1]{0,1,2:T(8,128)}, f32[128,64,1]{0,1,2:T(8,128)S(1)}, u32[]{:S(2)}) copy-start(f32[128,64,1]{0,1,2:T(8,128)S(1)} %maximum_bitcast_fusion) | copy-start | bytes 98308
  102.9 5.8 copy-start.3
  115.9 19.0 %copy-start.1 = (f32[64,32,1024]{2,0,1:T(8,128)}, f32[64,32,1024]{2,0,1:T(8,128)S(1)}, u32[]{:S(2)}) copy-start(f32[64,32,1024]{2,0,1:T(8,128)S(1)} %get-tuple-element.569) | copy-start | bytes 25165828
  134.9 395.9 %copy-start.13 = (f32[2048]{0:T(1024)}, f32[2048]{0:T(1024)S(1)}, u32[]{:S(2)}) copy-start(f32[2048]{0:T(1024)S(1)} %fusion.125) | copy-start | bytes 24580
  192.9 4.8 copy-start.5
  214.5 7.9 copy-start.20
  214.5 190.9 %all-to-all-start = ((f32[256,4,2048]{0,1,2:T(4,128)}), f32[256,4,2048]{0,1,2:T(4,128)}, u32[]{:S(2)}, u32[]{:S(2)}) async-start(f32[256,4,2048]{0,1,2:T(4,128)} %copy.200), calls=%async_computation | async-start | bytes 16777216 | tf_op jit(solution)/shard_map/all_to_all | solution.py:253
  459.9 20.9 %copy-start.2 = (f32[64,32,1024]{2,0,1:T(8,128)}, f32[64,32,1024]{2,0,1:T(8,128)S(1)}, u32[]{:S(2)}) copy-start(f32[64,32,1024]{2,0,1:T(8,128)S(1)} %get-tuple-element.567) | copy-start | bytes 25165828
  525.0 5.8 copy-start.6
  665.6 4.3 copy-start.4
  713.2 8.9 copy-start
  713.2 63.2 %slice-start = ((s8[8388608]{0:T(1024)(128)(4,1)}), s8[4194304]{0:T(1024)(128)(4,1)S(1)}, s32[]{:S(2)}) async-start(s8[8388608]{0:T(1024)(128)(4,1)} %bitcast.221), calls=%async_computation.2 | async-start | bytes 8388608
  713.3 63.2 %slice-start.2 = ((s8[8388608]{0:T(1024)(128)(4,1)}), s8[4194304]{0:T(1024)(128)(4,1)S(1)}, s32[]{:S(2)}) async-start(s8[8388608]{0:T(1024)(128)(4,1)} %bitcast.223), calls=%async_computation.4 | async-start | bytes 8388608
  713.8 62.7 %slice-start.1 = ((s8[8388608]{0:T(1024)(128)(4,1)}), s8[4194304]{0:T(1024)(128)(4,1)S(1)}, s32[]{:S(2)}) async-start(s8[8388608]{0:T(1024)(128)(4,1)} %bitcast.221), calls=%async_computation.3 | async-start | bytes 8388608
  713.8 62.7 %slice-start.3 = ((s8[8388608]{0:T(1024)(128)(4,1)}), s8[4194304]{0:T(1024)(128)(4,1)S(1)}, s32[]{:S(2)}) async-start(s8[8388608]{0:T(1024)(128)(4,1)} %bitcast.223), calls=%async_computation.5 | async-start | bytes 8388608
  713.8 8.3 collective-permute-start
  726.7 49.7 %collective-permute-start.1 = (f32[2,256,2048]{2,1,0:T(8,128)S(1)}, f32[2,256,2048]{2,1,0:T(8,128)S(1)}, u32[]{:S(2)}, u32[]{:S(2)}) collective-permute-start(f32[2,256,2048]{2,1,0:T(8,128)S(1)} %pad_maximum_fusion.1), channel_id=1, source_target_pairs={{0,1},{1,2},{2,3},{4,5},{5,6},{6,7},{8,9},{9,10},{10,11},{12,13},{... | collective-permute-start | bytes 12582920 | tf_op jit(solution)/shard_map/ppermute | solution.py:19
  778.5 49.8 %collective-permute-start.2 = (f32[2,256,2048]{2,1,0:T(8,128)S(1)}, f32[2,256,2048]{2,1,0:T(8,128)S(1)}, u32[]{:S(2)}, u32[]{:S(2)}) collective-permute-start(f32[2,256,2048]{2,1,0:T(8,128)S(1)} %pad_maximum_fusion.2), channel_id=1, source_target_pairs={{0,1},{1,2},{2,3},{4,5},{5,6},{6,7},{8,9},{9,10},{10,11},{12,13},{... | collective-permute-start | bytes 12582920 | tf_op jit(solution)/shard_map/ppermute | solution.py:19
  831.7 46.7 %collective-permute-start.3 = (f32[256,2048]{1,0:T(8,128)S(1)}, f32[256,2048]{1,0:T(8,128)S(1)}, u32[]{:S(2)}, u32[]{:S(2)}) collective-permute-start(f32[256,2048]{1,0:T(8,128)S(1)} %get-tuple-element.550), channel_id=1, source_target_pairs={{1,0},{2,1},{3,2},{5,4},{6,5},{7,6},{9,8},{10,9},{11,10},{13,12},{... | collective-permute-start | bytes 6291464 | tf_op jit(solution)/shard_map/ppermute | solution.py:19
  879.0 30.0 %copy-start.19 = (f32[32]{0:T(128)S(1)}, f32[32]{0:T(128)}, u32[]{:S(2)}) copy-start(f32[32]{0:T(128)} %copy-done.18) | copy-start | bytes 388
  879.0 28.1 %collective-permute-start.4 = (f32[256,2048]{1,0:T(8,128)S(1)}, f32[256,2048]{1,0:T(8,128)S(1)}, u32[]{:S(2)}, u32[]{:S(2)}) collective-permute-start(f32[256,2048]{1,0:T(8,128)S(1)} %multiply_add_fusion.5), channel_id=1, source_target_pairs={{1,0},{2,1},{3,2},{5,4},{6,5},{7,6},{9,8},{10,9},{11,10},{13,12},{... | collective-permute-start | bytes 6291464 | tf_op jit(solution)/shard_map/ppermute | solution.py:19
  907.6 27.4 %collective-permute-start.5 = (f32[256,2048]{1,0:T(8,128)S(1)}, f32[256,2048]{1,0:T(8,128)S(1)}, u32[]{:S(2)}, u32[]{:S(2)}) collective-permute-start(f32[256,2048]{1,0:T(8,128)S(1)} %multiply_add_fusion.4), channel_id=1, source_target_pairs={{1,0},{2,1},{3,2},{5,4},{6,5},{7,6},{9,8},{10,9},{11,10},{13,12},{... | collective-permute-start | bytes 6291464 | tf_op jit(solution)/shard_map/ppermute | solution.py:19
  948.0 9.3 copy-start.14
  957.3 4.0 copy-start.17
  993.3 10.3 copy-start.10
  993.3 10.3 copy-start.12
  1003.6 35.6 %copy-start.8 = (f32[128,64,1]{0,1,2:T(8,128)S(1)}, f32[128,64,1]{0,1,2:T(8,128)}, u32[]{:S(2)}) copy-start(f32[128,64,1]{0,1,2:T(8,128)} %copy-done.7) | copy-start | bytes 98308
where the time goes:
time: 1440 us; the launch traced here: 1420 us
  local copies, waits for them, and re-layouts  341 us (24%)
  waiting for transfers between devices  300 us (21%)
  other arithmetic  255 us (18%)
  matrix products  238 us (17%)
  blocking collectives  180 us (12%)
  starting transfers between devices  100 us (7%)
    dot_general x20, matrix products, product(): jnp.einsum(form, left, right, precision=highest, preferred_element_type=j...  238 us
    all_to_all x1, waiting for transfers between devices, body(): lax.all_to_all(spectral, 'rows', split_axis=2, concat_axis=0, tiled=True)  183 us
    all_to_all x1, blocking collectives, body(): lax.all_to_all(physical, 'rows', split_axis=0, concat_axis=2, tiled=True)  180 us
    ppermute x6, waiting for transfers between devices, shifted(): lax.ppermute(value, axis, [(source, source + steps) for source in range(f...  118 us
    ppermute x6, starting transfers between devices, shifted(): lax.ppermute(value, axis, [(source, source + steps) for source in range(f...  92.2 us
    dynamic_update_slice x8, other arithmetic, section_solve(): lax.scan(forward, (zero_plane, (zero_plane,) * system_count), sweep_in)  78.4 us
    add x2, other arithmetic, unfinish(): twisted_real * twist_cos - twisted_imag * twist_sin  69.9 us
    dynamic_slice x24, local copies, waits for them, and re-layouts, section_solve(): lax.scan(forward, (zero_plane, (zero_plane,) * system_count), sweep_in)  47.8 us
  transfers between devices with their start and end apart: 7, of which 7 were waited for; matrix products, arithmetic and copies ran while one was open for 0% of the time, Pallas kernels for 0%

commit v1 on v0

v1 whole, which is shorter than its diff:
```python
import functools
import math

import numpy as np

import jax
import jax.numpy as jnp
from jax import lax
from jax.experimental import pallas as pl
from jax.experimental.pallas import tpu as pltpu
from jax.sharding import PartitionSpec as P

BY = 8
BX = 64
PARTS = 16
VMEM_BYTES = 48 * 1024 * 1024

f32 = jnp.float32
bf16 = jnp.bfloat16


def split_host(table):
    high = table.astype(np.float32).astype(jnp.bfloat16)
    low = (table - high.astype(np.float64)).astype(np.float32).astype(jnp.bfloat16)
    return high, low


def split(values):
    high = values.astype(bf16)
    low = (values - high.astype(f32)).astype(bf16)
    return high, low


def split_outside(values):
    high = lax.reduce_precision(values, 8, 7)
    return high.astype(bf16), (values - high).astype(bf16)


def dot3(left, right):
    dot = functools.partial(jnp.dot, preferred_element_type=f32)
    return dot(left[0], right[0]) + (dot(left[0], right[1]) + dot(left[1], right[0]))


@functools.lru_cache(None)
def x_tables(length):
    width = length // PARTS
    half = PARTS // 2
    place = np.arange(width)
    blocks = np.zeros((half, 2 * width, 2 * width))
    slots = np.zeros((half, 2 * width))
    inner = math.sqrt(2.0 / length)
    edge = math.sqrt(1.0 / length)

    def angle(freq):
        return 2.0 * math.pi * (np.outer(place, freq) % length) / length

    low = PARTS * np.arange(width // 2 + 1)
    weight = np.where((low == 0) | (low == length // 2), edge, inner)
    cosines = np.cos(angle(low)) * weight
    sines = np.sin(angle(low[1:-1])) * inner
    blocks[0, :width, :width] = np.concatenate([cosines, sines], 1)
    slots[0, :width] = np.concatenate([low, low[1:-1]])
    middle = half + PARTS * np.arange(width // 2)
    blocks[0, width:, width:] = np.concatenate([np.cos(angle(middle)), np.sin(angle(middle))], 1) * inner
    slots[0, width:] = np.concatenate([middle, middle])
    for first in range(1, half):
        freq = first + PARTS * np.arange(width)
        turn = angle(freq)
        cosines, sines = np.cos(turn) * inner, np.sin(turn) * inner
        blocks[first] = np.block([[cosines, -sines], [sines, cosines]])
        slots[first] = np.concatenate([freq, freq])
    eigen = 4.0 * np.sin(math.pi * slots.reshape(-1) / length) ** 2
    return blocks, eigen.astype(np.float32)


def turn(index):
    return math.cos(2.0 * math.pi * index / PARTS), math.sin(2.0 * math.pi * index / PARTS)


def stage(x):
    s = [x[b] + x[b + 8] for b in range(8)]
    d = [x[b] - x[b + 8] for b in range(8)]
    out = [None] * 8
    minus = [d[b] - d[8 - b] for b in range(1, 4)]
    plus = [d[b] + d[8 - b] for b in range(1, 4)]
    for first in (1, 3, 5, 7):
        real = d[0]
        imag = d[4] * (-turn(4 * first)[1])
        for b in (1, 2, 3):
            cosine, sine = turn(b * first)
            real = real + minus[b - 1] * cosine
            imag = imag - plus[b - 1] * sine
        out[first] = (real, imag)
    ss = [s[b] + s[b + 4] for b in range(4)]
    sd = [s[b] - s[b + 4] for b in range(4)]
    root = math.sqrt(0.5)
    m = (sd[1] - sd[3]) * root
    p = (sd[1] + sd[3]) * root
    out[2] = (sd[0] + m, -p - sd[2])
    out[6] = (sd[0] - m, sd[2] - p)
    out[4] = (ss[0] - ss[2], ss[3] - ss[1])
    even, odd = ss[0] + ss[2], ss[1] + ss[3]
    out[0] = (even + odd, even - odd)
    return out


def unstage(y):
    root = math.sqrt(0.5)
    even, odd = y[0][0] + y[0][1], y[0][0] - y[0][1]
    ss = [even + y[4][0], odd - y[4][1], even - y[4][0], odd + y[4][1]]
    m = (y[2][0] - y[6][0]) * root
    p = (y[2][1] + y[6][1]) * root
    sd = [y[2][0] + y[6][0], m - p, y[6][1] - y[2][1], -m - p]
    s = [ss[b] + sd[b] for b in range(4)] + [ss[b] - sd[b] for b in range(4)]
    d = [None] * 8
    d[0] = (y[1][0] + y[3][0]) + (y[5][0] + y[7][0])
    d[4] = (y[3][1] - y[1][1]) + (y[7][1] - y[5][1])
    for b in (1, 2, 3):
        real = None
        imag = None
        for first in (1, 3, 5, 7):
            cosine, sine = turn(b * first)
            term, other = y[first][0] * cosine, y[first][1] * sine
            real = term if real is None else real + term
            imag = other if imag is None else imag + other
        d[b] = real - imag
        d[8 - b] = -real - imag
    return [s[b] + d[b] for b in range(8)] + [s[b] - d[b] for b in range(8)]


def half_place():
    group = lax.axis_size("lev") // 2
    me = lax.axis_index("lev")
    return me // group, me % group


def block_of(index, share, length):
    blocks = PARTS // 2
    _, own = half_place()
    return lax.rem(index + own * (share * blocks // length), blocks)


def forward_kernel(x_ref, keep_ref, spread_ref, high_ref, low_ref, *rest):
    out_refs, (kept, mixed) = rest[:-2], rest[-2:]
    rows, levels, length = x_ref.shape
    width = length // PARTS
    share = out_refs[0].shape[2]
    kept[...] = jnp.dot(keep_ref[...], spread_ref[...], preferred_element_type=f32)

    def group(index, unused):
        row = pl.multiple_of(index * BY, BY)
        for level in range(levels):
            mask = kept[pl.ds(index * levels + level, 1), :]
            x = [
                x_ref[pl.ds(row, BY), level, pl.ds(b * width, width)] * mask[:, b * width : (b + 1) * width]
                for b in range(PARTS)
            ]
            base = pl.multiple_of(level * rows + row, BY)
            for block, (real, imag) in enumerate(stage(x)):
                mixed[block, pl.ds(base, BY), :width] = real
                mixed[block, pl.ds(base, BY), width:] = imag
        return unused

    lax.fori_loop(0, rows // BY, group, 0)
    for index in range(PARTS // 2):
        block = block_of(index, share, length)
        product = dot3(split(mixed[block]), (high_ref[block], low_ref[block]))
        target, offset = divmod(2 * index * width, share)
        out_refs[target][:, :, offset : offset + 2 * width] = product.reshape(levels, rows, 2 * width)


def backward_kernel(*refs):
    x_refs, (high_ref, low_ref, out_ref, mixed) = refs[:-4], refs[-4:]
    rows, levels, length = out_ref.shape
    width = length // PARTS
    share = x_refs[0].shape[2]
    for index in range(PARTS // 2):
        block = block_of(index, share, length)
        source, offset = divmod(2 * index * width, share)
        values = split(x_refs[source][:, :, offset : offset + 2 * width].reshape(levels * rows, 2 * width))
        mixed[block] = dot3(values, (high_ref[block], low_ref[block]))

    def group(index, unused):
        row = pl.multiple_of(index * BY, BY)
        for level in range(levels):
            base = pl.multiple_of(level * rows + row, BY)
            y = [
                (mixed[block, pl.ds(base, BY), :width], mixed[block, pl.ds(base, BY), width:])
                for block in range(PARTS // 2)
            ]
            for b, value in enumerate(unstage(y)):
                out_ref[pl.ds(row, BY), level, pl.ds(b * width, width)] = value
        return unused

    lax.fori_loop(0, rows // BY, group, 0)


def eigen_kernel(start_ref, out_ref, *, sizes, top):
    lanes = start_ref.shape[1]
    lane = lax.broadcasted_iota(jnp.int32, (1, lanes), 1)
    in_first = lane < sizes[0]
    local = jnp.where(in_first, lane, lane - sizes[0])
    count = jnp.where(in_first, sizes[0], sizes[1])

    def rotate(values, parity):
        is_left = local % 2 == parity
        alone = (lane >= sum(sizes)) | (is_left & (local == count - 1)) | (jnp.logical_not(is_left) & (local == 0))
        partner = jnp.where(is_left, pltpu.roll(values, lanes - 1, 1), pltpu.roll(values, 1, 1))
        head = values[:top]
        head_partner = partner[:top]
        own = jnp.sum(head * head, axis=0, keepdims=True)
        other = jnp.sum(head_partner * head_partner, axis=0, keepdims=True)
        cross = jnp.sum(head * head_partner, axis=0, keepdims=True)
        delta = other - own
        sign = jnp.where((delta > 0) | ((delta == 0) & is_left), 1.0, -1.0)
        bottom = jnp.abs(delta) + jnp.sqrt(delta * delta + 4.0 * cross * cross)
        tangent = 2.0 * cross * sign / jnp.maximum(bottom, 1e-30)
        cosine = 1.0 / jnp.sqrt(1.0 + tangent * tangent)
        sine = cosine * tangent
        angle = jnp.where(alone, 0.0, jnp.abs(cross) * lax.rsqrt(jnp.maximum(own * other, 1e-30)))
        return jnp.where(alone, values, cosine * partner + sine * values), angle

    def sweep(carry):
        values, done, unused = carry
        worst = jnp.zeros((1, lanes), f32)
        for step in range(max(sizes)):
            values, angle = rotate(values, step % 2)
            worst = jnp.maximum(worst, angle)
        return values, done + 1, jnp.max(worst)

    def going(carry):
        return (carry[2] > 1e-6) & (carry[1] < 20)

    values, _, _ = lax.while_loop(going, sweep, (start_ref[...], jnp.int32(0), jnp.float32(1.0)))
    out_ref[...] = values


def eigen(weights):
    sizes = tuple(weight.shape[0] - 1 for weight in weights)
    top = -(-(sizes[0] + 1) // 8) * 8
    low = -(-sizes[0] // 8) * 8
    lanes = 128
    columns = []
    turns = []
    for size, weight in zip(sizes, weights):
        differences = np.zeros((top, size), np.float32)
        differences[np.arange(size), np.arange(size)] = 1.0
        differences[np.arange(size) + 1, np.arange(size)] = -1.0
        columns.append(differences * jnp.pad(jnp.sqrt(weight), (0, top - size - 1))[:, None])
        turns.append(np.eye(low, size, dtype=np.float32))
    start = jnp.concatenate([jnp.concatenate(columns, 1), jnp.asarray(np.concatenate(turns, 1))], 0)
    start = jnp.pad(start, ((0, 0), (0, lanes - sum(sizes))))
    turned = pl.pallas_call(
        functools.partial(eigen_kernel, sizes=sizes, top=top),
        out_shape=jax.ShapeDtypeStruct(start.shape, f32),
        name="eigen",
    )(start)
    found = []
    first = 0
    for size in sizes:
        part = turned[:, first : first + size]
        found.append((jnp.sum(part[:top] ** 2, axis=0), part[top : top + size]))
        first += size
    return found


def to_modes_kernel(*refs):
    x_refs, (high_ref, low_ref, ratio_ref, modes_ref, ends_ref, power) = refs[:-6], refs[-6:]
    modes, share = ratio_ref.shape

    @pl.when(pl.program_id(0) == 0)
    def _():
        ends_ref[...] = jnp.zeros(ends_ref.shape, f32)
        power[...] = jnp.ones(power.shape, f32)

    values = jnp.concatenate([x_ref[...].reshape(-1, share) for x_ref in x_refs], 0)
    modes_ref[...] = dot3((high_ref[...], low_ref[...]), split(values))
    ratio = ratio_ref[...]
    first, last, scale = ends_ref[0], ends_ref[1], power[...]
    for row in range(modes_ref.shape[0] // modes):
        current = modes_ref[row * modes : (row + 1) * modes, :]
        first = first * ratio + current
        last = last + scale * current
        scale = scale * ratio
    ends_ref[0] = first
    ends_ref[1] = last
    power[...] = scale


def two_way(rows, ratio_ref, edge_ref, held, chunk, carry, source, finish):
    step = pl.program_id(0)
    steps = pl.num_programs(0) // 2
    modes = ratio_ref.shape[0]
    ratio = ratio_ref[...]

    @pl.when(step == 0)
    def _():
        carry[...] = edge_ref[0]

    @pl.when(step == steps)
    def _():
        carry[...] = edge_ref[1]

    @pl.when(step < steps)
    def _():
        base = pl.multiple_of(step * rows * modes, rows * modes)
        value = carry[...]
        for row in range(rows):
            value = value * ratio + source(row)
            held[pl.ds(base + row * modes, modes), :] = value
        carry[...] = value

    @pl.when(step >= steps)
    def _():
        base = pl.multiple_of((2 * steps - 1 - step) * rows * modes, rows * modes)
        value = carry[...]
        for row in reversed(range(rows)):
            value = (value + held[pl.ds(base + row * modes, modes), :]) * ratio
            chunk[row * modes : (row + 1) * modes, :] = value
        carry[...] = value
        finish(split(chunk[...]))


def interface_kernel(modes_ref, high_ref, low_ref, ratio_ref, edge_ref, keep_ref, send_ref, held, chunk, carry, line):
    modes = ratio_ref.shape[0]
    piece = keep_ref.shape[1]
    half, _ = half_place()

    def finish(values):
        line[...] = dot3((high_ref[...], low_ref[...]), values)
        keep_ref[...] = line[:, pl.ds(pl.multiple_of(half * piece, piece), piece)]
        send_ref[...] = line[:, pl.ds(pl.multiple_of((1 - half) * piece, piece), piece)]

    two_way(
        keep_ref.shape[0], ratio_ref, edge_ref, held, chunk, carry,
        lambda row: modes_ref[row * modes : (row + 1) * modes, :], finish,
    )


def plane_ends(plane_ref, ratio_ref, ends_ref, weight):
    rows = plane_ref.shape[0]
    shape = ratio_ref.shape
    ratio = ratio_ref[...]

    def group(index, carry):
        first, last, scale = carry
        lines = plane_ref[pl.ds(pl.multiple_of(index * BY, BY), BY), :]
        for row in range(BY):
            current = jnp.broadcast_to(lines[row : row + 1], shape)
            first = first * ratio + current
            last = last + scale * current
            scale = scale * ratio
        return first, last, scale

    zero = jnp.zeros(shape, f32)
    first, last, _ = lax.fori_loop(0, rows // BY, group, (zero, zero, jnp.ones(shape, f32)))
    ends_ref[0] = first if weight is None else first * weight
    ends_ref[1] = last if weight is None else last * weight


def sum_kernel(own_ref, other_ref, ratio_ref, plane_ref, ends_ref):
    plane_ref[...] = own_ref[...] + other_ref[...]
    plane_ends(plane_ref, ratio_ref, ends_ref, None)


def join_kernel(own_ref, other_ref, ratio_ref, weight_ref, plane_ref, ends_ref):
    half, _ = half_place()
    piece = own_ref.shape[1]
    plane_ref[:, pl.ds(pl.multiple_of(half * piece, piece), piece)] = own_ref[...]
    plane_ref[:, pl.ds(pl.multiple_of((1 - half) * piece, piece), piece)] = other_ref[...]
    plane_ends(plane_ref, ratio_ref, ends_ref, weight_ref[...])


def couple_kernel(
    plane_ref, again_ref, high_ref, low_ref, ratio_ref, edge_ref, strength_ref, out_ref, held, chunk, carry
):
    shape = ratio_ref.shape

    def finish(values):
        out_ref[...] = dot3((high_ref[...], low_ref[...]), values) + again_ref[...] * strength_ref[...]

    two_way(
        out_ref.shape[0], ratio_ref, edge_ref, held, chunk, carry,
        lambda row: jnp.broadcast_to(plane_ref[row : row + 1, :], shape), finish,
    )


def from_modes_kernel(modes_ref, plane_ref, weight_ref, high_ref, low_ref, ratio_ref, edge_ref, *rest):
    out_refs, (held, chunk, carry) = rest[:-3], rest[-3:]
    modes, share = ratio_ref.shape
    levels, rows, _ = out_refs[0].shape
    weight = weight_ref[...]

    def finish(values):
        result = dot3((high_ref[...], low_ref[...]), values).reshape(len(out_refs), levels, rows, share)
        for index, out_ref in enumerate(out_refs):
            out_ref[...] = result[index]

    two_way(
        rows, ratio_ref, edge_ref, held, chunk, carry,
        lambda row: modes_ref[row * modes : (row + 1) * modes, :] + weight * plane_ref[row : row + 1, :], finish,
    )


def params():
    return pltpu.CompilerParams(vmem_limit_bytes=VMEM_BYTES)


def cost(flops, moved):
    return pl.CostEstimate(flops=int(flops), bytes_accessed=int(moved), transcendentals=0)


def whole(shape):
    return pl.BlockSpec(shape, lambda *index: (0,) * len(shape))


def struct(*shape):
    return jax.ShapeDtypeStruct(shape, f32)


def decay(values, eigen_x):
    sigma = values[:, None] + eigen_x[None, :]
    return 1.0 / (1.0 + 0.5 * sigma + jnp.sqrt(sigma + 0.25 * sigma * sigma))


def edges(ends, ratio, row_count):
    row_devices = lax.axis_size("rows")
    everyone = lax.all_gather(ends, "rows")
    me = lax.axis_index("rows")
    across = ratio**row_count
    closing = 1.0 / (1.0 - across**row_devices)

    def around(which, direction):
        total = jnp.zeros(ratio.shape, f32)
        for hop in range(row_devices, 0, -1):
            place = jnp.mod(me + direction * hop, row_devices)
            total = total * across + lax.dynamic_index_in_dim(everyone, place, 0, keepdims=False)[which]
        return total * closing

    before = around(0, -1)
    after = around(1, 1)
    last = ends[0] + across * before
    above = ratio * (ratio * last + after) / (1.0 - ratio * ratio)
    return jnp.stack([before, above])


def body(source, solid, couplings):
    row_count, levels, length = source.shape
    lev_devices = lax.axis_size("lev")
    group = lev_devices // 2
    half, own = half_place()
    share = length // group
    piece = share // 2
    width = length // PARTS
    half_levels = levels * group
    all_levels = 2 * half_levels
    tile = 64 if row_count % 64 == 0 else BY
    size = source.size

    def passed(value, shift):
        pairs = [
            (side * group + place, side * group + (place + shift) % group) for side in range(2) for place in range(group)
        ]
        return lax.ppermute(value, "lev", pairs)

    def across_halves(value):
        return lax.ppermute(value, "lev", [(place, (place + group) % lev_devices) for place in range(lev_devices)])

    blocks, eigen_x = x_tables(length)
    high, low = split_host(blocks)
    back_high, back_low = split_host(np.swapaxes(blocks, 1, 2))
    keep = (1 - solid).astype(bf16).reshape(-1, length // BX)
    spread = (np.arange(length)[None, :] // BX == np.arange(length // BX)[:, None]).astype(jnp.bfloat16)
    groups = tile // BY * levels
    table = whole(blocks.shape)
    part_spec = pl.BlockSpec((levels, tile, share), lambda i: (0, i, 0))
    field_spec = pl.BlockSpec((tile, levels, length), lambda i: (i, 0, 0))
    mixed = pltpu.VMEM((PARTS // 2, levels * tile, 2 * width), f32)
    spectral = pl.pallas_call(
        forward_kernel,
        grid=(row_count // tile,),
        in_specs=[field_spec, pl.BlockSpec((groups, length // BX), lambda i: (i, 0)), whole(spread.shape), table, table],
        out_specs=[part_spec] * group,
        out_shape=[struct(levels, row_count, share)] * group,
        scratch_shapes=[pltpu.VMEM((groups, length), f32), mixed],
        compiler_params=params(),
        cost_estimate=cost(6 * size * 2 * width, 8 * size),
        name="forward_x",
    )(source, keep, spread, high, low)
    sections = [spectral[0]] + [passed(spectral[shift], shift) for shift in range(1, group)]

    middle = couplings[half_levels]
    edge_at = jnp.where(half == 0, half_levels, 0)
    mine = lax.dynamic_slice_in_dim(couplings, half * half_levels, half_levels + 1)
    mine = jnp.where(jnp.arange(half_levels + 1) == edge_at, 2.0 * middle, mine)
    (full_values, full_vectors), (values, vectors) = eigen([couplings, mine])
    edge_weight = jnp.where(half == 0, vectors[half_levels - 1], vectors[0])
    jump = middle * (full_vectors[half_levels - 1] + full_vectors[half_levels])
    eigen_x = lax.dynamic_slice_in_dim(jnp.asarray(eigen_x), own * share, share)
    ratio = decay(values, eigen_x)
    full_ratio = decay(full_values, lax.dynamic_slice_in_dim(eigen_x, half * piece, piece))

    chunk = max(BY, 256 // half_levels)
    thin = max(BY, 256 // all_levels)
    rows = chunk * half_levels
    plane_rows = thin * all_levels
    order = jnp.mod(own - jnp.arange(group), group)
    turned = vectors.reshape(group, levels, half_levels)[order].reshape(half_levels, half_levels)
    eye = jnp.eye(chunk, dtype=f32)
    to_modes = (eye[:, None, None, :] * turned.T[None, :, :, None]).reshape(rows, rows)
    from_modes = (eye[None, :, :, None] * turned[:, None, None, :]).reshape(rows, rows)
    to_edge = (eye[:, :, None] * edge_weight).reshape(chunk, rows)
    to_jump = (jnp.eye(thin, dtype=f32)[:, :, None] * (jump * jump)).reshape(thin, plane_rows)

    steps = row_count // chunk
    plane_steps = row_count // thin
    shape = (half_levels, share)
    plane_shape = (all_levels, piece)
    modes_shape = struct(row_count * half_levels, share)
    section_spec = pl.BlockSpec((levels, chunk, share), lambda i: (0, i, 0))

    def ahead(count):
        return lambda i: (jnp.minimum(i, count - 1), 0)

    def behind(count):
        return lambda i: (jnp.minimum(2 * count - 1 - i, count - 1), 0)

    def scratch(rows, shape):
        return [pltpu.VMEM((row_count * shape[0], shape[1]), f32), pltpu.VMEM((rows, shape[1]), f32), pltpu.VMEM(shape, f32)]

    modes, ends = pl.pallas_call(
        to_modes_kernel,
        grid=(steps,),
        in_specs=[section_spec] * group + [whole((rows, rows))] * 2 + [whole(shape)],
        out_specs=[pl.BlockSpec((rows, share), lambda i: (i, 0)), whole((2,) + shape)],
        out_shape=[modes_shape, struct(2, *shape)],
        scratch_shapes=[pltpu.VMEM(shape, f32)],
        compiler_params=params(),
        cost_estimate=cost(6 * size * rows, 8 * size),
        name="to_modes",
    )(*sections, *split_outside(to_modes), ratio)
    edge = edges(ends, ratio, row_count)

    kept, sent = pl.pallas_call(
        interface_kernel,
        grid=(2 * steps,),
        in_specs=[pl.BlockSpec((rows, share), ahead(steps))] + [whole((chunk, rows))] * 2 + [whole(shape), whole((2,) + shape)],
        out_specs=[pl.BlockSpec((chunk, piece), behind(steps))] * 2,
        out_shape=[struct(row_count, piece)] * 2,
        scratch_shapes=scratch(rows, shape) + [pltpu.VMEM((chunk, share), f32)],
        compiler_params=params(),
        cost_estimate=cost(6 * size * chunk, 5 * size),
        name="interface",
    )(modes, *split_outside(to_edge), ratio, edge)

    plane, plane_ends = pl.pallas_call(
        sum_kernel,
        out_shape=[struct(row_count, piece), struct(2, *plane_shape)],
        compiler_params=params(),
        name="plane_sum",
    )(kept, across_halves(sent), full_ratio)
    plane_edge = edges(plane_ends, full_ratio, row_count)

    moved = pl.pallas_call(
        couple_kernel,
        grid=(2 * plane_steps,),
        in_specs=[
            pl.BlockSpec((thin, piece), ahead(plane_steps)),
            pl.BlockSpec((thin, piece), behind(plane_steps)),
            whole((thin, plane_rows)),
            whole((thin, plane_rows)),
            whole(plane_shape),
            whole((2,) + plane_shape),
            whole((1, piece)),
        ],
        out_specs=pl.BlockSpec((thin, piece), behind(plane_steps)),
        out_shape=struct(row_count, piece),
        scratch_shapes=scratch(plane_rows, plane_shape),
        compiler_params=params(),
        cost_estimate=cost(6 * size * thin, 2 * size),
        name="couple",
    )(plane, plane, *split_outside(to_jump), full_ratio, plane_edge, jnp.full((1, piece), middle))

    weight = jnp.broadcast_to(edge_weight[:, None], shape)
    joined, joined_ends = pl.pallas_call(
        join_kernel,
        out_shape=[struct(row_count, share), struct(2, *shape)],
        compiler_params=params(),
        name="plane_join",
    )(moved, across_halves(moved), ratio, weight)
    edge = edge + edges(joined_ends, ratio, row_count)

    solved = pl.pallas_call(
        from_modes_kernel,
        grid=(2 * steps,),
        in_specs=[pl.BlockSpec((rows, share), ahead(steps)), pl.BlockSpec((chunk, share), ahead(steps)), whole(shape)]
        + [whole((rows, rows))] * 2
        + [whole(shape), whole((2,) + shape)],
        out_specs=[pl.BlockSpec((levels, chunk, share), lambda i: (0,) + behind(steps)(i))] * group,
        out_shape=[struct(levels, row_count, share)] * group,
        scratch_shapes=scratch(rows, shape),
        compiler_params=params(),
        cost_estimate=cost(6 * size * rows, 8 * size),
        name="from_modes",
    )(modes, joined, weight, *split_outside(from_modes), ratio, edge)
    returned = [solved[0]] + [passed(solved[shift], group - shift) for shift in range(1, group)]
    return pl.pallas_call(
        backward_kernel,
        grid=(row_count // tile,),
        in_specs=[part_spec] * group + [table, table],
        out_specs=field_spec,
        out_shape=struct(*source.shape),
        scratch_shapes=[mixed],
        compiler_params=params(),
        cost_estimate=cost(6 * size * 2 * width, 8 * size),
        name="backward_x",
    )(*returned, back_high, back_low)


def solution(mesh):
    return jax.shard_map(
        body,
        mesh=mesh,
        in_specs=(P("rows", "lev", None), P("rows", "lev", None), P()),
        out_specs=P("rows", "lev", None),
        check_vma=False,
    )
```

time: 1440 us -> 228 us (0.16); the launches traced: 1420 us -> 227 us
  local copies, waits for them, and re-layouts: 341 us -> 13.8 us
  waiting for transfers between devices: 300 us -> 21.7 us
  other arithmetic: 255 us -> 5.96 us
  matrix products: 238 us -> 0 us
  starting transfers between devices: 100 us -> 3.65 us
  Pallas kernels: 0 us -> 85.3 us
  blocking collectives: 180 us -> 95.1 us
    dot_general x20 -> x0, matrix products: 238 us -> none  [product(): jnp.einsum(form, left, right, precision=highest, preferred_element_type=j...]
    all_to_all x1 -> x0, waiting for transfers between devices: 183 us -> none  [body(): lax.all_to_all(spectral, 'rows', split_axis=2, concat_axis=0, tiled=True)]
    all_to_all x1 -> x0, blocking collectives: 180 us -> none  [body(): lax.all_to_all(physical, 'rows', split_axis=0, concat_axis=2, tiled=True)]
    add x12 -> x1, other arithmetic: 114 us -> 0.01 us  [body(): edge = edge + edges(joined_ends, ratio, row_count)]
    ppermute x6 -> x4, waiting for transfers between devices: 118 us -> 21.7 us  [the longest x2 14.3 us: across_halves(): lax.ppermute(value, 'lev', [(place, (place + group) % lev_devices) for pl...]
    all_gather x0 -> x3, blocking collectives: none -> 95.1 us  [edges(): everyone = lax.all_gather(ends, 'rows')]
    ppermute x6 -> x4, starting transfers between devices: 92.2 us -> 3.65 us  [the longest x2 3.2 us: across_halves(): lax.ppermute(value, 'lev', [(place, (place + group) % lev_devices) for pl...]
    pallas_call x0 -> x9, Pallas kernels: none -> 85.3 us  [the longest x1 15.4 us: body(): pl.pallas_call(forward_kernel, grid=(row_count // tile,), in_specs=[field...]
  transfers between devices with their start and end apart: 7 -> 4, of which waited for: 7 -> 3; matrix products, arithmetic and copies ran while one was open for 0% -> 4% of each run, Pallas kernels for 0% -> 7%
where the time goes in v1:
time: 228 us; the launch traced here: 227 us
  blocking collectives  95.1 us (42%)
  Pallas kernels  85.3 us (37%)
  waiting for transfers between devices  21.7 us (10%)
  local copies, waits for them, and re-layouts  13.8 us (6%)
  other arithmetic  5.96 us (3%)
  starting transfers between devices  3.65 us (2%)
    all_gather x3, blocking collectives, edges(): everyone = lax.all_gather(ends, 'rows')  95.1 us
    pallas_call x1, Pallas kernels, body(): pl.pallas_call(forward_kernel, grid=(row_count // tile,), in_specs=[field...  15.4 us
    pallas_call x1, Pallas kernels, eigen(): pl.pallas_call(functools.partial(eigen_kernel, sizes=sizes, top=top), out...  14.8 us
    ppermute x2, waiting for transfers between devices, across_halves(): lax.ppermute(value, 'lev', [(place, (place + group) % lev_devices) for pl...  14.3 us
    pallas_call x1, Pallas kernels, body(): pl.pallas_call(from_modes_kernel, grid=(2 * steps,), in_specs=[pl.BlockSp...  13.5 us
    pallas_call x1, Pallas kernels, body(): pl.pallas_call(backward_kernel, grid=(row_count // tile,), in_specs=[part...  13.4 us
    pallas_call x1, Pallas kernels, body(): pl.pallas_call(interface_kernel, grid=(2 * steps,), in_specs=[pl.BlockSpe...  9.98 us
    unnamed x28, local copies, waits for them, and re-layouts  9.52 us
  transfers between devices with their start and end apart: 4, of which 3 were waited for; matrix products, arithmetic and copies ran while one was open for 4% of the time, Pallas kernels for 7%

profile of v1, /device:TPU:0, one launch (start us, length us, event | category | flops | bytes accessed | tf_op | source)
XLA Modules:
  0.0 226.6 jit_solution(7454601619980764930)
XLA Ops:
  0.0 0.9 subtract_convert_fusion
  0.9 0.0 copy-start.3
  0.9 1.2 copy-done.3
  2.1 1.2 copy-done.4
  3.3 0.9 copy-done.5
  4.2 0.0 copy-start.11
  4.2 15.4 %forward_x.1 = (f32[4,256,1024]{2,1,0:T(8,128)}, f32[4,256,1024]{2,1,0:T(8,128)}) custom-call(f32[256,4,2048]{2,1,0:T(4,128)} %x_ref.1, bf16[128,32]{1,0:T(8,128)(2,1)S(1)} %bitcast.437, bf16[32,2048]{1,0:T(8,128)(2,1)S(1)} %copy-done.5, bf16[8,256,256]{2,1,0:T(8,128)(2,1)S(1)} %copy-done.4, bf16[8,256,256]{2,1,0:T(8,128)(2,1)S(1)} %copy-done.3), custom_call_target="tpu_custom_call" | custom-call | flops 3221225472 | bytes 16777216 | tf_op jit(solution)/shard_map/forward_x/pallas_call | solution.py:479
  19.6 0.4 collective-permute-start
  20.1 0.7 slice.236
  21.4 0.1 fusion.131
  21.6 0.1 dynamic_slice.176
  21.6 0.1 broadcast_multiply_fusion.3
  21.7 0.1 broadcast_multiply_fusion.2
  21.8 0.0 copy-done.11
  21.8 0.7 select_maximum_fusion.start_ref
  22.5 14.8 %eigen.1 = f32[40,128]{1,0:T(8,128)} custom-call(f32[40,128]{1,0:T(8,128)} %select_maximum_fusion.start_ref), custom_call_target="tpu_custom_call" | custom-call | tf_op jit(solution)/shard_map/eigen/pallas_call | solution.py:253
  37.3 0.8 slice.297
  38.1 0.6 gather_fusion
  38.7 0.1 copy.21
  38.7 1.4 fusion.136
  40.1 0.1 mul.1537
  40.2 0.1 copy.20
  40.3 0.8 fusion.130
  41.1 0.1 mul.1486
  41.2 0.1 mul.1530
  41.3 0.1 mul.1531
  41.5 0.1 copy.22
  41.5 0.2 broadcast_multiply_fusion.1
  41.7 0.3 mul.1476
  42.1 0.8 fusion.128
  42.9 0.1 fusion.5.refs_4_.ratio_ref
  43.1 0.0 collective-permute-done.refs_1_
  43.1 0.0 copy-start.6
  43.1 2.2 copy-done.6
  45.3 9.4 %to_modes.1 = (f32[2048,1024]{1,0:T(8,128)}, f32[2,8,1024]{2,1,0:T(8,128)S(1)}) custom-call(f32[4,256,1024]{2,1,0:T(8,128)S(1)} %copy-done.6, f32[4,256,1024]{2,1,0:T(8,128)} %collective-permute-done.refs_1_, bf16[256,256]{1,0:T(8,128)(2,1)S(1)} %get-tuple-element.38.refs_2_, bf16[256,256]{1,0:T(8,128)(2,1)S(1)} %get-tuple-element.37.refs_3_, ...), custom_call_target="tpu_custom_call" | custom-call | flops 3221225472 | bytes 16777216 | tf_op jit(solution)/shard_map/to_modes/pallas_call | solution.py:531
  54.7 32.7 %all-gather = f32[16,8,1024]{2,1,0:T(8,128)S(1)} all-gather(f32[2,8,1024]{2,1,0:T(8,128)S(1)} %get-tuple-element.20), channel_id=2, replica_groups=mesh['rows'=8,'lev'=4] {'rows'}, dimensions={0}, use_global_device_ids=true | all-gather | bytes 589824 | tf_op jit(solution)/shard_map/all_gather | solution.py:428
  87.4 0.2 fusion.93
  87.6 10.0 %interface.1 = (f32[256,512]{1,0:T(8,128)S(1)}, f32[256,512]{1,0:T(8,128)S(1)}) custom-call(f32[2048,1024]{1,0:T(8,128)} %get-tuple-element.19.modes_ref, bf16[32,256]{1,0:T(8,128)(2,1)S(1)} %get-tuple-element.40.high_ref, bf16[32,256]{1,0:T(8,128)(2,1)S(1)} %get-tuple-element.39.low_ref, f32[8,1024]{1,0:T(8,128)S(1)} %fusion.5.refs_4_.ratio_ref, ...), custom_call_target="tpu_custom_call" | custom-call | flops 402653184 | bytes 10485760 | tf_op jit(solution)/shard_map/interface/pallas_call | solution.py:544
  97.6 1.6 collective-permute-start.1
  99.2 0.1 fusion.13.ratio_ref
  99.3 7.5 %collective-permute-done.1.other_ref = f32[256,512]{1,0:T(8,128)S(1)} collective-permute-done((f32[256,512]{1,0:T(8,128)S(1)}, f32[256,512]{1,0:T(8,128)S(1)}, u32[]{:S(2)}, u32[]{:S(2)}) %collective-permute-start.1) | collective-permute-done | bytes 524320 | tf_op jit(solution)/shard_map/ppermute | solution.py:467
  106.9 1.5 plane_sum.1
  108.4 31.2 %all-gather.1 = f32[16,16,512]{2,1,0:T(8,128)S(1)} all-gather(f32[2,16,512]{2,1,0:T(8,128)S(1)} %get-tuple-element.24), channel_id=3, replica_groups=mesh['rows'=8,'lev'=4] {'rows'}, dimensions={0}, use_global_device_ids=true | all-gather | bytes 589824 | tf_op jit(solution)/shard_map/all_gather | solution.py:428
  139.6 0.2 fusion.58
  139.8 0.7 broadcast_in_dim.9.strength_ref
  140.5 5.7 %couple.1.own_ref = f32[256,512]{1,0:T(8,128)S(1)} custom-call(f32[256,512]{1,0:T(8,128)S(1)} %get-tuple-element.23.plane_ref.again_ref, f32[256,512]{1,0:T(8,128)S(1)} %get-tuple-element.23.plane_ref.again_ref, bf16[16,256]{1,0:T(8,128)(2,1)S(1)} %get-tuple-element.42.high_ref, bf16[16,256]{1,0:T(8,128)(2,1)S(1)} %get-tuple-element.41.low_ref, ...), custom_call_target="tpu_custom_call" | custom-call | flops 201326592 | bytes 4194304 | tf_op jit(solution)/shard_map/couple/pallas_call | solution.py:564
  146.1 1.6 collective-permute-start.2
  147.7 0.1 copy.23
  147.8 0.2 broadcast_multiply_fusion
  148.0 0.3 mul.1578
  148.3 0.1 copy.24
  148.5 6.8 %collective-permute-done.2.other_ref = f32[256,512]{1,0:T(8,128)S(1)} collective-permute-done((f32[256,512]{1,0:T(8,128)S(1)}, f32[256,512]{1,0:T(8,128)S(1)}, u32[]{:S(2)}, u32[]{:S(2)}) %collective-permute-start.2) | collective-permute-done | bytes 524320 | tf_op jit(solution)/shard_map/ppermute | solution.py:467
  155.3 0.1 broadcast_in_dim.10.weight_ref
  155.4 1.6 plane_join.1
  157.0 31.2 %all-gather.2 = f32[16,8,1024]{2,1,0:T(8,128)S(1)} all-gather(f32[2,8,1024]{2,1,0:T(8,128)S(1)} %get-tuple-element.26), channel_id=4, replica_groups=mesh['rows'=8,'lev'=4] {'rows'}, dimensions={0}, use_global_device_ids=true | all-gather | bytes 589824 | tf_op jit(solution)/shard_map/all_gather | solution.py:428
  188.2 0.2 fusion.23
  188.4 0.0 copy-start.1
  188.4 0.0 copy-start.2
  188.4 13.5 %from_modes.1 = (f32[4,256,1024]{2,1,0:T(8,128)S(1)}, f32[4,256,1024]{2,1,0:T(8,128)}) custom-call(f32[2048,1024]{1,0:T(8,128)} %get-tuple-element.19.modes_ref, f32[256,1024]{1,0:T(8,128)S(1)} %get-tuple-element.25.plane_ref, f32[8,1024]{1,0:T(8,128)S(1)} %broadcast_in_dim.10.weight_ref, bf16[256,256]{1,0:T(8,128)(2,1)S(1)} %get-tuple-element.36.high_ref, ...), custom_call_target="tpu_custom_call" | custom-call | flops 3221225472 | bytes 16777216 | tf_op jit(solution)/shard_map/from_modes/pallas_call | solution.py:593
  201.9 1.9 copy-done
  203.9 0.0 collective-permute-start.3
  203.9 7.4 %collective-permute-done.3.refs_1_ = f32[4,256,1024]{2,1,0:T(8,128)S(1)} collective-permute-done((f32[4,256,1024]{2,1,0:T(8,128)}, f32[4,256,1024]{2,1,0:T(8,128)S(1)}, u32[]{:S(2)}, u32[]{:S(2)}) %collective-permute-start.3) | collective-permute-done | bytes 4194336 | tf_op jit(solution)/shard_map/ppermute | solution.py:464
  211.2 2.0 copy-done.7
  213.2 13.4 %backward_x.1 = f32[256,4,2048]{2,1,0:T(4,128)} custom-call(f32[4,256,1024]{2,1,0:T(8,128)} %copy-done, f32[4,256,1024]{2,1,0:T(8,128)} %copy-done.7, bf16[8,256,256]{2,1,0:T(8,128)(2,1)S(1)} %copy-done.2, bf16[8,256,256]{2,1,0:T(8,128)(2,1)S(1)} %copy-done.1), custom_call_target="tpu_custom_call" | custom-call | flops 3221225472 | bytes 16777216 | tf_op jit(solution)/shard_map/backward_x/pallas_call | solution.py:607
  (35 shorter events, 0.2 us)
Async XLA Ops:
  0.9 1.2 copy-start.3
  2.1 1.2 copy-start.4
  3.3 0.9 copy-start.5
  4.2 15.8 %copy-start.13 = (f32[17]{0:T(128)S(1)}, f32[17]{0:T(128)}, u32[]{:S(2)}) copy-start(f32[17]{0:T(128)} %param.14) | copy-start | bytes 208
  4.2 17.3 %copy-start.12 = (f32[2048]{0:T(1024)S(1)}, f32[2048]{0:T(1024)}, u32[]{:S(2)}) copy-start(f32[2048]{0:T(1024)} %constant.356.clone) | copy-start | bytes 24580
  4.2 17.4 %copy-start.10 = (f32[24,16]{1,0:T(8,128)S(1)}, f32[24,16]{1,0:T(8,128)}, u32[]{:S(2)}) copy-start(f32[24,16]{1,0:T(8,128)} %constant.353.clone) | copy-start | bytes 4612
  4.2 17.5 %copy-start.9 = (f32[24,8]{1,0:T(8,128)S(1)}, f32[24,8]{1,0:T(8,128)}, u32[]{:S(2)}) copy-start(f32[24,8]{1,0:T(8,128)} %constant.354.clone) | copy-start | bytes 2308
  4.2 17.6 %copy-start.11 = (f32[16,24]{1,0:T(8,128)S(1)}, f32[16,24]{1,0:T(8,128)}, u32[]{:S(2)}) copy-start(f32[16,24]{1,0:T(8,128)} %constant.355.clone) | copy-start | bytes 4612
  19.6 23.5 %collective-permute-start = (f32[4,256,1024]{2,1,0:T(8,128)}, f32[4,256,1024]{2,1,0:T(8,128)}, u32[]{:S(2)}, u32[]{:S(2)}) collective-permute-start(f32[4,256,1024]{2,1,0:T(8,128)} %get-tuple-element.18), channel_id=1, source_target_pairs={{0,1},{1,0},{2,3},{3,2},{4,5},{5,4},{6,7},{7,6},{8,9},{9,8},{10,11... | collective-permute-start | bytes 12582920 | tf_op jit(solution)/shard_map/ppermute | solution.py:464
  43.1 2.2 copy-start.6
  87.6 11.6 %copy-start.8 = (f32[40,128]{1,0:T(8,128)S(1)}, f32[40,128]{1,0:T(8,128)}, u32[]{:S(2)}) copy-start(f32[40,128]{1,0:T(8,128)} %eigen.1) | copy-start | bytes 61444
  97.6 9.2 %collective-permute-start.1 = (f32[256,512]{1,0:T(8,128)S(1)}, f32[256,512]{1,0:T(8,128)S(1)}, u32[]{:S(2)}, u32[]{:S(2)}) collective-permute-start(f32[256,512]{1,0:T(8,128)S(1)} %get-tuple-element.22), channel_id=1, source_target_pairs={{0,2},{1,3},{2,0},{3,1},{4,6},{5,7},{6,4},{7,5},{8,10},{9,11},{10,... | collective-permute-start | bytes 1572872 | tf_op jit(solution)/shard_map/ppermute | solution.py:467
  146.1 9.2 %collective-permute-start.2 = (f32[256,512]{1,0:T(8,128)S(1)}, f32[256,512]{1,0:T(8,128)S(1)}, u32[]{:S(2)}, u32[]{:S(2)}) collective-permute-start(f32[256,512]{1,0:T(8,128)S(1)} %couple.1.own_ref), channel_id=1, source_target_pairs={{0,2},{1,3},{2,0},{3,1},{4,6},{5,7},{6,4},{7,5},{8,10},{9,11},{10,... | collective-permute-start | bytes 1572872 | tf_op jit(solution)/shard_map/ppermute | solution.py:467
  188.4 24.9 %copy-start.1 = (bf16[8,256,256]{2,1,0:T(8,128)(2,1)S(1)}, bf16[8,256,256]{2,1,0:T(8,128)(2,1)}, u32[]{:S(2)}) copy-start(bf16[8,256,256]{2,1,0:T(8,128)(2,1)} %constant.358.clone.refs_3_) | copy-start | bytes 3145732
  188.4 24.9 %copy-start.2 = (bf16[8,256,256]{2,1,0:T(8,128)(2,1)S(1)}, bf16[8,256,256]{2,1,0:T(8,128)(2,1)}, u32[]{:S(2)}) copy-start(bf16[8,256,256]{2,1,0:T(8,128)(2,1)} %constant.357.clone.refs_2_) | copy-start | bytes 3145732
  201.9 1.9 copy-start
  203.9 7.4 %collective-permute-start.3 = (f32[4,256,1024]{2,1,0:T(8,128)}, f32[4,256,1024]{2,1,0:T(8,128)S(1)}, u32[]{:S(2)}, u32[]{:S(2)}) collective-permute-start(f32[4,256,1024]{2,1,0:T(8,128)} %get-tuple-element.28), channel_id=1, source_target_pairs={{0,1},{1,0},{2,3},{3,2},{4,5},{5,4},{6,7},{7,6},{8,9},{9,8},{10,11... | collective-permute-start | bytes 12582920 | tf_op jit(solution)/shard_map/ppermute | solution.py:464
  211.2 2.0 copy-start.7

commit v2 on v1

--- a/solution.py
+++ b/solution.py
@@ -17,12 +17,6 @@
 
 f32 = jnp.float32
 bf16 = jnp.bfloat16
-
-
-def split_host(table):
-    high = table.astype(np.float32).astype(jnp.bfloat16)
-    low = (table - high.astype(np.float64)).astype(np.float32).astype(jnp.bfloat16)
-    return high, low
 
 
 def split(values):
@@ -140,25 +134,39 @@
     return lax.rem(index + own * (share * blocks // length), blocks)
 
 
-def forward_kernel(x_ref, keep_ref, spread_ref, high_ref, low_ref, *rest):
-    out_refs, (kept, mixed) = rest[:-2], rest[-2:]
+def keep_split(table_ref, high_ref, low_ref):
+    @pl.when(pl.program_id(0) == 0)
+    def _():
+        for block in range(table_ref.shape[0]):
+            high_ref[block], low_ref[block] = split(table_ref[block])
+
+
+def forward_kernel(x_ref, keep_ref, table_ref, *rest):
+    out_refs, (kept, mixed, high_ref, low_ref) = rest[:-4], rest[-4:]
     rows, levels, length = x_ref.shape
     width = length // PARTS
-    share = out_refs[0].shape[2]
-    kept[...] = jnp.dot(keep_ref[...], spread_ref[...], preferred_element_type=f32)
+    share = out_refs[0].shape[1]
+    pair = 8 // levels
+    keep_split(table_ref, high_ref, low_ref)
+    shape = (length // BX, length)
+    first = lax.broadcasted_iota(jnp.int32, shape, 0) * BX
+    lane = lax.broadcasted_iota(jnp.int32, shape, 1)
+    spread = jnp.where((lane >= first) & (lane < first + BX), 1.0, 0.0).astype(bf16)
+    kept[...] = jnp.dot(keep_ref[...], spread, preferred_element_type=f32)
 
     def group(index, unused):
-        row = pl.multiple_of(index * BY, BY)
-        for level in range(levels):
-            mask = kept[pl.ds(index * levels + level, 1), :]
+        mask = kept[pl.ds(pl.multiple_of(index * 8, 8), 8), :]
+        for part in range(BY // pair):
+            row = index * BY + part * pair
             x = [
-                x_ref[pl.ds(row, BY), level, pl.ds(b * width, width)] * mask[:, b * width : (b + 1) * width]
+                x_ref[pl.ds(row, pair), :, pl.ds(b * width, width)].reshape(8, width)
+                * mask[:, b * width : (b + 1) * width]
                 for b in range(PARTS)
             ]
-            base = pl.multiple_of(level * rows + row, BY)
+            base = pl.multiple_of(row * levels, 8)
             for block, (real, imag) in enumerate(stage(x)):
-                mixed[block, pl.ds(base, BY), :width] = real
-                mixed[block, pl.ds(base, BY), width:] = imag
+                mixed[block, pl.ds(base, 8), :width] = real
+                mixed[block, pl.ds(base, 8), width:] = imag
         return unused
 
     lax.fori_loop(0, rows // BY, group, 0)
@@ -166,33 +174,34 @@
         block = block_of(index, share, length)
         product = dot3(split(mixed[block]), (high_ref[block], low_ref[block]))
         target, offset = divmod(2 * index * width, share)
-        out_refs[target][:, :, offset : offset + 2 * width] = product.reshape(levels, rows, 2 * width)
+        out_refs[target][:, offset : offset + 2 * width] = product
 
 
 def backward_kernel(*refs):
-    x_refs, (high_ref, low_ref, out_ref, mixed) = refs[:-4], refs[-4:]
+    x_refs, (table_ref, out_ref, mixed, high_ref, low_ref) = refs[:-5], refs[-5:]
     rows, levels, length = out_ref.shape
     width = length // PARTS
-    share = x_refs[0].shape[2]
+    share = x_refs[0].shape[1]
+    pair = 8 // levels
+    keep_split(table_ref, high_ref, low_ref)
     for index in range(PARTS // 2):
         block = block_of(index, share, length)
         source, offset = divmod(2 * index * width, share)
-        values = split(x_refs[source][:, :, offset : offset + 2 * width].reshape(levels * rows, 2 * width))
+        values = split(x_refs[source][:, offset : offset + 2 * width])
         mixed[block] = dot3(values, (high_ref[block], low_ref[block]))
 
     def group(index, unused):
-        row = pl.multiple_of(index * BY, BY)
-        for level in range(levels):
-            base = pl.multiple_of(level * rows + row, BY)
-            y = [
-                (mixed[block, pl.ds(base, BY), :width], mixed[block, pl.ds(base, BY), width:])
-                for block in range(PARTS // 2)
-            ]
-            for b, value in enumerate(unstage(y)):
-                out_ref[pl.ds(row, BY), level, pl.ds(b * width, width)] = value
+        row = index * pair
+        base = pl.multiple_of(index * 8, 8)
+        y = [
+            (mixed[block, pl.ds(base, 8), :width], mixed[block, pl.ds(base, 8), width:])
+            for block in range(PARTS // 2)
+        ]
+        for b, value in enumerate(unstage(y)):
+            out_ref[pl.ds(row, pair), :, pl.ds(b * width, width)] = value.reshape(pair, levels, width)
         return unused
 
-    lax.fori_loop(0, rows // BY, group, 0)
+    lax.fori_loop(0, rows // pair, group, 0, unroll=4)
 
 
 def eigen_kernel(start_ref, out_ref, *, sizes, top):
@@ -229,7 +238,7 @@
         return values, done + 1, jnp.max(worst)
 
     def going(carry):
-        return (carry[2] > 1e-6) & (carry[1] < 20)
+        return (carry[2] > 1e-4) & (carry[1] < 20)
 
     values, _, _ = lax.while_loop(going, sweep, (start_ref[...], jnp.int32(0), jnp.float32(1.0)))
     out_ref[...] = values
@@ -264,27 +273,105 @@
     return found
 
 
+def power(value, exponent):
+    result = None
+    while exponent:
+        if exponent % 2:
+            result = value if result is None else result * value
+        value = value * value
+        exponent //= 2
+    return result
+
+
+def rows_place():
+    me = lax.axis_index("rows")
+    return me // 2, lax.rem(me, 2), lax.axis_size("rows") // 2
+
+
+def partners():
+    pair, place, pairs = rows_place()
+    return [2 * pair + 1 - place] + [2 * lax.rem(pair + hop, pairs) + place for hop in range(1, pairs)]
+
+
+def greet():
+    barrier = pltpu.get_barrier_semaphore()
+    for partner in partners():
+        pl.semaphore_signal(barrier, inc=1, device_id={"rows": partner}, device_id_type=pl.DeviceIdType.MESH)
+
+
+def exchange(row_count, ratio, ends, mate, total, others, send_sem, recv_sem):
+    pair, place, pairs = rows_place()
+    targets = partners()
+    pl.semaphore_wait(pltpu.get_barrier_semaphore(), pairs)
+
+    def copy(index, source, target):
+        return pltpu.make_async_remote_copy(
+            src_ref=source,
+            dst_ref=target,
+            send_sem=send_sem.at[index],
+            recv_sem=recv_sem.at[index],
+            device_id={"rows": targets[index]},
+            device_id_type=pl.DeviceIdType.MESH,
+        )
+
+    near = copy(0, ends, mate)
+    near.start()
+    across = power(ratio, row_count)
+    twice = across * across
+    closing = 1.0 / (1.0 - power(twice, pairs))
+    near.wait()
+    is_first = place == 0
+    first_f, last_f = jnp.where(is_first, ends[0], mate[0]), jnp.where(is_first, mate[0], ends[0])
+    first_b, last_b = jnp.where(is_first, ends[1], mate[1]), jnp.where(is_first, mate[1], ends[1])
+    total[0] = last_f + across * first_f
+    total[1] = first_b + across * last_b
+    far = [copy(hop, total, others.at[hop - 1]) for hop in range(1, pairs)]
+    for one in far:
+        one.start()
+    for one in far:
+        one.wait()
+    before, after = total[0], total[1]
+    for hop in range(pairs - 1, 0, -1):
+        before = before * twice + others[hop - 1, 0]
+        after = after * twice + others[pairs - hop - 1, 1]
+    before, after = before * closing, after * closing
+    before = jnp.where(is_first, before, first_f + across * before)
+    after = jnp.where(is_first, last_b + across * after, after)
+    last = ends[0] + across * before
+    above = ratio * (ratio * last + after) / (1.0 - ratio * ratio)
+    return before, above
+
+
 def to_modes_kernel(*refs):
-    x_refs, (high_ref, low_ref, ratio_ref, modes_ref, ends_ref, power) = refs[:-6], refs[-6:]
+    x_refs = refs[:-12]
+    high_ref, low_ref, ratio_ref, modes_ref, edge_ref, scale_ref, ends, mate, total, others, send_sem, recv_sem = refs[-12:]
     modes, share = ratio_ref.shape
-
-    @pl.when(pl.program_id(0) == 0)
+    step = pl.program_id(0)
+
+    @pl.when(step == 0)
     def _():
-        ends_ref[...] = jnp.zeros(ends_ref.shape, f32)
-        power[...] = jnp.ones(power.shape, f32)
-
-    values = jnp.concatenate([x_ref[...].reshape(-1, share) for x_ref in x_refs], 0)
+        greet()
+        ends[...] = jnp.zeros(ends.shape, f32)
+        scale_ref[...] = jnp.ones(scale_ref.shape, f32)
+
+    values = jnp.concatenate([x_ref[...] for x_ref in x_refs], 0)
     modes_ref[...] = dot3((high_ref[...], low_ref[...]), split(values))
     ratio = ratio_ref[...]
-    first, last, scale = ends_ref[0], ends_ref[1], power[...]
-    for row in range(modes_ref.shape[0] // modes):
+    first, last, scale = ends[0], ends[1], scale_ref[...]
+    rows = modes_ref.shape[0] // modes
+    for row in range(rows):
         current = modes_ref[row * modes : (row + 1) * modes, :]
         first = first * ratio + current
         last = last + scale * current
         scale = scale * ratio
-    ends_ref[0] = first
-    ends_ref[1] = last
-    power[...] = scale
+    ends[0] = first
+    ends[1] = last
+    scale_ref[...] = scale
+
+    @pl.when(step == pl.num_programs(0) - 1)
+    def _():
+        count = rows * pl.num_programs(0)
+        edge_ref[0], edge_ref[1] = exchange(count, ratio_ref[...], ends, mate, total, others, send_sem, recv_sem)
 
 
 def two_way(rows, ratio_ref, edge_ref, held, chunk, carry, source, finish):
@@ -337,7 +424,7 @@
     )
 
 
-def plane_ends(plane_ref, ratio_ref, ends_ref, weight):
+def plane_ends(plane_ref, ratio_ref, ends, weight):
     rows = plane_ref.shape[0]
     shape = ratio_ref.shape
     ratio = ratio_ref[...]
@@ -354,21 +441,27 @@
 
     zero = jnp.zeros(shape, f32)
     first, last, _ = lax.fori_loop(0, rows // BY, group, (zero, zero, jnp.ones(shape, f32)))
-    ends_ref[0] = first if weight is None else first * weight
-    ends_ref[1] = last if weight is None else last * weight
-
-
-def sum_kernel(own_ref, other_ref, ratio_ref, plane_ref, ends_ref):
+    ends[0] = first if weight is None else first * weight
+    ends[1] = last if weight is None else last * weight
+
+
+def sum_kernel(own_ref, other_ref, ratio_ref, plane_ref, edge_ref, ends, *rest):
+    greet()
     plane_ref[...] = own_ref[...] + other_ref[...]
-    plane_ends(plane_ref, ratio_ref, ends_ref, None)
-
-
-def join_kernel(own_ref, other_ref, ratio_ref, weight_ref, plane_ref, ends_ref):
+    plane_ends(plane_ref, ratio_ref, ends, None)
+    edge_ref[0], edge_ref[1] = exchange(plane_ref.shape[0], ratio_ref[...], ends, *rest)
+
+
+def join_kernel(own_ref, other_ref, ratio_ref, weight_ref, known_ref, plane_ref, edge_ref, ends, *rest):
+    greet()
     half, _ = half_place()
     piece = own_ref.shape[1]
     plane_ref[:, pl.ds(pl.multiple_of(half * piece, piece), piece)] = own_ref[...]
     plane_ref[:, pl.ds(pl.multiple_of((1 - half) * piece, piece), piece)] = other_ref[...]
-    plane_ends(plane_ref, ratio_ref, ends_ref, weight_ref[...])
+    plane_ends(plane_ref, ratio_ref, ends, weight_ref[...])
+    before, above = exchange(plane_ref.shape[0], ratio_ref[...], ends, *rest)
+    edge_ref[0] = known_ref[0] + before
+    edge_ref[1] = known_ref[1] + above
 
 
 def couple_kernel(
@@ -388,13 +481,14 @@
 def from_modes_kernel(modes_ref, plane_ref, weight_ref, high_ref, low_ref, ratio_ref, edge_ref, *rest):
     out_refs, (held, chunk, carry) = rest[:-3], rest[-3:]
     modes, share = ratio_ref.shape
-    levels, rows, _ = out_refs[0].shape
+    rows = plane_ref.shape[0]
     weight = weight_ref[...]
 
     def finish(values):
-        result = dot3((high_ref[...], low_ref[...]), values).reshape(len(out_refs), levels, rows, share)
+        result = dot3((high_ref[...], low_ref[...]), values)
+        each = out_refs[0].shape[0]
         for index, out_ref in enumerate(out_refs):
-            out_ref[...] = result[index]
+            out_ref[...] = result[index * each : (index + 1) * each]
 
     two_way(
         rows, ratio_ref, edge_ref, held, chunk, carry,
@@ -402,8 +496,20 @@
     )
 
 
-def params():
-    return pltpu.CompilerParams(vmem_limit_bytes=VMEM_BYTES)
+def params(collective_id=None):
+    if collective_id is None:
+        return pltpu.CompilerParams(vmem_limit_bytes=VMEM_BYTES)
+    return pltpu.CompilerParams(vmem_limit_bytes=VMEM_BYTES, collective_id=collective_id, has_side_effects=True)
+
+
+def exchange_scratch(shape, row_devices):
+    pairs = row_devices // 2
+    two = (2,) + shape
+    return [pltpu.VMEM(two, f32)] * 3 + [
+        pltpu.VMEM((pairs - 1,) + two, f32),
+        pltpu.SemaphoreType.DMA((pairs,)),
+        pltpu.SemaphoreType.DMA((pairs,)),
+    ]
 
 
 def cost(flops, moved):
@@ -423,30 +529,10 @@
     return 1.0 / (1.0 + 0.5 * sigma + jnp.sqrt(sigma + 0.25 * sigma * sigma))
 
 
-def edges(ends, ratio, row_count):
-    row_devices = lax.axis_size("rows")
-    everyone = lax.all_gather(ends, "rows")
-    me = lax.axis_index("rows")
-    across = ratio**row_count
-    closing = 1.0 / (1.0 - across**row_devices)
-
-    def around(which, direction):
-        total = jnp.zeros(ratio.shape, f32)
-        for hop in range(row_devices, 0, -1):
-            place = jnp.mod(me + direction * hop, row_devices)
-            total = total * across + lax.dynamic_index_in_dim(everyone, place, 0, keepdims=False)[which]
-        return total * closing
-
-    before = around(0, -1)
-    after = around(1, 1)
-    last = ends[0] + across * before
-    above = ratio * (ratio * last + after) / (1.0 - ratio * ratio)
-    return jnp.stack([before, above])
-
-
 def body(source, solid, couplings):
     row_count, levels, length = source.shape
     lev_devices = lax.axis_size("lev")
+    row_devices = lax.axis_size("rows")
     group = lev_devices // 2
     half, own = half_place()
     share = length // group
@@ -467,26 +553,27 @@
         return lax.ppermute(value, "lev", [(place, (place + group) % lev_devices) for place in range(lev_devices)])
 
     blocks, eigen_x = x_tables(length)
-    high, low = split_host(blocks)
-    back_high, back_low = split_host(np.swapaxes(blocks, 1, 2))
-    keep = (1 - solid).astype(bf16).reshape(-1, length // BX)
-    spread = (np.arange(length)[None, :] // BX == np.arange(length // BX)[:, None]).astype(jnp.bfloat16)
-    groups = tile // BY * levels
+    forward_table = blocks.astype(np.float32)
+    backward_table = np.swapaxes(blocks, 1, 2).astype(np.float32)
+    keep = (1 - solid).astype(bf16)[:, None]
+    keep = jnp.broadcast_to(keep, (keep.shape[0], 8 // levels) + keep.shape[2:]).reshape(-1, length // BX)
+    groups = tile // BY * 8
     table = whole(blocks.shape)
-    part_spec = pl.BlockSpec((levels, tile, share), lambda i: (0, i, 0))
+    part_spec = pl.BlockSpec((tile * levels, share), lambda i: (i, 0))
     field_spec = pl.BlockSpec((tile, levels, length), lambda i: (i, 0, 0))
     mixed = pltpu.VMEM((PARTS // 2, levels * tile, 2 * width), f32)
+    halves = [pltpu.VMEM(blocks.shape, bf16)] * 2
     spectral = pl.pallas_call(
         forward_kernel,
         grid=(row_count // tile,),
-        in_specs=[field_spec, pl.BlockSpec((groups, length // BX), lambda i: (i, 0)), whole(spread.shape), table, table],
+        in_specs=[field_spec, pl.BlockSpec((groups, length // BX), lambda i: (i, 0)), table],
         out_specs=[part_spec] * group,
-        out_shape=[struct(levels, row_count, share)] * group,
-        scratch_shapes=[pltpu.VMEM((groups, length), f32), mixed],
+        out_shape=[struct(row_count * levels, share)] * group,
+        scratch_shapes=[pltpu.VMEM((groups, length), f32), mixed] + halves,
         compiler_params=params(),
         cost_estimate=cost(6 * size * 2 * width, 8 * size),
         name="forward_x",
-    )(source, keep, spread, high, low)
+    )(source, keep, forward_table)
     sections = [spectral[0]] + [passed(spectral[shift], shift) for shift in range(1, group)]
 
     middle = couplings[half_levels]
@@ -505,10 +592,10 @@
     rows = chunk * half_levels
     plane_rows = thin * all_levels
     order = jnp.mod(own - jnp.arange(group), group)
-    turned = vectors.reshape(group, levels, half_levels)[order].reshape(half_levels, half_levels)
+    turned = vectors.reshape(group, levels, half_levels)[order]
     eye = jnp.eye(chunk, dtype=f32)
-    to_modes = (eye[:, None, None, :] * turned.T[None, :, :, None]).reshape(rows, rows)
-    from_modes = (eye[None, :, :, None] * turned[:, None, None, :]).reshape(rows, rows)
+    to_modes = (eye[:, None, None, :, None] * turned.transpose(2, 0, 1)[None, :, :, None, :]).reshape(rows, rows)
+    from_modes = (eye[None, :, None, :, None] * turned[:, None, :, None, :]).reshape(rows, rows)
     to_edge = (eye[:, :, None] * edge_weight).reshape(chunk, rows)
     to_jump = (jnp.eye(thin, dtype=f32)[:, :, None] * (jump * jump)).reshape(thin, plane_rows)
 
@@ -517,7 +604,7 @@
     shape = (half_levels, share)
     plane_shape = (all_levels, piece)
     modes_shape = struct(row_count * half_levels, share)
-    section_spec = pl.BlockSpec((levels, chunk, share), lambda i: (0, i, 0))
+    section_spec = pl.BlockSpec((chunk * levels, share), lambda i: (i, 0))
 
     def ahead(count):
         return lambda i: (jnp.minimum(i, count - 1), 0)
@@ -528,18 +615,17 @@
     def scratch(rows, shape):
         return [pltpu.VMEM((row_count * shape[0], shape[1]), f32), pltpu.VMEM((rows, shape[1]), f32), pltpu.VMEM(shape, f32)]
 
-    modes, ends = pl.pallas_call(
+    modes, edge = pl.pallas_call(
         to_modes_kernel,
         grid=(steps,),
         in_specs=[section_spec] * group + [whole((rows, rows))] * 2 + [whole(shape)],
         out_specs=[pl.BlockSpec((rows, share), lambda i: (i, 0)), whole((2,) + shape)],
         out_shape=[modes_shape, struct(2, *shape)],
-        scratch_shapes=[pltpu.VMEM(shape, f32)],
-        compiler_params=params(),
+        scratch_shapes=[pltpu.VMEM(shape, f32)] + exchange_scratch(shape, row_devices),
+        compiler_params=params(0),
         cost_estimate=cost(6 * size * rows, 8 * size),
         name="to_modes",
     )(*sections, *split_outside(to_modes), ratio)
-    edge = edges(ends, ratio, row_count)
 
     kept, sent = pl.pallas_call(
         interface_kernel,
@@ -553,13 +639,13 @@
         name="interface",
     )(modes, *split_outside(to_edge), ratio, edge)
 
-    plane, plane_ends = pl.pallas_call(
+    plane, plane_edge = pl.pallas_call(
         sum_kernel,
         out_shape=[struct(row_count, piece), struct(2, *plane_shape)],
-        compiler_params=params(),
+        scratch_shapes=exchange_scratch(plane_shape, row_devices),
+        compiler_params=params(1),
         name="plane_sum",
     )(kept, across_halves(sent), full_ratio)
-    plane_edge = edges(plane_ends, full_ratio, row_count)
 
     moved = pl.pallas_call(
         couple_kernel,
@@ -582,13 +668,13 @@
     )(plane, plane, *split_outside(to_jump), full_ratio, plane_edge, jnp.full((1, piece), middle))
 
     weight = jnp.broadcast_to(edge_weight[:, None], shape)
-    joined, joined_ends = pl.pallas_call(
+    joined, edge = pl.pallas_call(
         join_kernel,
         out_shape=[struct(row_count, share), struct(2, *shape)],
-        compiler_params=params(),
+        scratch_shapes=exchange_scratch(shape, row_devices),
+        compiler_params=params(2),
         name="plane_join",
-    )(moved, across_halves(moved), ratio, weight)
-    edge = edge + edges(joined_ends, ratio, row_count)
+    )(moved, across_halves(moved), ratio, weight, edge)
 
     solved = pl.pallas_call(
         from_modes_kernel,
@@ -596,8 +682,8 @@
         in_specs=[pl.BlockSpec((rows, share), ahead(steps)), pl.BlockSpec((chunk, share), ahead(steps)), whole(shape)]
         + [whole((rows, rows))] * 2
         + [whole(shape), whole((2,) + shape)],
-        out_specs=[pl.BlockSpec((levels, chunk, share), lambda i: (0,) + behind(steps)(i))] * group,
-        out_shape=[struct(levels, row_count, share)] * group,
+        out_specs=[pl.BlockSpec((chunk * levels, share), behind(steps))] * group,
+        out_shape=[struct(row_count * levels, share)] * group,
         scratch_shapes=scratch(rows, shape),
         compiler_params=params(),
         cost_estimate=cost(6 * size * rows, 8 * size),
@@ -607,14 +693,14 @@
     return pl.pallas_call(
         backward_kernel,
         grid=(row_count // tile,),
-        in_specs=[part_spec] * group + [table, table],
+        in_specs=[part_spec] * group + [table],
         out_specs=field_spec,
         out_shape=struct(*source.shape),
-        scratch_shapes=[mixed],
+        scratch_shapes=[mixed] + halves,
         compiler_params=params(),
         cost_estimate=cost(6 * size * 2 * width, 8 * size),
         name="backward_x",
-    )(*returned, back_high, back_low)
+    )(*returned, backward_table)
 
 
 def solution(mesh):

time: 228 us -> 166 us (0.73)
  blocking collectives: 95.1 us -> 0 us
  Pallas kernels: 85.3 us -> 113 us
  local copies, waits for them, and re-layouts: 13.8 us -> 19.3 us
  other arithmetic: 5.96 us -> 9.59 us
  waiting for transfers between devices: 21.7 us -> 18.9 us
    all_gather x3 -> x0, blocking collectives: 95.1 us -> none  [edges(): everyone = lax.all_gather(ends, 'rows')]
    pallas_call x1, Pallas kernels: 9.44 us -> 23.2 us  [body(): pl.pallas_call(to_modes_kernel, grid=(steps,), in_specs=[section_spec] *...]
    pallas_call x1, Pallas kernels: 1.52 us -> 11.9 us  [body(): pl.pallas_call(sum_kernel, out_shape=[struct(row_count, piece), struct(2,...]
    pallas_call x1, Pallas kernels: 1.57 us -> 10.9 us  [body(): pl.pallas_call(join_kernel, out_shape=[struct(row_count, share), struct(2...]
    mul x3, local copies, waits for them, and re-layouts: 0.75 us -> 8.16 us  [the longest x2 4.15 us: body(): eye[:, None, None, :, None] * turned.transpose(2, 0, 1)[None, :, :, None, :]]
    mul x2, other arithmetic: 0.37 us -> 5.21 us  [the longest x1 2.61 us: body(): eye[None, :, None, :, None] * turned[:, None, :, None, :]]
    pallas_call x1, Pallas kernels: 13.4 us -> 10.4 us  [body(): pl.pallas_call(backward_kernel, grid=(row_count // tile,), in_specs=[part...]
    ppermute x2, waiting for transfers between devices: 14.3 us -> 11.6 us  [across_halves(): lax.ppermute(value, 'lev', [(place, (place + group) % lev_devices) for pl...]
  transfers between devices with their start and end apart: 4 -> 4, of which waited for: 3 -> 3; matrix products, arithmetic and copies ran while one was open for 4% -> 12% of each run, Pallas kernels for 7% -> 9%
where the time goes in v2:
time: 166 us; the launch traced here: 165 us
  Pallas kernels  113 us (68%)
  local copies, waits for them, and re-layouts  19.3 us (12%)
  waiting for transfers between devices  18.9 us (11%)
  other arithmetic  9.59 us (6%)
  starting transfers between devices  3.47 us (2%)
    pallas_call x1, Pallas kernels, body(): pl.pallas_call(to_modes_kernel, grid=(steps,), in_specs=[section_spec] *...  23.2 us
    pallas_call x1, Pallas kernels, eigen(): pl.pallas_call(functools.partial(eigen_kernel, sizes=sizes, top=top), out...  14.9 us
    pallas_call x1, Pallas kernels, body(): pl.pallas_call(from_modes_kernel, grid=(2 * steps,), in_specs=[pl.BlockSp...  13.2 us
    pallas_call x1, Pallas kernels, body(): pl.pallas_call(forward_kernel, grid=(row_count // tile,), in_specs=[field...  12.8 us
    pallas_call x1, Pallas kernels, body(): pl.pallas_call(sum_kernel, out_shape=[struct(row_count, piece), struct(2,...  11.9 us
    ppermute x2, waiting for transfers between devices, across_halves(): lax.ppermute(value, 'lev', [(place, (place + group) % lev_devices) for pl...  11.6 us
    pallas_call x1, Pallas kernels, body(): pl.pallas_call(join_kernel, out_shape=[struct(row_count, share), struct(2...  10.9 us
    pallas_call x1, Pallas kernels, body(): pl.pallas_call(backward_kernel, grid=(row_count // tile,), in_specs=[part...  10.4 us
  transfers between devices with their start and end apart: 4, of which 3 were waited for; matrix products, arithmetic and copies ran while one was open for 12% of the time, Pallas kernels for 9%

profile of v2, /device:TPU:0, one launch (start us, length us, event | category | flops | bytes accessed | tf_op | source)
XLA Modules:
  0.0 165.2 jit_solution(11896170993581351311)
XLA Ops:
  0.0 0.9 subtract_convert_fusion
  0.9 0.0 copy-start.2
  0.9 1.6 copy-done.2
  2.5 0.0 copy-start.6
  2.5 0.0 copy-start.8
  2.5 0.0 copy-start.7
  2.5 0.0 copy-start.9
  2.5 12.8 %forward_x.1 = (f32[1024,1024]{1,0:T(8,128)}, f32[1024,1024]{1,0:T(8,128)}) custom-call(f32[256,4,2048]{2,1,0:T(4,128)} %x_ref.1, bf16[256,32]{1,0:T(8,128)(2,1)S(1)} %bitcast.18, f32[8,256,256]{2,1,0:T(8,128)S(1)} %copy-done.2), custom_call_target="tpu_custom_call" | custom-call | flops 3221225472 | bytes 16777216 | tf_op jit(solution)/shard_map/forward_x/pallas_call | solution.py:566
  15.3 0.4 collective-permute-start
  15.7 0.0 copy-done.10
  15.7 0.6 slice.35
  17.1 0.1 fusion.17
  17.2 0.0 copy-done.6
  17.2 0.1 dynamic_slice.14
  17.2 0.0 copy-done.8
  17.2 0.1 broadcast_multiply_fusion.3
  17.3 0.0 copy-done.7
  17.3 0.1 broadcast_multiply_fusion.2
  17.4 0.0 copy-done.9
  17.4 0.7 select_maximum_fusion.start_ref
  18.1 14.9 %eigen.1 = f32[40,128]{1,0:T(8,128)} custom-call(f32[40,128]{1,0:T(8,128)} %select_maximum_fusion.start_ref), custom_call_target="tpu_custom_call" | custom-call | tf_op jit(solution)/shard_map/eigen/pallas_call | solution.py:262
  32.9 0.8 slice.45
  33.7 1.4 fusion.22
  35.1 0.1 mul.184
  35.1 0.1 copy.11
  35.2 0.8 fusion.16
  36.1 0.1 mul.168
  36.2 0.1 mul.177
  36.3 0.1 mul.178
  36.4 0.1 copy.15
  36.5 0.6 gather_fusion
  37.1 0.0 dynamic-slice-start
  37.1 2.6 %broadcast_multiply_fusion.1 = f32[32,8,2,32,4]{1,0,4,3,2:T(8,128)} fusion(f32[8,2,4]{0,2,1:T(4,128)S(1)} %bitcast.19, f32[32,32]{0,1:T(8,128)S(1)} %copy.11), kind=kLoop, calls=%fused_computation.2 | loop fusion | flops 65536 | bytes 266496 | tf_op jit(solution)/shard_map/mul | solution.py:597
  39.7 4.0 %mul.158 = f32[256,256]{0,1:T(8,128)S(1)} reshape(f32[32,8,2,32,4]{1,0,4,3,2:T(8,128)} %broadcast_multiply_fusion.1) | data formatting | bytes 524288 | tf_op jit(solution)/shard_map/mul | solution.py:597
  43.7 0.1 copy.12
  43.8 0.0 copy-done.5
  43.9 0.1 fusion.14
  43.9 0.0 dynamic-slice-done
  43.9 0.1 fusion.5.refs_4_.ratio_ref
  44.1 0.0 collective-permute-done.refs_1_
  44.1 0.0 copy-start.3
  44.1 2.2 %copy-done.3 = f32[1024,1024]{1,0:T(8,128)S(1)} copy-done((f32[1024,1024]{1,0:T(8,128)S(1)}, f32[1024,1024]{1,0:T(8,128)}, u32[]{:S(2)}) %copy-start.3) | copy-done | bytes 4194328
  46.3 23.2 %to_modes.1 = (f32[2048,1024]{1,0:T(8,128)}, f32[2,8,1024]{2,1,0:T(8,128)S(1)}) custom-call(f32[1024,1024]{1,0:T(8,128)S(1)} %copy-done.3, f32[1024,1024]{1,0:T(8,128)} %collective-permute-done.refs_1_, bf16[256,256]{1,0:T(8,128)(2,1)S(1)} %get-tuple-element.32.refs_2_, bf16[256,256]{1,0:T(8,128)(2,1)S(1)} %get-tuple-element.31.refs_3_, ...), custom_call_target="tpu_custom_call" | custom-call | flops 3221225472 | bytes 16777216 | tf_op jit(solution)/shard_map/to_modes/pallas_call | solution.py:618
  69.6 10.0 %interface.1 = (f32[256,512]{1,0:T(8,128)S(1)}, f32[256,512]{1,0:T(8,128)S(1)}) custom-call(f32[2048,1024]{1,0:T(8,128)} %get-tuple-element.19.modes_ref, bf16[32,256]{1,0:T(8,128)(2,1)S(1)} %get-tuple-element.34.high_ref, bf16[32,256]{1,0:T(8,128)(2,1)S(1)} %get-tuple-element.33.low_ref, f32[8,1024]{1,0:T(8,128)S(1)} %fusion.5.refs_4_.ratio_ref, ...), custom_call_target="tpu_custom_call" | custom-call | flops 402653184 | bytes 10485760 | tf_op jit(solution)/shard_map/interface/pallas_call | solution.py:630
  79.5 1.6 collective-permute-start.1
  81.1 0.1 fusion.9.ratio_ref
  81.2 9.0 %collective-permute-done.1.other_ref = f32[256,512]{1,0:T(8,128)S(1)} collective-permute-done((f32[256,512]{1,0:T(8,128)S(1)}, f32[256,512]{1,0:T(8,128)S(1)}, u32[]{:S(2)}, u32[]{:S(2)}) %collective-permute-start.1) | collective-permute-done | bytes 524320 | tf_op jit(solution)/shard_map/ppermute | solution.py:553
  90.2 11.9 %plane_sum.1 = (f32[256,512]{1,0:T(8,128)S(1)}, f32[2,16,512]{2,1,0:T(8,128)S(1)}) custom-call(f32[256,512]{1,0:T(8,128)S(1)} %get-tuple-element.21.own_ref, f32[256,512]{1,0:T(8,128)S(1)} %collective-permute-done.1.other_ref, f32[16,512]{1,0:T(8,128)S(1)} %fusion.9.ratio_ref), custom_call_target="tpu_custom_call" | custom-call | tf_op jit(solution)/shard_map/plane_sum/pallas_call | solution.py:642
  102.2 0.7 broadcast_in_dim.12.strength_ref
  102.8 5.7 %couple.1.own_ref = f32[256,512]{1,0:T(8,128)S(1)} custom-call(f32[256,512]{1,0:T(8,128)S(1)} %get-tuple-element.23.plane_ref.again_ref, f32[256,512]{1,0:T(8,128)S(1)} %get-tuple-element.23.plane_ref.again_ref, bf16[16,256]{1,0:T(8,128)(2,1)S(1)} %get-tuple-element.36.high_ref, bf16[16,256]{1,0:T(8,128)(2,1)S(1)} %get-tuple-element.35.low_ref, ...), custom_call_target="tpu_custom_call" | custom-call | flops 201326592 | bytes 4194304 | tf_op jit(solution)/shard_map/couple/pallas_call | solution.py:650
  108.5 1.4 collective-permute-start.2
  109.9 2.6 %broadcast_multiply_fusion = f32[2,32,4,32,8]{4,3,2,1,0:T(8,128)} fusion(f32[2,4,8]{2,1,0:T(4,128)S(1)} %gather_fusion, f32[32,32]{1,0:T(8,128)S(1)} %fusion.12), kind=kLoop, calls=%fused_computation.1 | loop fusion | flops 65536 | bytes 266496 | tf_op jit(solution)/shard_map/mul | solution.py:598
  112.6 4.0 %mul.190 = f32[256,256]{1,0:T(8,128)S(1)} reshape(f32[2,32,4,32,8]{4,3,2,1,0:T(8,128)} %broadcast_multiply_fusion) | data formatting | bytes 524288 | tf_op jit(solution)/shard_map/mul | solution.py:598
  116.6 2.6 %collective-permute-done.2.other_ref = f32[256,512]{1,0:T(8,128)S(1)} collective-permute-done((f32[256,512]{1,0:T(8,128)S(1)}, f32[256,512]{1,0:T(8,128)S(1)}, u32[]{:S(2)}, u32[]{:S(2)}) %collective-permute-start.2) | collective-permute-done | bytes 524320 | tf_op jit(solution)/shard_map/ppermute | solution.py:553
  119.2 0.1 broadcast_in_dim.13.weight_ref
  119.3 10.9 %plane_join.1 = (f32[256,1024]{1,0:T(8,128)S(1)}, f32[2,8,1024]{2,1,0:T(8,128)S(1)}) custom-call(f32[256,512]{1,0:T(8,128)S(1)} %couple.1.own_ref, f32[256,512]{1,0:T(8,128)S(1)} %collective-permute-done.2.other_ref, f32[8,1024]{1,0:T(8,128)S(1)} %fusion.5.refs_4_.ratio_ref, f32[8,1024]{1,0:T(8,128)S(1)} %broadcast_in_dim.13.weight_ref, ...), custom_call_target="tpu_custom_call" | custom-call | tf_op jit(solution)/shard_map/plane_join/pallas_call | solution.py:671
  130.2 0.0 copy-start.1
  130.2 13.2 %from_modes.1 = (f32[1024,1024]{1,0:T(8,128)S(1)}, f32[1024,1024]{1,0:T(8,128)}) custom-call(f32[2048,1024]{1,0:T(8,128)} %get-tuple-element.19.modes_ref, f32[256,1024]{1,0:T(8,128)S(1)} %get-tuple-element.25.plane_ref, f32[8,1024]{1,0:T(8,128)S(1)} %broadcast_in_dim.13.weight_ref, bf16[256,256]{1,0:T(8,128)(2,1)S(1)} %get-tuple-element.30.high_ref, ...), custom_call_target="tpu_custom_call" | custom-call | flops 3221225472 | bytes 16777216 | tf_op jit(solution)/shard_map/from_modes/pallas_call | solution.py:679
  143.4 1.9 %copy-done = f32[1024,1024]{1,0:T(8,128)} copy-done((f32[1024,1024]{1,0:T(8,128)}, f32[1024,1024]{1,0:T(8,128)S(1)}, u32[]{:S(2)}) %copy-start) | copy-done | bytes 4194328
  145.4 0.0 collective-permute-start.3
  145.4 7.4 %collective-permute-done.3.refs_1_ = f32[1024,1024]{1,0:T(8,128)S(1)} collective-permute-done((f32[1024,1024]{1,0:T(8,128)}, f32[1024,1024]{1,0:T(8,128)S(1)}, u32[]{:S(2)}, u32[]{:S(2)}) %collective-permute-start.3) | collective-permute-done | bytes 4194336 | tf_op jit(solution)/shard_map/ppermute | solution.py:550
  152.7 2.0 %copy-done.4 = f32[1024,1024]{1,0:T(8,128)} copy-done((f32[1024,1024]{1,0:T(8,128)}, f32[1024,1024]{1,0:T(8,128)S(1)}, u32[]{:S(2)}) %copy-start.4) | copy-done | bytes 4194328
  154.7 0.0 copy-done.1
  154.7 10.4 %backward_x.1 = f32[256,4,2048]{2,1,0:T(4,128)} custom-call(f32[1024,1024]{1,0:T(8,128)} %copy-done, f32[1024,1024]{1,0:T(8,128)} %copy-done.4, f32[8,256,256]{2,1,0:T(8,128)S(1)} %copy-done.1), custom_call_target="tpu_custom_call" | custom-call | flops 3221225472 | bytes 16777216 | tf_op jit(solution)/shard_map/backward_x/pallas_call | solution.py:693
  (20 shorter events, 0.2 us)
Async XLA Ops:
  0.9 1.6 copy-start.2
  2.5 13.2 %copy-start.10 = (f32[17]{0:T(128)S(1)}, f32[17]{0:T(128)}, u32[]{:S(2)}) copy-start(f32[17]{0:T(128)} %param.11) | copy-start | bytes 208
  2.5 14.7 %copy-start.6 = (f32[2048]{0:T(1024)S(1)}, f32[2048]{0:T(1024)}, u32[]{:S(2)}) copy-start(f32[2048]{0:T(1024)} %constant.84.clone) | copy-start | bytes 24580
  2.5 14.8 %copy-start.8 = (f32[24,16]{1,0:T(8,128)S(1)}, f32[24,16]{1,0:T(8,128)}, u32[]{:S(2)}) copy-start(f32[24,16]{1,0:T(8,128)} %constant.81.clone) | copy-start | bytes 4612
  2.5 14.8 %copy-start.7 = (f32[24,8]{1,0:T(8,128)S(1)}, f32[24,8]{1,0:T(8,128)}, u32[]{:S(2)}) copy-start(f32[24,8]{1,0:T(8,128)} %constant.82.clone) | copy-start | bytes 2308
  2.5 14.9 %copy-start.9 = (f32[16,24]{1,0:T(8,128)S(1)}, f32[16,24]{1,0:T(8,128)}, u32[]{:S(2)}) copy-start(f32[16,24]{1,0:T(8,128)} %constant.83.clone) | copy-start | bytes 4612
  15.3 28.8 %collective-permute-start = (f32[1024,1024]{1,0:T(8,128)}, f32[1024,1024]{1,0:T(8,128)}, u32[]{:S(2)}, u32[]{:S(2)}) collective-permute-start(f32[1024,1024]{1,0:T(8,128)} %get-tuple-element.18), channel_id=1, source_target_pairs={{0,1},{1,0},{2,3},{3,2},{4,5},{5,4},{6,7},{7,6},{8,9},{9,8},{10,11... | collective-permute-start | bytes 12582920 | tf_op jit(solution)/shard_map/ppermute | solution.py:550
  37.1 6.8 %copy-start.5 = (f32[40,128]{1,0:T(8,128)S(1)}, f32[40,128]{1,0:T(8,128)}, u32[]{:S(2)}) copy-start(f32[40,128]{1,0:T(8,128)} %eigen.1) | copy-start | bytes 61444
  37.1 6.9 %dynamic-slice-start = ((f32[2048]{0:T(1024)}, s32[]{:T(128)}), f32[1024]{0:T(1024)S(1)}, s32[]{:S(2)}) async-start(f32[2048]{0:T(1024)} %constant.84.clone, s32[]{:T(128)} %select_n.81), calls=%async_computation | async-start | bytes 8704 | tf_op jit(solution)/shard_map/dynamic_slice | solution.py:586
  44.1 2.2 %copy-start.3 = (f32[1024,1024]{1,0:T(8,128)S(1)}, f32[1024,1024]{1,0:T(8,128)}, u32[]{:S(2)}) copy-start(f32[1024,1024]{1,0:T(8,128)} %get-tuple-element.17.refs_0_) | copy-start | bytes 12582916
  79.5 10.7 %collective-permute-start.1 = (f32[256,512]{1,0:T(8,128)S(1)}, f32[256,512]{1,0:T(8,128)S(1)}, u32[]{:S(2)}, u32[]{:S(2)}) collective-permute-start(f32[256,512]{1,0:T(8,128)S(1)} %get-tuple-element.22), channel_id=1, source_target_pairs={{0,2},{1,3},{2,0},{3,1},{4,6},{5,7},{6,4},{7,5},{8,10},{9,11},{10,... | collective-permute-start | bytes 1572872 | tf_op jit(solution)/shard_map/ppermute | solution.py:553
  108.5 10.7 %collective-permute-start.2 = (f32[256,512]{1,0:T(8,128)S(1)}, f32[256,512]{1,0:T(8,128)S(1)}, u32[]{:S(2)}, u32[]{:S(2)}) collective-permute-start(f32[256,512]{1,0:T(8,128)S(1)} %couple.1.own_ref), channel_id=1, source_target_pairs={{0,2},{1,3},{2,0},{3,1},{4,6},{5,7},{6,4},{7,5},{8,10},{9,11},{10,... | collective-permute-start | bytes 1572872 | tf_op jit(solution)/shard_map/ppermute | solution.py:553
  130.2 24.5 %copy-start.1 = (f32[8,256,256]{2,1,0:T(8,128)S(1)}, f32[8,256,256]{2,1,0:T(8,128)}, u32[]{:S(2)}) copy-start(f32[8,256,256]{2,1,0:T(8,128)} %constant.85.clone.refs_2_) | copy-start | bytes 6291460
  143.4 1.9 %copy-start = (f32[1024,1024]{1,0:T(8,128)}, f32[1024,1024]{1,0:T(8,128)S(1)}, u32[]{:S(2)}) copy-start(f32[1024,1024]{1,0:T(8,128)S(1)} %get-tuple-element.27.refs_0_) | copy-start | bytes 12582916
  145.4 7.4 %collective-permute-start.3 = (f32[1024,1024]{1,0:T(8,128)}, f32[1024,1024]{1,0:T(8,128)S(1)}, u32[]{:S(2)}, u32[]{:S(2)}) collective-permute-start(f32[1024,1024]{1,0:T(8,128)} %get-tuple-element.28), channel_id=1, source_target_pairs={{0,1},{1,0},{2,3},{3,2},{4,5},{5,4},{6,7},{7,6},{8,9},{9,8},{10,11... | collective-permute-start | bytes 12582920 | tf_op jit(solution)/shard_map/ppermute | solution.py:550
  152.7 2.0 %copy-start.4 = (f32[1024,1024]{1,0:T(8,128)}, f32[1024,1024]{1,0:T(8,128)S(1)}, u32[]{:S(2)}) copy-start(f32[1024,1024]{1,0:T(8,128)S(1)} %collective-permute-done.3.refs_1_) | copy-start | bytes 12582916

commit v3 on v2

--- a/solution.py
+++ b/solution.py
@@ -16,6 +16,7 @@
 VMEM_BYTES = 48 * 1024 * 1024
 
 f32 = jnp.float32
+highest = lax.Precision.HIGHEST
 bf16 = jnp.bfloat16
 
 
@@ -23,11 +24,6 @@
     high = values.astype(bf16)
     low = (values - high.astype(f32)).astype(bf16)
     return high, low
-
-
-def split_outside(values):
-    high = lax.reduce_precision(values, 8, 7)
-    return high.astype(bf16), (values - high).astype(bf16)
 
 
 def dot3(left, right):
@@ -204,8 +200,8 @@
     lax.fori_loop(0, rows // pair, group, 0, unroll=4)
 
 
-def eigen_kernel(start_ref, out_ref, *, sizes, top):
-    lanes = start_ref.shape[1]
+def jacobi(start, sizes, top):
+    lanes = start.shape[1]
     lane = lax.broadcasted_iota(jnp.int32, (1, lanes), 1)
     in_first = lane < sizes[0]
     local = jnp.where(in_first, lane, lane - sizes[0])
@@ -240,37 +236,83 @@
     def going(carry):
         return (carry[2] > 1e-4) & (carry[1] < 20)
 
-    values, _, _ = lax.while_loop(going, sweep, (start_ref[...], jnp.int32(0), jnp.float32(1.0)))
-    out_ref[...] = values
-
-
-def eigen(weights):
-    sizes = tuple(weight.shape[0] - 1 for weight in weights)
-    top = -(-(sizes[0] + 1) // 8) * 8
-    low = -(-sizes[0] // 8) * 8
+    return lax.while_loop(going, sweep, (start, jnp.int32(0), jnp.float32(1.0)))[0]
+
+
+def levels_kernel(
+    couplings_ref, eigen_ref, to_high, to_low, from_high, from_low, edge_high, edge_low, jump_high, jump_low,
+    ratio_ref, full_ref, weight_ref, *, group,
+):
+    modes, share = ratio_ref.shape
+    all_modes, piece = full_ref.shape
     lanes = 128
-    columns = []
-    turns = []
-    for size, weight in zip(sizes, weights):
-        differences = np.zeros((top, size), np.float32)
-        differences[np.arange(size), np.arange(size)] = 1.0
-        differences[np.arange(size) + 1, np.arange(size)] = -1.0
-        columns.append(differences * jnp.pad(jnp.sqrt(weight), (0, top - size - 1))[:, None])
-        turns.append(np.eye(low, size, dtype=np.float32))
-    start = jnp.concatenate([jnp.concatenate(columns, 1), jnp.asarray(np.concatenate(turns, 1))], 0)
-    start = jnp.pad(start, ((0, 0), (0, lanes - sum(sizes))))
-    turned = pl.pallas_call(
-        functools.partial(eigen_kernel, sizes=sizes, top=top),
-        out_shape=jax.ShapeDtypeStruct(start.shape, f32),
-        name="eigen",
-    )(start)
-    found = []
-    first = 0
-    for size in sizes:
-        part = turned[:, first : first + size]
-        found.append((jnp.sum(part[:top] ** 2, axis=0), part[top : top + size]))
-        first += size
-    return found
+    rows = to_high.shape[0]
+    chunk = edge_high.shape[0]
+    levels = modes // group
+    top = -(-(all_modes + 1) // 8) * 8
+    low = -(-all_modes // 8) * 8
+    half, own = half_place()
+    exact = functools.partial(jnp.dot, precision=highest, preferred_element_type=f32)
+
+    def iota(shape, axis):
+        return lax.broadcasted_iota(jnp.int32, shape, axis)
+
+    def spot(condition):
+        return jnp.where(condition, 1.0, 0.0)
+
+    row, lane = iota((top, lanes), 0), iota((top, lanes), 1)
+    in_first = lane < all_modes
+    local = jnp.where(in_first, lane, lane - all_modes)
+    used = lane < all_modes + modes
+    weights = jnp.zeros((top, lanes), f32)
+    for place in range(all_modes + 1):
+        weights = jnp.where(in_first & (row == place), couplings_ref[place], weights)
+    cut = jnp.where(half == 0, modes, 0)
+    for place in range(modes + 1):
+        value = couplings_ref[half * modes + place] * jnp.where(cut == place, 2.0, 1.0)
+        weights = jnp.where(jnp.logical_not(in_first) & (row == place), value, weights)
+    head = jnp.sqrt(weights) * (spot(used & (row == local)) - spot(used & (row == local + 1)))
+    tail = spot(used & (row == local))[:low]
+    turned = jacobi(jnp.concatenate([head, tail], 0), (all_modes, modes), top)
+    head, vectors = turned[:top], turned[top : top + low]
+    values = jnp.sum(head * head, axis=0, keepdims=True)
+
+    at, to = iota((rows, low), 0), iota((rows, low), 1)
+    section = at // (chunk * levels)
+    level = lax.rem(own - section + group, group) * levels + lax.rem(at, levels)
+    pick = spot(to == level)
+    column = iota((lanes, rows), 1)
+    place = spot(iota((lanes, rows), 0) == all_modes + lax.rem(column, modes))
+    spread = exact(exact(pick, vectors), place)
+    at, to = iota((rows, rows), 0), iota((rows, rows), 1)
+    spread = jnp.where(lax.rem(at // levels, chunk) == to // modes, spread, 0.0)
+    from_high[...], from_low[...] = split(spread)
+    to_high[...], to_low[...] = split(spread.T)
+
+    edge = jnp.where(half == 0, vectors[modes - 1 : modes], vectors[0:1])
+    line = exact(jnp.broadcast_to(edge, (8, lanes)), place)[0:1]
+    at, to = iota((chunk, rows), 0), iota((chunk, rows), 1)
+    edge_high[...], edge_low[...] = split(jnp.where(at == to // modes, line, 0.0))
+    jump = couplings_ref[modes] * (vectors[modes - 1 : modes] + vectors[modes : modes + 1])
+    thin, plane_rows = jump_high.shape
+    column = iota((lanes, plane_rows), 1)
+    place = spot(iota((lanes, plane_rows), 0) == lax.rem(column, all_modes))
+    line = exact(jnp.broadcast_to(jump * jump, (8, lanes)), place)[0:1]
+    at, to = iota((thin, plane_rows), 0), iota((thin, plane_rows), 1)
+    jump_high[...], jump_low[...] = split(jnp.where(at == to // all_modes, line, 0.0))
+
+    def decay(count, first, mine):
+        at, to = iota((count, lanes), 0), iota((count, lanes), 1)
+        own_values = jnp.sum(jnp.where(to == at + first, values, 0.0), axis=1, keepdims=True)
+        sigma = own_values + mine
+        return 1.0 / (1.0 + 0.5 * sigma + jnp.sqrt(sigma + 0.25 * sigma * sigma))
+
+    start = pl.multiple_of(own * share, share)
+    ratio_ref[...] = decay(modes, all_modes, eigen_ref[:, pl.ds(start, share)])
+    full_ref[...] = decay(all_modes, 0, eigen_ref[:, pl.ds(pl.multiple_of(start + half * piece, piece), piece)])
+    at, to = iota((modes, lanes), 0), iota((modes, lanes), 1)
+    weight = jnp.sum(jnp.where(to == at + all_modes, edge, 0.0), axis=1, keepdims=True)
+    weight_ref[...] = jnp.broadcast_to(weight, (modes, share))
 
 
 def power(value, exponent):
@@ -465,12 +507,13 @@
 
 
 def couple_kernel(
-    plane_ref, again_ref, high_ref, low_ref, ratio_ref, edge_ref, strength_ref, out_ref, held, chunk, carry
+    plane_ref, again_ref, high_ref, low_ref, ratio_ref, edge_ref, couplings_ref, out_ref, held, chunk, carry
 ):
     shape = ratio_ref.shape
+    strength = couplings_ref[shape[0] // 2]
 
     def finish(values):
-        out_ref[...] = dot3((high_ref[...], low_ref[...]), values) + again_ref[...] * strength_ref[...]
+        out_ref[...] = dot3((high_ref[...], low_ref[...]), values) + again_ref[...] * strength
 
     two_way(
         out_ref.shape[0], ratio_ref, edge_ref, held, chunk, carry,
@@ -478,22 +521,64 @@
     )
 
 
-def from_modes_kernel(modes_ref, plane_ref, weight_ref, high_ref, low_ref, ratio_ref, edge_ref, *rest):
-    out_refs, (held, chunk, carry) = rest[:-3], rest[-3:]
+def from_modes_kernel(modes_ref, plane_ref, weight_ref, high_ref, low_ref, ratio_ref, edge_ref, *rest, group):
+    out_refs, (held, chunk, carry, *remote) = rest[:group], rest[group:]
     modes, share = ratio_ref.shape
     rows = plane_ref.shape[0]
     weight = weight_ref[...]
+    step = pl.program_id(0)
+    steps = pl.num_programs(0) // 2
+    half, own = half_place()
+    each = out_refs[0].shape[0]
+    targets = [half * group + lax.rem(own + group - hop, group) for hop in range(1, group)]
+
+    def copy(hop, index):
+        outgoing, send_sem, recv_sem = remote
+        place = pl.ds(pl.multiple_of(index * each, each), each)
+        return pltpu.make_async_remote_copy(
+            src_ref=outgoing.at[hop - 1, place],
+            dst_ref=out_refs[hop].at[place],
+            send_sem=send_sem.at[hop - 1, index],
+            recv_sem=recv_sem.at[hop - 1, index],
+            device_id={"lev": targets[hop - 1]},
+            device_id_type=pl.DeviceIdType.MESH,
+        )
+
+    if group > 1:
+
+        @pl.when(step == 0)
+        def _():
+            barrier = pltpu.get_barrier_semaphore()
+            for target in targets:
+                pl.semaphore_signal(barrier, inc=1, device_id={"lev": target}, device_id_type=pl.DeviceIdType.MESH)
+
+        @pl.when(step == steps)
+        def _():
+            pl.semaphore_wait(pltpu.get_barrier_semaphore(), group - 1)
 
     def finish(values):
         result = dot3((high_ref[...], low_ref[...]), values)
-        each = out_refs[0].shape[0]
-        for index, out_ref in enumerate(out_refs):
-            out_ref[...] = result[index * each : (index + 1) * each]
+        out_refs[0][...] = result[:each]
+        index = 2 * steps - 1 - step
+        for hop in range(1, group):
+            remote[0][hop - 1, pl.ds(pl.multiple_of(index * each, each), each), :] = result[hop * each : (hop + 1) * each]
+            copy(hop, index).start()
 
     two_way(
         rows, ratio_ref, edge_ref, held, chunk, carry,
         lambda row: modes_ref[row * modes : (row + 1) * modes, :] + weight * plane_ref[row : row + 1, :], finish,
     )
+
+    if group > 1:
+
+        @pl.when(step == 2 * steps - 1)
+        def _():
+            def settle(index, unused):
+                for hop in range(1, group):
+                    copy(hop, index).wait()
+                return unused
+
+            lax.fori_loop(0, steps, settle, 0)
 
 
 def params(collective_id=None):
@@ -524,17 +609,11 @@
     return jax.ShapeDtypeStruct(shape, f32)
 
 
-def decay(values, eigen_x):
-    sigma = values[:, None] + eigen_x[None, :]
-    return 1.0 / (1.0 + 0.5 * sigma + jnp.sqrt(sigma + 0.25 * sigma * sigma))
-
-
 def body(source, solid, couplings):
     row_count, levels, length = source.shape
     lev_devices = lax.axis_size("lev")
     row_devices = lax.axis_size("rows")
     group = lev_devices // 2
-    half, own = half_place()
     share = length // group
     piece = share // 2
     width = length // PARTS
@@ -576,28 +655,21 @@
     )(source, keep, forward_table)
     sections = [spectral[0]] + [passed(spectral[shift], shift) for shift in range(1, group)]
 
-    middle = couplings[half_levels]
-    edge_at = jnp.where(half == 0, half_levels, 0)
-    mine = lax.dynamic_slice_in_dim(couplings, half * half_levels, half_levels + 1)
-    mine = jnp.where(jnp.arange(half_levels + 1) == edge_at, 2.0 * middle, mine)
-    (full_values, full_vectors), (values, vectors) = eigen([couplings, mine])
-    edge_weight = jnp.where(half == 0, vectors[half_levels - 1], vectors[0])
-    jump = middle * (full_vectors[half_levels - 1] + full_vectors[half_levels])
-    eigen_x = lax.dynamic_slice_in_dim(jnp.asarray(eigen_x), own * share, share)
-    ratio = decay(values, eigen_x)
-    full_ratio = decay(full_values, lax.dynamic_slice_in_dim(eigen_x, half * piece, piece))
-
     chunk = max(BY, 256 // half_levels)
     thin = max(BY, 256 // all_levels)
     rows = chunk * half_levels
     plane_rows = thin * all_levels
-    order = jnp.mod(own - jnp.arange(group), group)
-    turned = vectors.reshape(group, levels, half_levels)[order]
-    eye = jnp.eye(chunk, dtype=f32)
-    to_modes = (eye[:, None, None, :, None] * turned.transpose(2, 0, 1)[None, :, :, None, :]).reshape(rows, rows)
-    from_modes = (eye[None, :, None, :, None] * turned[:, None, :, None, :]).reshape(rows, rows)
-    to_edge = (eye[:, :, None] * edge_weight).reshape(chunk, rows)
-    to_jump = (jnp.eye(thin, dtype=f32)[:, :, None] * (jump * jump)).reshape(thin, plane_rows)
+    in_smem = pl.BlockSpec(memory_space=pltpu.SMEM)
+    built = [(rows, rows)] * 4 + [(chunk, rows)] * 2 + [(thin, plane_rows)] * 2
+    *matrices, ratio, full_ratio, weight = pl.pallas_call(
+        functools.partial(levels_kernel, group=group),
+        in_specs=[in_smem, pl.BlockSpec(memory_space=pltpu.VMEM)],
+        out_shape=[jax.ShapeDtypeStruct(each, bf16) for each in built]
+        + [struct(half_levels, share), struct(all_levels, piece), struct(half_levels, share)],
+        compiler_params=params(),
+        name="levels",
+    )(couplings, eigen_x[None, :])
+    to_modes, from_modes, to_edge, to_jump = (matrices[2 * index : 2 * index + 2] for index in range(4))
 
     steps = row_count // chunk
     plane_steps = row_count // thin
@@ -625,7 +697,7 @@
         compiler_params=params(0),
         cost_estimate=cost(6 * size * rows, 8 * size),
         name="to_modes",
-    )(*sections, *split_outside(to_modes), ratio)
+    )(*sections, *to_modes, ratio)
 
     kept, sent = pl.pallas_call(
         interface_kernel,
@@ -637,7 +709,7 @@
         compiler_params=params(),
         cost_estimate=cost(6 * size * chunk, 5 * size),
         name="interface",
-    )(modes, *split_outside(to_edge), ratio, edge)
+    )(modes, *to_edge, ratio, edge)
 
     plane, plane_edge = pl.pallas_call(
         sum_kernel,
@@ -657,7 +729,7 @@
             whole((thin, plane_rows)),
             whole(plane_shape),
             whole((2,) + plane_shape),
-            whole((1, piece)),
+            in_smem,
         ],
         out_specs=pl.BlockSpec((thin, piece), behind(plane_steps)),
         out_shape=struct(row_count, piece),
@@ -665,9 +737,8 @@
         compiler_params=params(),
         cost_estimate=cost(6 * size * thin, 2 * size),
         name="couple",
-    )(plane, plane, *split_outside(to_jump), full_ratio, plane_edge, jnp.full((1, piece), middle))
-
-    weight = jnp.broadcast_to(edge_weight[:, None], shape)
+    )(plane, plane, *to_jump, full_ratio, plane_edge, couplings)
+
     joined, edge = pl.pallas_call(
         join_kernel,
         out_shape=[struct(row_count, share), struct(2, *shape)],
@@ -676,20 +747,24 @@
         name="plane_join",
     )(moved, across_halves(moved), ratio, weight, edge)
 
-    solved = pl.pallas_call(
-        from_modes_kernel,
+    outgoing = [
+        pltpu.VMEM((group - 1, row_count * levels, share), f32),
+        pltpu.SemaphoreType.DMA((group - 1, steps)),
+        pltpu.SemaphoreType.DMA((group - 1, steps)),
+    ]
+    returned = pl.pallas_call(
+        functools.partial(from_modes_kernel, group=group),
         grid=(2 * steps,),
         in_specs=[pl.BlockSpec((rows, share), ahead(steps)), pl.BlockSpec((chunk, share), ahead(steps)), whole(shape)]
         + [whole((rows, rows))] * 2
         + [whole(shape), whole((2,) + shape)],
-        out_specs=[pl.BlockSpec((chunk * levels, share), behind(steps))] * group,
+        out_specs=[pl.BlockSpec((chunk * levels, share), behind(steps))] + [pl.BlockSpec(memory_space=pl.ANY)] * (group - 1),
         out_shape=[struct(row_count * levels, share)] * group,
-        scratch_shapes=scratch(rows, shape),
-        compiler_params=params(),
+        scratch_shapes=scratch(rows, shape) + (outgoing if group > 1 else []),
+        compiler_params=params(3 if group > 1 else None),
         cost_estimate=cost(6 * size * rows, 8 * size),
         name="from_modes",
-    )(modes, joined, weight, *split_outside(from_modes), ratio, edge)
-    returned = [solved[0]] + [passed(solved[shift], group - shift) for shift in range(1, group)]
+    )(modes, joined, weight, *from_modes, ratio, edge)
     return pl.pallas_call(
         backward_kernel,
         grid=(row_count // tile,),

time: 166 us -> 146 us (0.88)
  local copies, waits for them, and re-layouts: 19.3 us -> 7.75 us
  other arithmetic: 9.59 us -> 0.86 us
  Pallas kernels: 113 us -> 116 us
    mul x11 -> x0, local copies, waits for them, and re-layouts: 8.62 us -> none  [the longest x2 4.15 us: body(): eye[:, None, None, :, None] * turned.transpose(2, 0, 1)[None, :, :, None, :]]
    ppermute x2 -> x1, waiting for transfers between devices: 7.37 us -> 0.01 us  [passed(): return lax.ppermute(value, 'lev', pairs)]
    ppermute x2, waiting for transfers between devices: 11.6 us -> 18.3 us  [across_halves(): lax.ppermute(value, 'lev', [(place, (place + group) % lev_devices) for pl...]
    mul x5 -> x0, other arithmetic: 6.71 us -> none  [the longest x1 2.61 us: body(): eye[None, :, None, :, None] * turned[:, None, :, None, :]]
    unnamed x22 -> x14, local copies, waits for them, and re-layouts: 7.74 us -> 7.73 us
  transfers between devices with their start and end apart: 4 -> 3, of which waited for: 3 -> 2; matrix products, arithmetic and copies ran while one was open for 12% -> 0% of each run, Pallas kernels for 9% -> 10%
where the time goes in v3:
time: 146 us
  Pallas kernels  116 us (79%)
  waiting for transfers between devices  18.3 us (13%)
  local copies, waits for them, and re-layouts  7.75 us (5%)
  starting transfers between devices  3.48 us (2%)
    pallas_call x1, Pallas kernels, body(): pl.pallas_call(to_modes_kernel, grid=(steps,), in_specs=[section_spec] *...  23.2 us
    ppermute x2, waiting for transfers between devices, across_halves(): lax.ppermute(value, 'lev', [(place, (place + group) % lev_devices) for pl...  18.3 us
    pallas_call x1, Pallas kernels, body(): pl.pallas_call(functools.partial(levels_kernel, group=group), in_specs=[i...  15 us
    pallas_call x1, Pallas kernels, body(): pl.pallas_call(functools.partial(from_modes_kernel, group=group), grid=(2...  14.5 us
    pallas_call x1, Pallas kernels, body(): pl.pallas_call(forward_kernel, grid=(row_count // tile,), in_specs=[field...  12.8 us
    pallas_call x1, Pallas kernels, body(): pl.pallas_call(sum_kernel, out_shape=[struct(row_count, piece), struct(2,...  11.9 us
    pallas_call x1, Pallas kernels, body(): pl.pallas_call(join_kernel, out_shape=[struct(row_count, share), struct(2...  11 us
    pallas_call x1, Pallas kernels, body(): pl.pallas_call(backward_kernel, grid=(row_count // tile,), in_specs=[part...  10.4 us
  transfers between devices with their start and end apart: 3, of which 2 were waited for; matrix products, arithmetic and copies ran while one was open for 0% of the time, Pallas kernels for 10%

profile of v3, /device:TPU:0, one launch (start us, length us, event | category | flops | bytes accessed | tf_op | source)
XLA Modules:
  0.0 146.0 jit_solution(16090057209347346165)
XLA Ops:
  0.0 0.9 subtract_convert_fusion
  0.9 0.0 copy-start.4
  0.9 1.6 %copy-done.4 = f32[8,256,256]{2,1,0:T(8,128)S(1)} copy-done((f32[8,256,256]{2,1,0:T(8,128)S(1)}, f32[8,256,256]{2,1,0:T(8,128)}, u32[]{:S(2)}) %copy-start.4) | copy-done | bytes 2097176
  2.5 0.0 copy-start.2
  2.5 0.0 copy-start.3
  2.5 12.8 %forward_x.1 = (f32[1024,1024]{1,0:T(8,128)}, f32[1024,1024]{1,0:T(8,128)}) custom-call(f32[256,4,2048]{2,1,0:T(4,128)} %x_ref.1, bf16[256,32]{1,0:T(8,128)(2,1)S(1)} %bitcast.1, f32[8,256,256]{2,1,0:T(8,128)S(1)} %copy-done.4), custom_call_target="tpu_custom_call" | custom-call | flops 3221225472 | bytes 16777216 | tf_op jit(solution)/shard_map/forward_x/pallas_call | solution.py:645
  15.3 0.4 collective-permute-start
  15.7 0.0 copy-done.2
  15.7 0.0 copy-done.3
  15.7 15.0 %levels.1 = (bf16[256,256]{1,0:T(8,128)(2,1)S(1)}, bf16[256,256]{1,0:T(8,128)(2,1)S(1)}, bf16[256,256]{1,0:T(8,128)(2,1)S(1)}, bf16[256,256]{1,0:T(8,128)(2,1)S(...) custom-call(f32[17]{0:T(128)S(1)} %copy-done.3, ...), custom_call_target="tpu_custom_call" | custom-call | tf_op jit(solution)/shard_map/levels/pallas_call | solution.py:664
  30.7 0.0 collective-permute-done.refs_1_
  30.7 0.0 copy-start.6
  30.7 2.0 %copy-done.6 = f32[1024,1024]{1,0:T(8,128)} copy-done((f32[1024,1024]{1,0:T(8,128)}, f32[1024,1024]{1,0:T(8,128)S(1)}, u32[]{:S(2)}) %copy-start.6) | copy-done | bytes 4194328
  32.7 0.0 copy-start.5
  32.7 2.2 %copy-done.5 = f32[1024,1024]{1,0:T(8,128)S(1)} copy-done((f32[1024,1024]{1,0:T(8,128)S(1)}, f32[1024,1024]{1,0:T(8,128)}, u32[]{:S(2)}) %copy-start.5) | copy-done | bytes 4194328
  34.9 23.2 %to_modes.1 = (f32[2048,1024]{1,0:T(8,128)}, f32[2,8,1024]{2,1,0:T(8,128)S(1)}) custom-call(f32[1024,1024]{1,0:T(8,128)S(1)} %copy-done.5, f32[1024,1024]{1,0:T(8,128)} %copy-done.6, bf16[256,256]{1,0:T(8,128)(2,1)S(1)} %get-tuple-element.30.refs_2_, bf16[256,256]{1,0:T(8,128)(2,1)S(1)} %get-tuple-element.31.refs_3_, ...), custom_call_target="tpu_custom_call" | custom-call | flops 3221225472 | bytes 16777216 | tf_op jit(solution)/shard_map/to_modes/pallas_call | solution.py:690
  58.1 10.0 %interface.1 = (f32[256,512]{1,0:T(8,128)S(1)}, f32[256,512]{1,0:T(8,128)S(1)}) custom-call(f32[2048,1024]{1,0:T(8,128)} %get-tuple-element.33.modes_ref, bf16[32,256]{1,0:T(8,128)(2,1)S(1)} %get-tuple-element.34.high_ref, bf16[32,256]{1,0:T(8,128)(2,1)S(1)} %get-tuple-element.35.low_ref, f32[8,1024]{1,0:T(8,128)S(1)} %get-tuple-element.32.refs_4_.ratio_ref, ...), custom_call_target="tpu_custom_call" | custom-call | flops 402653184 | bytes 10485760 | tf_op jit(solution)/shard_map/interface/pallas_call | solution.py:702
  68.1 1.6 %collective-permute-start.1 = (f32[256,512]{1,0:T(8,128)S(1)}, f32[256,512]{1,0:T(8,128)S(1)}, u32[]{:S(2)}, u32[]{:S(2)}) collective-permute-start(f32[256,512]{1,0:T(8,128)S(1)} %get-tuple-element.38), channel_id=1, source_target_pairs={{0,2},{1,3},{2,0},{3,1},{4,6},{5,7},{6,4},{7,5},{8,10},{9,11},{10,... | collective-permute-start | bytes 1572872 | tf_op jit(solution)/shard_map/ppermute | solution.py:632
  69.7 9.1 %collective-permute-done.1.other_ref = f32[256,512]{1,0:T(8,128)S(1)} collective-permute-done((f32[256,512]{1,0:T(8,128)S(1)}, f32[256,512]{1,0:T(8,128)S(1)}, u32[]{:S(2)}, u32[]{:S(2)}) %collective-permute-start.1) | collective-permute-done | bytes 524320 | tf_op jit(solution)/shard_map/ppermute | solution.py:632
  78.8 11.9 %plane_sum.1 = (f32[256,512]{1,0:T(8,128)S(1)}, f32[2,16,512]{2,1,0:T(8,128)S(1)}) custom-call(f32[256,512]{1,0:T(8,128)S(1)} %get-tuple-element.37.own_ref, f32[256,512]{1,0:T(8,128)S(1)} %collective-permute-done.1.other_ref, f32[16,512]{1,0:T(8,128)S(1)} %get-tuple-element.39.ratio_ref), custom_call_target="tpu_custom_call" | custom-call | tf_op jit(solution)/shard_map/plane_sum/pallas_call | solution.py:714
  90.7 6.8 %couple.1.own_ref = f32[256,512]{1,0:T(8,128)S(1)} custom-call(f32[256,512]{1,0:T(8,128)S(1)} %get-tuple-element.40.plane_ref.again_ref, f32[256,512]{1,0:T(8,128)S(1)} %get-tuple-element.40.plane_ref.again_ref, bf16[16,256]{1,0:T(8,128)(2,1)S(1)} %get-tuple-element.41.high_ref, bf16[16,256]{1,0:T(8,128)(2,1)S(1)} %get-tuple-element.42.low_ref, ...), custom_call_target="tpu_custom_call" | custom-call | flops 201326592 | bytes 4194304 | tf_op jit(solution)/shard_map/couple/pallas_call | solution.py:722
  97.5 1.4 collective-permute-start.2
  98.9 9.3 %collective-permute-done.2.other_ref = f32[256,512]{1,0:T(8,128)S(1)} collective-permute-done((f32[256,512]{1,0:T(8,128)S(1)}, f32[256,512]{1,0:T(8,128)S(1)}, u32[]{:S(2)}, u32[]{:S(2)}) %collective-permute-start.2) | collective-permute-done | bytes 524320 | tf_op jit(solution)/shard_map/ppermute | solution.py:632
  108.1 11.0 %plane_join.1 = (f32[256,1024]{1,0:T(8,128)S(1)}, f32[2,8,1024]{2,1,0:T(8,128)S(1)}) custom-call(f32[256,512]{1,0:T(8,128)S(1)} %couple.1.own_ref, f32[256,512]{1,0:T(8,128)S(1)} %collective-permute-done.2.other_ref, f32[8,1024]{1,0:T(8,128)S(1)} %get-tuple-element.32.refs_4_.ratio_ref, f32[8,1024]{1,0:T(8,128)S(1)} %get-tuple-element.44.weight_ref, ...), custom_call_target="tpu_custom_call" | custom-call | tf_op jit(solution)/shard_map/plane_join/pallas_call | solution.py:742
  119.2 0.0 copy-start.1
  119.2 14.5 %from_modes.1 = (f32[1024,1024]{1,0:T(8,128)S(1)}, f32[1024,1024]{1,0:T(8,128)}) custom-call(f32[2048,1024]{1,0:T(8,128)} %get-tuple-element.33.modes_ref, f32[256,1024]{1,0:T(8,128)S(1)} %get-tuple-element.45.plane_ref, f32[8,1024]{1,0:T(8,128)S(1)} %get-tuple-element.44.weight_ref, bf16[256,256]{1,0:T(8,128)(2,1)S(1)} %get-tuple-element.46.high_ref, ...), custom_call_target="tpu_custom_call" | custom-call | flops 3221225472 | bytes 16777216 | tf_op jit(solution)/shard_map/from_modes/pallas_call | solution.py:755
  133.6 0.0 copy-start
  133.6 2.0 %copy-done = f32[1024,1024]{1,0:T(8,128)} copy-done((f32[1024,1024]{1,0:T(8,128)}, f32[1024,1024]{1,0:T(8,128)S(1)}, u32[]{:S(2)}) %copy-start) | copy-done | bytes 4194328
  135.6 0.0 copy-done.1
  135.6 10.4 %backward_x.1 = f32[256,4,2048]{2,1,0:T(4,128)} custom-call(f32[1024,1024]{1,0:T(8,128)} %copy-done, f32[1024,1024]{1,0:T(8,128)} %get-tuple-element.50.refs_1_, f32[8,256,256]{2,1,0:T(8,128)S(1)} %copy-done.1), custom_call_target="tpu_custom_call" | custom-call | flops 3221225472 | bytes 16777216 | tf_op jit(solution)/shard_map/backward_x/pallas_call | solution.py:768
  (1 shorter events, 0.0 us)
Async XLA Ops:
  0.9 1.6 %copy-start.4 = (f32[8,256,256]{2,1,0:T(8,128)S(1)}, f32[8,256,256]{2,1,0:T(8,128)}, u32[]{:S(2)}) copy-start(f32[8,256,256]{2,1,0:T(8,128)} %constant.8.clone.table_ref) | copy-start | bytes 6291460
  2.5 13.2 %copy-start.2 = (f32[1,2048]{1,0:T(1,128)S(1)}, f32[1,2048]{1,0:T(1,128)}, u32[]{:S(2)}) copy-start(f32[1,2048]{1,0:T(1,128)} %constant.9.clone.eigen_ref) | copy-start | bytes 24580
  2.5 13.2 %copy-start.3 = (f32[17]{0:T(128)S(1)}, f32[17]{0:T(128)}, u32[]{:S(2)}) copy-start(f32[17]{0:T(128)} %couplings_ref.3) | copy-start | bytes 208
  15.3 15.5 %collective-permute-start = (f32[1024,1024]{1,0:T(8,128)}, f32[1024,1024]{1,0:T(8,128)S(1)}, u32[]{:S(2)}, u32[]{:S(2)}) collective-permute-start(f32[1024,1024]{1,0:T(8,128)} %get-tuple-element.29), channel_id=1, source_target_pairs={{0,1},{1,0},{2,3},{3,2},{4,5},{5,4},{6,7},{7,6},{8,9},{9,8},{10,11... | collective-permute-start | bytes 12582920 | tf_op jit(solution)/shard_map/ppermute | solution.py:629
  30.7 2.0 %copy-start.6 = (f32[1024,1024]{1,0:T(8,128)}, f32[1024,1024]{1,0:T(8,128)S(1)}, u32[]{:S(2)}) copy-start(f32[1024,1024]{1,0:T(8,128)S(1)} %collective-permute-done.refs_1_) | copy-start | bytes 12582916
  32.7 2.2 %copy-start.5 = (f32[1024,1024]{1,0:T(8,128)S(1)}, f32[1024,1024]{1,0:T(8,128)}, u32[]{:S(2)}) copy-start(f32[1024,1024]{1,0:T(8,128)} %get-tuple-element.28.refs_0_) | copy-start | bytes 12582916
  68.1 10.7 %collective-permute-start.1 = (f32[256,512]{1,0:T(8,128)S(1)}, f32[256,512]{1,0:T(8,128)S(1)}, u32[]{:S(2)}, u32[]{:S(2)}) collective-permute-start(f32[256,512]{1,0:T(8,128)S(1)} %get-tuple-element.38), channel_id=1, source_target_pairs={{0,2},{1,3},{2,0},{3,1},{4,6},{5,7},{6,4},{7,5},{8,10},{9,11},{10,... | collective-permute-start | bytes 1572872 | tf_op jit(solution)/shard_map/ppermute | solution.py:632
  97.5 10.7 %collective-permute-start.2 = (f32[256,512]{1,0:T(8,128)S(1)}, f32[256,512]{1,0:T(8,128)S(1)}, u32[]{:S(2)}, u32[]{:S(2)}) collective-permute-start(f32[256,512]{1,0:T(8,128)S(1)} %couple.1.own_ref), channel_id=1, source_target_pairs={{0,2},{1,3},{2,0},{3,1},{4,6},{5,7},{6,4},{7,5},{8,10},{9,11},{10,... | collective-permute-start | bytes 1572872 | tf_op jit(solution)/shard_map/ppermute | solution.py:632
  119.2 16.4 %copy-start.1 = (f32[8,256,256]{2,1,0:T(8,128)S(1)}, f32[8,256,256]{2,1,0:T(8,128)}, u32[]{:S(2)}) copy-start(f32[8,256,256]{2,1,0:T(8,128)} %constant.10.clone.refs_2_) | copy-start | bytes 6291460
  133.6 2.0 %copy-start = (f32[1024,1024]{1,0:T(8,128)}, f32[1024,1024]{1,0:T(8,128)S(1)}, u32[]{:S(2)}) copy-start(f32[1024,1024]{1,0:T(8,128)S(1)} %get-tuple-element.49.refs_0_) | copy-start | bytes 12582916

commit v4 on v3

--- a/solution.py
+++ b/solution.py
@@ -13,7 +13,7 @@
 BY = 8
 BX = 64
 PARTS = 16
-VMEM_BYTES = 48 * 1024 * 1024
+VMEM_BYTES = 60 * 1024 * 1024
 
 f32 = jnp.float32
 highest = lax.Precision.HIGHEST
@@ -137,7 +137,7 @@
             high_ref[block], low_ref[block] = split(table_ref[block])
 
 
-def forward_kernel(x_ref, keep_ref, table_ref, *rest):
+def forward_kernel(x_ref, solid_ref, table_ref, *rest):
     out_refs, (kept, mixed, high_ref, low_ref) = rest[:-4], rest[-4:]
     rows, levels, length = x_ref.shape
     width = length // PARTS
@@ -148,7 +148,9 @@
     first = lax.broadcasted_iota(jnp.int32, shape, 0) * BX
     lane = lax.broadcasted_iota(jnp.int32, shape, 1)
     spread = jnp.where((lane >= first) & (lane < first + BX), 1.0, 0.0).astype(bf16)
-    kept[...] = jnp.dot(keep_ref[...], spread, preferred_element_type=f32)
+    keep = (1 - solid_ref[...]).astype(f32)
+    keep = jnp.concatenate([keep] * pair, 1).reshape(kept.shape[0], length // BX)
+    kept[...] = jnp.dot(keep.astype(bf16), spread, preferred_element_type=f32)
 
     def group(index, unused):
         mask = kept[pl.ds(pl.multiple_of(index * 8, 8), 8), :]
@@ -234,7 +236,7 @@
         return values, done + 1, jnp.max(worst)
 
     def going(carry):
-        return (carry[2] > 1e-4) & (carry[1] < 20)
+        return (carry[2] > 1e-5) & (carry[1] < 20)
 
     return lax.while_loop(going, sweep, (start, jnp.int32(0), jnp.float32(1.0)))[0]
 
@@ -450,20 +452,73 @@
         finish(split(chunk[...]))
 
 
-def interface_kernel(modes_ref, high_ref, low_ref, ratio_ref, edge_ref, keep_ref, send_ref, held, chunk, carry, line):
+class Mirror:
+    def __init__(self, received, outgoing, send_sem, recv_sem):
+        half, own = half_place()
+        self.target = (1 - half) * (lax.axis_size("lev") // 2) + own
+        self.refs = received, outgoing, send_sem, recv_sem
+        self.step = pl.program_id(0)
+        self.steps = pl.num_programs(0) // 2
+        self.rows = outgoing.shape[0]
+
+    def copy(self, index, rows):
+        received, outgoing, send_sem, recv_sem = self.refs
+        place = pl.ds(pl.multiple_of(index * rows, rows), rows)
+        return pltpu.make_async_remote_copy(
+            src_ref=outgoing.at[place],
+            dst_ref=received.at[place],
+            send_sem=send_sem.at[index],
+            recv_sem=recv_sem.at[index],
+            device_id={"lev": self.target},
+            device_id_type=pl.DeviceIdType.MESH,
+        )
+
+    def greet(self):
+        @pl.when(self.step == 0)
+        def _():
+            pl.semaphore_signal(
+                pltpu.get_barrier_semaphore(), inc=1, device_id={"lev": self.target}, device_id_type=pl.DeviceIdType.MESH
+            )
+
+        @pl.when(self.step == self.steps)
+        def _():
+            pl.semaphore_wait(pltpu.get_barrier_semaphore(), 1)
+
+    def send(self, values):
+        rows = values.shape[0]
+        index = 2 * self.steps - 1 - self.step
+        self.refs[1][pl.ds(pl.multiple_of(index * rows, rows), rows), :] = values
+        self.copy(index, rows).start()
+
+    def settle(self, rows):
+        @pl.when(self.step == 2 * self.steps - 1)
+        def _():
+            def one(index, unused):
+                self.copy(index, rows).wait()
+                return unused
+
+            lax.fori_loop(0, self.steps, one, 0)
+
+
+def interface_kernel(
+    modes_ref, high_ref, low_ref, ratio_ref, edge_ref, keep_ref, received, held, chunk, carry, line, *remote
+):
     modes = ratio_ref.shape[0]
     piece = keep_ref.shape[1]
     half, _ = half_place()
+    mirror = Mirror(received, *remote)
+    mirror.greet()
 
     def finish(values):
         line[...] = dot3((high_ref[...], low_ref[...]), values)
         keep_ref[...] = line[:, pl.ds(pl.multiple_of(half * piece, piece), piece)]
-        send_ref[...] = line[:, pl.ds(pl.multiple_of((1 - half) * piece, piece), piece)]
+        mirror.send(line[:, pl.ds(pl.multiple_of((1 - half) * piece, piece), piece)])
 
     two_way(
         keep_ref.shape[0], ratio_ref, edge_ref, held, chunk, carry,
         lambda row: modes_ref[row * modes : (row + 1) * modes, :], finish,
     )
+    mirror.settle(keep_ref.shape[0])
 
 
 def plane_ends(plane_ref, ratio_ref, ends, weight):
@@ -507,18 +562,24 @@
 
 
 def couple_kernel(
-    plane_ref, again_ref, high_ref, low_ref, ratio_ref, edge_ref, couplings_ref, out_ref, held, chunk, carry
+    plane_ref, again_ref, high_ref, low_ref, ratio_ref, edge_ref, couplings_ref, out_ref, received, held, chunk, carry,
+    *remote,
 ):
     shape = ratio_ref.shape
     strength = couplings_ref[shape[0] // 2]
+    mirror = Mirror(received, *remote)
+    mirror.greet()
 
     def finish(values):
-        out_ref[...] = dot3((high_ref[...], low_ref[...]), values) + again_ref[...] * strength
+        result = dot3((high_ref[...], low_ref[...]), values) + again_ref[...] * strength
+        out_ref[...] = result
+        mirror.send(result)
 
     two_way(
         out_ref.shape[0], ratio_ref, edge_ref, held, chunk, carry,
         lambda row: jnp.broadcast_to(plane_ref[row : row + 1, :], shape), finish,
     )
+    mirror.settle(out_ref.shape[0])
 
 
 def from_modes_kernel(modes_ref, plane_ref, weight_ref, high_ref, low_ref, ratio_ref, edge_ref, *rest, group):
@@ -628,14 +689,9 @@
         ]
         return lax.ppermute(value, "lev", pairs)
 
-    def across_halves(value):
-        return lax.ppermute(value, "lev", [(place, (place + group) % lev_devices) for place in range(lev_devices)])
-
     blocks, eigen_x = x_tables(length)
     forward_table = blocks.astype(np.float32)
     backward_table = np.swapaxes(blocks, 1, 2).astype(np.float32)
-    keep = (1 - solid).astype(bf16)[:, None]
-    keep = jnp.broadcast_to(keep, (keep.shape[0], 8 // levels) + keep.shape[2:]).reshape(-1, length // BX)
     groups = tile // BY * 8
     table = whole(blocks.shape)
     part_spec = pl.BlockSpec((tile * levels, share), lambda i: (i, 0))
@@ -645,14 +701,14 @@
     spectral = pl.pallas_call(
         forward_kernel,
         grid=(row_count // tile,),
-        in_specs=[field_spec, pl.BlockSpec((groups, length // BX), lambda i: (i, 0)), table],
+        in_specs=[field_spec, pl.BlockSpec((tile // BY, levels, length // BX), lambda i: (i, 0, 0)), table],
         out_specs=[part_spec] * group,
         out_shape=[struct(row_count * levels, share)] * group,
         scratch_shapes=[pltpu.VMEM((groups, length), f32), mixed] + halves,
         compiler_params=params(),
         cost_estimate=cost(6 * size * 2 * width, 8 * size),
         name="forward_x",
-    )(source, keep, forward_table)
+    )(source, solid, forward_table)
     sections = [spectral[0]] + [passed(spectral[shift], shift) for shift in range(1, group)]
 
     chunk = max(BY, 256 // half_levels)
@@ -699,14 +755,21 @@
         name="to_modes",
     )(*sections, *to_modes, ratio)
 
-    kept, sent = pl.pallas_call(
+    def mirrored(count):
+        return [
+            pltpu.VMEM((row_count, piece), f32),
+            pltpu.SemaphoreType.DMA((count,)),
+            pltpu.SemaphoreType.DMA((count,)),
+        ]
+
+    kept, received = pl.pallas_call(
         interface_kernel,
         grid=(2 * steps,),
         in_specs=[pl.BlockSpec((rows, share), ahead(steps))] + [whole((chunk, rows))] * 2 + [whole(shape), whole((2,) + shape)],
-        out_specs=[pl.BlockSpec((chunk, piece), behind(steps))] * 2,
+        out_specs=[pl.BlockSpec((chunk, piece), behind(steps)), pl.BlockSpec(memory_space=pl.ANY)],
         out_shape=[struct(row_count, piece)] * 2,
-        scratch_shapes=scratch(rows, shape) + [pltpu.VMEM((chunk, share), f32)],
-        compiler_params=params(),
+        scratch_shapes=scratch(rows, shape) + [pltpu.VMEM((chunk, share), f32)] + mirrored(steps),
+        compiler_params=params(4),
         cost_estimate=cost(6 * size * chunk, 5 * size),
         name="interface",
     )(modes, *to_edge, ratio, edge)
@@ -717,9 +780,9 @@
         scratch_shapes=exchange_scratch(plane_shape, row_devices),
         compiler_params=params(1),
         name="plane_sum",
-    )(kept, across_halves(sent), full_ratio)
-
-    moved = pl.pallas_call(
+    )(kept, received, full_ratio)
+
+    moved, received = pl.pallas_call(
         couple_kernel,
         grid=(2 * plane_steps,),
         in_specs=[
@@ -731,10 +794,10 @@
             whole((2,) + plane_shape),
             in_smem,
         ],
-        out_specs=pl.BlockSpec((thin, piece), behind(plane_steps)),
-        out_shape=struct(row_count, piece),
-        scratch_shapes=scratch(plane_rows, plane_shape),
-        compiler_params=params(),
+        out_specs=[pl.BlockSpec((thin, piece), behind(plane_steps)), pl.BlockSpec(memory_space=pl.ANY)],
+        out_shape=[struct(row_count, piece)] * 2,
+        scratch_shapes=scratch(plane_rows, plane_shape) + mirrored(plane_steps),
+        compiler_params=params(5),
         cost_estimate=cost(6 * size * thin, 2 * size),
         name="couple",
     )(plane, plane, *to_jump, full_ratio, plane_edge, couplings)
@@ -745,7 +808,7 @@
         scratch_shapes=exchange_scratch(shape, row_devices),
         compiler_params=params(2),
         name="plane_join",
-    )(moved, across_halves(moved), ratio, weight, edge)
+    )(moved, received, ratio, weight, edge)
 
     outgoing = [
         pltpu.VMEM((group - 1, row_count * levels, share), f32),

time: 146 us -> 148 us (1.014)
  Pallas kernels: 116 us -> 146 us
  waiting for transfers between devices: 18.3 us -> 0.01 us
  local copies, waits for them, and re-layouts: 7.75 us -> 0 us
  starting transfers between devices: 3.48 us -> 0.45 us
    ppermute x2 -> x0, waiting for transfers between devices: 18.3 us -> none  [across_halves(): lax.ppermute(value, 'lev', [(place, (place + group) % lev_devices) for pl...]
    pallas_call x1, Pallas kernels: 6.75 us -> 20.3 us  [body(): pl.pallas_call(couple_kernel, grid=(2 * plane_steps,), in_specs=[pl.Block...]
    pallas_call x1, Pallas kernels: 9.98 us -> 18 us  [body(): pl.pallas_call(interface_kernel, grid=(2 * steps,), in_specs=[pl.BlockSpe...]
    unnamed x14 -> x0, local copies, waits for them, and re-layouts: 7.73 us -> none
    ppermute x2 -> x0, starting transfers between devices: 3.03 us -> none  [across_halves(): lax.ppermute(value, 'lev', [(place, (place + group) % lev_devices) for pl...]
    pallas_call x1, Pallas kernels: 11 us -> 14 us  [body(): pl.pallas_call(join_kernel, out_shape=[struct(row_count, share), struct(2...]
    pallas_call x1, Pallas kernels: 11.9 us -> 13.6 us  [body(): pl.pallas_call(sum_kernel, out_shape=[struct(row_count, piece), struct(2,...]
  transfers between devices with their start and end apart: 3 -> 1, of which waited for: 2 -> 0; matrix products, arithmetic and copies ran while one was open for 0% -> 0% of each run, Pallas kernels for 10% -> 11%
where the time goes in v4:
time: 148 us; the launch traced here: 147 us
  Pallas kernels  146 us (99%)
    pallas_call x1, Pallas kernels, body(): pl.pallas_call(to_modes_kernel, grid=(steps,), in_specs=[section_spec] *...  24.3 us
    pallas_call x1, Pallas kernels, body(): pl.pallas_call(couple_kernel, grid=(2 * plane_steps,), in_specs=[pl.Block...  20.3 us
    pallas_call x1, Pallas kernels, body(): pl.pallas_call(interface_kernel, grid=(2 * steps,), in_specs=[pl.BlockSpe...  18 us
    pallas_call x1, Pallas kernels, body(): pl.pallas_call(functools.partial(levels_kernel, group=group), in_specs=[i...  15.9 us
    pallas_call x1, Pallas kernels, body(): pl.pallas_call(functools.partial(from_modes_kernel, group=group), grid=(2...  15.4 us
    pallas_call x1, Pallas kernels, body(): pl.pallas_call(join_kernel, out_shape=[struct(row_count, share), struct(2...  14 us
    pallas_call x1, Pallas kernels, body(): pl.pallas_call(sum_kernel, out_shape=[struct(row_count, piece), struct(2,...  13.6 us
    pallas_call x1, Pallas kernels, body(): pl.pallas_call(forward_kernel, grid=(row_count // tile,), in_specs=[field...  13.3 us
  transfers between devices with their start and end apart: 1, of which 0 were waited for; matrix products, arithmetic and copies ran while one was open for 0% of the time, Pallas kernels for 11%

profile of v4, /device:TPU:0, one launch (start us, length us, event | category | flops | bytes accessed | tf_op | source)
XLA Modules:
  0.0 146.6 jit_solution(15509009269907720179)
XLA Ops:
  0.0 13.3 %forward_x.1 = (f32[1024,1024]{1,0:T(8,128)}, f32[1024,1024]{1,0:T(8,128)}) custom-call(f32[256,4,2048]{2,1,0:T(4,128)} %x_ref.1, s32[32,4,32]{2,1,0:T(4,128)} %solid_ref.1, f32[8,256,256]{2,1,0:T(8,128)} %constant.6.clone.table_ref), custom_call_target="tpu_custom_call" | custom-call | flops 3221225472 | bytes 16777216 | tf_op jit(solution)/shard_map/forward_x/pallas_call | solution.py:701
  13.3 0.4 collective-permute-start
  13.7 15.9 %levels.1 = (bf16[256,256]{1,0:T(8,128)(2,1)}, bf16[256,256]{1,0:T(8,128)(2,1)}, bf16[256,256]{1,0:T(8,128)(2,1)}, bf16[256,256]{1,0:T(8,128)(2,1)}, bf16[32,256...) custom-call(f32[17]{0:T(128)} %couplings_ref.3, ...), custom_call_target="tpu_custom_call" | custom-call | tf_op jit(solution)/shard_map/levels/pallas_call | solution.py:720
  29.6 0.0 collective-permute-done.refs_1_
  29.7 24.3 %to_modes.1 = (f32[2048,1024]{1,0:T(8,128)}, f32[2,8,1024]{2,1,0:T(8,128)}) custom-call(f32[1024,1024]{1,0:T(8,128)} %get-tuple-element.30.refs_0_, f32[1024,1024]{1,0:T(8,128)} %collective-permute-done.refs_1_, bf16[256,256]{1,0:T(8,128)(2,1)} %get-tuple-element.32.refs_2_, bf16[256,256]{1,0:T(8,128)(2,1)} %get-tuple-element.33.refs_3_, ...), custom_call_target="tpu_custom_call" | custom-call | flops 3221225472 | bytes 16777216 | tf_op jit(solution)/shard_map/to_modes/pallas_call | solution.py:746
  53.9 18.0 %interface.1 = (f32[256,512]{1,0:T(8,128)}, f32[256,512]{1,0:T(8,128)}) custom-call(f32[2048,1024]{1,0:T(8,128)} %get-tuple-element.35.modes_ref, bf16[32,256]{1,0:T(8,128)(2,1)} %get-tuple-element.36.high_ref, bf16[32,256]{1,0:T(8,128)(2,1)} %get-tuple-element.37.low_ref, f32[8,1024]{1,0:T(8,128)} %get-tuple-element.34.refs_4_.ratio_ref, ...), custom_call_target="tpu_custom_call" | custom-call | flops 402653184 | bytes 10485760 | tf_op jit(solution)/shard_map/interface/pallas_call | solution.py:765
  72.0 13.6 %plane_sum.1 = (f32[256,512]{1,0:T(8,128)}, f32[2,16,512]{2,1,0:T(8,128)}) custom-call(f32[256,512]{1,0:T(8,128)} %get-tuple-element.39.own_ref, f32[256,512]{1,0:T(8,128)} %get-tuple-element.40.other_ref, f32[16,512]{1,0:T(8,128)} %get-tuple-element.41.ratio_ref), custom_call_target="tpu_custom_call" | custom-call | tf_op jit(solution)/shard_map/plane_sum/pallas_call | solution.py:777
  85.6 20.3 %couple.1 = (f32[256,512]{1,0:T(8,128)}, f32[256,512]{1,0:T(8,128)}) custom-call(f32[256,512]{1,0:T(8,128)} %get-tuple-element.42.plane_ref.again_ref, f32[256,512]{1,0:T(8,128)} %get-tuple-element.42.plane_ref.again_ref, bf16[16,256]{1,0:T(8,128)(2,1)} %get-tuple-element.43.high_ref, bf16[16,256]{1,0:T(8,128)(2,1)} %get-tuple-element.44.low_ref, ...), custom_call_target="tpu_custom_call" | custom-call | flops 201326592 | bytes 4194304 | tf_op jit(solution)/shard_map/couple/pallas_call | solution.py:785
  106.0 14.0 %plane_join.1 = (f32[256,1024]{1,0:T(8,128)}, f32[2,8,1024]{2,1,0:T(8,128)}) custom-call(f32[256,512]{1,0:T(8,128)} %get-tuple-element.46.own_ref, f32[256,512]{1,0:T(8,128)} %get-tuple-element.47.other_ref, f32[8,1024]{1,0:T(8,128)} %get-tuple-element.34.refs_4_.ratio_ref, f32[8,1024]{1,0:T(8,128)} %get-tuple-element.48.weight_ref, ...), custom_call_target="tpu_custom_call" | custom-call | tf_op jit(solution)/shard_map/plane_join/pallas_call | solution.py:805
  120.0 15.4 %from_modes.1 = (f32[1024,1024]{1,0:T(8,128)}, f32[1024,1024]{1,0:T(8,128)}) custom-call(f32[2048,1024]{1,0:T(8,128)} %get-tuple-element.35.modes_ref, f32[256,1024]{1,0:T(8,128)} %get-tuple-element.49.plane_ref, f32[8,1024]{1,0:T(8,128)} %get-tuple-element.48.weight_ref, bf16[256,256]{1,0:T(8,128)(2,1)} %get-tuple-element.50.high_ref, ...), custom_call_target="tpu_custom_call" | custom-call | flops 3221225472 | bytes 16777216 | tf_op jit(solution)/shard_map/from_modes/pallas_call | solution.py:818
  135.4 11.2 %backward_x.1 = f32[256,4,2048]{2,1,0:T(4,128)} custom-call(f32[1024,1024]{1,0:T(8,128)} %get-tuple-element.53.refs_0_, f32[1024,1024]{1,0:T(8,128)} %get-tuple-element.54.refs_1_, f32[8,256,256]{2,1,0:T(8,128)} %constant.8.clone.refs_2_), custom_call_target="tpu_custom_call" | custom-call | flops 3221225472 | bytes 16777216 | tf_op jit(solution)/shard_map/backward_x/pallas_call | solution.py:831
Async XLA Ops:
  13.3 16.4 %collective-permute-start = (f32[1024,1024]{1,0:T(8,128)}, f32[1024,1024]{1,0:T(8,128)}, u32[]{:S(2)}, u32[]{:S(2)}) collective-permute-start(f32[1024,1024]{1,0:T(8,128)} %get-tuple-element.31), channel_id=1, source_target_pairs={{0,1},{1,0},{2,3},{3,2},{4,5},{5,4},{6,7},{7,6},{8,9},{9,8},{10,11... | collective-permute-start | bytes 12582920 | tf_op jit(solution)/shard_map/ppermute | solution.py:690

commit v5 on v3

--- a/solution.py
+++ b/solution.py
@@ -14,6 +14,7 @@
 BX = 64
 PARTS = 16
 VMEM_BYTES = 48 * 1024 * 1024
+ALL_VMEM_BYTES = 60 * 1024 * 1024
 
 f32 = jnp.float32
 highest = lax.Precision.HIGHEST
@@ -27,8 +28,9 @@
 
 
 def dot3(left, right):
-    dot = functools.partial(jnp.dot, preferred_element_type=f32)
-    return dot(left[0], right[0]) + (dot(left[0], right[1]) + dot(left[1], right[0]))
+    left = jnp.concatenate([left[0], left[0], left[1]], 1)
+    right = jnp.concatenate([right[0], right[1], right[0]], 0)
+    return jnp.dot(left, right, preferred_element_type=f32)
 
 
 @functools.lru_cache(None)
@@ -137,7 +139,7 @@
             high_ref[block], low_ref[block] = split(table_ref[block])
 
 
-def forward_kernel(x_ref, keep_ref, table_ref, *rest):
+def forward_kernel(x_ref, solid_ref, table_ref, *rest):
     out_refs, (kept, mixed, high_ref, low_ref) = rest[:-4], rest[-4:]
     rows, levels, length = x_ref.shape
     width = length // PARTS
@@ -148,7 +150,9 @@
     first = lax.broadcasted_iota(jnp.int32, shape, 0) * BX
     lane = lax.broadcasted_iota(jnp.int32, shape, 1)
     spread = jnp.where((lane >= first) & (lane < first + BX), 1.0, 0.0).astype(bf16)
-    kept[...] = jnp.dot(keep_ref[...], spread, preferred_element_type=f32)
+    keep = (1 - solid_ref[...]).astype(f32)
+    keep = jnp.concatenate([keep] * pair, 1).reshape(kept.shape[0], length // BX)
+    kept[...] = jnp.dot(keep.astype(bf16), spread, preferred_element_type=f32)
 
     def group(index, unused):
         mask = kept[pl.ds(pl.multiple_of(index * 8, 8), 8), :]
@@ -581,10 +585,10 @@
             lax.fori_loop(0, steps, settle, 0)
 
 
-def params(collective_id=None):
+def params(collective_id=None, room=VMEM_BYTES):
     if collective_id is None:
-        return pltpu.CompilerParams(vmem_limit_bytes=VMEM_BYTES)
-    return pltpu.CompilerParams(vmem_limit_bytes=VMEM_BYTES, collective_id=collective_id, has_side_effects=True)
+        return pltpu.CompilerParams(vmem_limit_bytes=room)
+    return pltpu.CompilerParams(vmem_limit_bytes=room, collective_id=collective_id, has_side_effects=True)
 
 
 def exchange_scratch(shape, row_devices):
@@ -634,8 +638,6 @@
     blocks, eigen_x = x_tables(length)
     forward_table = blocks.astype(np.float32)
     backward_table = np.swapaxes(blocks, 1, 2).astype(np.float32)
-    keep = (1 - solid).astype(bf16)[:, None]
-    keep = jnp.broadcast_to(keep, (keep.shape[0], 8 // levels) + keep.shape[2:]).reshape(-1, length // BX)
     groups = tile // BY * 8
     table = whole(blocks.shape)
     part_spec = pl.BlockSpec((tile * levels, share), lambda i: (i, 0))
@@ -645,14 +647,14 @@
     spectral = pl.pallas_call(
         forward_kernel,
         grid=(row_count // tile,),
-        in_specs=[field_spec, pl.BlockSpec((groups, length // BX), lambda i: (i, 0)), table],
+        in_specs=[field_spec, pl.BlockSpec((tile // BY, levels, length // BX), lambda i: (i, 0, 0)), table],
         out_specs=[part_spec] * group,
         out_shape=[struct(row_count * levels, share)] * group,
         scratch_shapes=[pltpu.VMEM((groups, length), f32), mixed] + halves,
-        compiler_params=params(),
+        compiler_params=params(room=ALL_VMEM_BYTES),
         cost_estimate=cost(6 * size * 2 * width, 8 * size),
         name="forward_x",
-    )(source, keep, forward_table)
+    )(source, solid, forward_table)
     sections = [spectral[0]] + [passed(spectral[shift], shift) for shift in range(1, group)]
 
     chunk = max(BY, 256 // half_levels)
@@ -694,7 +696,7 @@
         out_specs=[pl.BlockSpec((rows, share), lambda i: (i, 0)), whole((2,) + shape)],
         out_shape=[modes_shape, struct(2, *shape)],
         scratch_shapes=[pltpu.VMEM(shape, f32)] + exchange_scratch(shape, row_devices),
-        compiler_params=params(0),
+        compiler_params=params(0, ALL_VMEM_BYTES),
         cost_estimate=cost(6 * size * rows, 8 * size),
         name="to_modes",
     )(*sections, *to_modes, ratio)
@@ -772,7 +774,7 @@
         out_specs=field_spec,
         out_shape=struct(*source.shape),
         scratch_shapes=[mixed] + halves,
-        compiler_params=params(),
+        compiler_params=params(room=ALL_VMEM_BYTES),
         cost_estimate=cost(6 * size * 2 * width, 8 * size),
         name="backward_x",
     )(*returned, backward_table)

time: 146 us -> 145 us (level)
    pallas_call x1, Pallas kernels: 15 us -> 12.8 us  [body(): pl.pallas_call(functools.partial(levels_kernel, group=group), in_specs=[i...]
    unnamed x14 -> x20, local copies, waits for them, and re-layouts: 7.73 us -> 6.68 us
  transfers between devices with their start and end apart: 3 -> 3, of which waited for: 2 -> 2; matrix products, arithmetic and copies ran while one was open for 0% -> 0% of each run, Pallas kernels for 10% -> 9%
where the time goes in v5:
time: 145 us
  Pallas kernels  116 us (80%)
  waiting for transfers between devices  18.2 us (13%)
  local copies, waits for them, and re-layouts  6.68 us (5%)
  starting transfers between devices  3.51 us (2%)
    pallas_call x1, Pallas kernels, body(): pl.pallas_call(to_modes_kernel, grid=(steps,), in_specs=[section_spec] *...  24.3 us
    ppermute x2, waiting for transfers between devices, across_halves(): lax.ppermute(value, 'lev', [(place, (place + group) % lev_devices) for pl...  18.2 us
    pallas_call x1, Pallas kernels, body(): pl.pallas_call(functools.partial(from_modes_kernel, group=group), grid=(2...  14.3 us
    pallas_call x1, Pallas kernels, body(): pl.pallas_call(forward_kernel, grid=(row_count // tile,), in_specs=[field...  13.6 us
    pallas_call x1, Pallas kernels, body(): pl.pallas_call(functools.partial(levels_kernel, group=group), in_specs=[i...  12.8 us
    pallas_call x1, Pallas kernels, body(): pl.pallas_call(sum_kernel, out_shape=[struct(row_count, piece), struct(2,...  12 us
    pallas_call x1, Pallas kernels, body(): pl.pallas_call(backward_kernel, grid=(row_count // tile,), in_specs=[part...  11.3 us
    pallas_call x1, Pallas kernels, body(): pl.pallas_call(join_kernel, out_shape=[struct(row_count, share), struct(2...  10.9 us
  transfers between devices with their start and end apart: 3, of which 2 were waited for; matrix products, arithmetic and copies ran while one was open for 0% of the time, Pallas kernels for 9%

profile of v5, /device:TPU:0, one launch (start us, length us, event | category | flops | bytes accessed | tf_op | source)
XLA Modules:
  0.0 144.8 jit_solution(17227936056260280589)
XLA Ops:
  0.0 0.0 copy-start.5
  0.0 0.0 copy-start.6
  0.0 13.6 %forward_x.1 = (f32[1024,1024]{1,0:T(8,128)}, f32[1024,1024]{1,0:T(8,128)}) custom-call(f32[256,4,2048]{2,1,0:T(4,128)} %x_ref.1, s32[32,4,32]{2,1,0:T(4,128)} %solid_ref.1, f32[8,256,256]{2,1,0:T(8,128)} %constant.6.clone.table_ref), custom_call_target="tpu_custom_call" | custom-call | flops 3221225472 | bytes 16777216 | tf_op jit(solution)/shard_map/forward_x/pallas_call | solution.py:647
  13.6 0.4 collective-permute-start
  14.0 0.0 copy-done.5
  14.0 0.0 copy-done.6
  14.0 12.8 %levels.1 = (bf16[256,256]{1,0:T(8,128)(2,1)S(1)}, bf16[256,256]{1,0:T(8,128)(2,1)S(1)}, bf16[256,256]{1,0:T(8,128)(2,1)S(1)}, bf16[256,256]{1,0:T(8,128)(2,1)S(...) custom-call(f32[17]{0:T(128)S(1)} %copy-done.6, ...), custom_call_target="tpu_custom_call" | custom-call | tf_op jit(solution)/shard_map/levels/pallas_call | solution.py:666
  26.8 0.0 copy-start.3
  26.8 0.6 copy-done.3
  27.4 0.0 copy-start.7
  27.4 0.6 copy-done.7
  28.1 0.0 copy-start.8
  28.1 0.7 copy-done.8
  28.7 0.0 collective-permute-done.refs_1_
  28.7 0.0 copy-start.9
  28.7 2.0 %copy-done.9 = f32[1024,1024]{1,0:T(8,128)} copy-done((f32[1024,1024]{1,0:T(8,128)}, f32[1024,1024]{1,0:T(8,128)S(1)}, u32[]{:S(2)}) %copy-start.9) | copy-done | bytes 4194328
  30.7 0.0 copy-start.4
  30.7 24.3 %to_modes.1 = (f32[2048,1024]{1,0:T(8,128)}, f32[2,8,1024]{2,1,0:T(8,128)}) custom-call(f32[1024,1024]{1,0:T(8,128)} %get-tuple-element.28.refs_0_, f32[1024,1024]{1,0:T(8,128)} %copy-done.9, bf16[256,256]{1,0:T(8,128)(2,1)} %copy-done.7, bf16[256,256]{1,0:T(8,128)(2,1)} %copy-done.8, f32[8,1024]{1,0:T(8,128)} %copy-done.3), custom_call_target="tpu_custom_call" | custom-call | flops 3221225472 | bytes 16777216 | tf_op jit(solution)/shard_map/to_modes/pallas_call | solution.py:692
  55.1 0.0 copy-done.4
  55.1 0.0 copy-start.1
  55.1 0.8 copy-done.1
  55.9 0.0 copy-start.2
  55.9 10.4 %interface.1 = (f32[256,512]{1,0:T(8,128)S(1)}, f32[256,512]{1,0:T(8,128)S(1)}) custom-call(f32[2048,1024]{1,0:T(8,128)} %get-tuple-element.33.modes_ref, bf16[32,256]{1,0:T(8,128)(2,1)S(1)} %get-tuple-element.34.high_ref, bf16[32,256]{1,0:T(8,128)(2,1)S(1)} %get-tuple-element.35.low_ref, f32[8,1024]{1,0:T(8,128)S(1)} %copy-done.4, f32[2,8,1024]{2,1,0:T(8,128)S(1)} %copy-done.1), custom_call_target="tpu_custom_call" | custom-call | flops 402653184 | bytes 10485760 | tf_op jit(solution)/shard_map/interface/pallas_call | solution.py:704
  66.3 1.6 %collective-permute-start.1 = (f32[256,512]{1,0:T(8,128)S(1)}, f32[256,512]{1,0:T(8,128)S(1)}, u32[]{:S(2)}, u32[]{:S(2)}) collective-permute-start(f32[256,512]{1,0:T(8,128)S(1)} %get-tuple-element.38), channel_id=1, source_target_pairs={{0,2},{1,3},{2,0},{3,1},{4,6},{5,7},{6,4},{7,5},{8,10},{9,11},{10,... | collective-permute-start | bytes 1572872 | tf_op jit(solution)/shard_map/ppermute | solution.py:636
  67.8 9.0 %collective-permute-done.1.other_ref = f32[256,512]{1,0:T(8,128)S(1)} collective-permute-done((f32[256,512]{1,0:T(8,128)S(1)}, f32[256,512]{1,0:T(8,128)S(1)}, u32[]{:S(2)}, u32[]{:S(2)}) %collective-permute-start.1) | collective-permute-done | bytes 524320 | tf_op jit(solution)/shard_map/ppermute | solution.py:636
  76.9 12.0 %plane_sum.1 = (f32[256,512]{1,0:T(8,128)S(1)}, f32[2,16,512]{2,1,0:T(8,128)S(1)}) custom-call(f32[256,512]{1,0:T(8,128)S(1)} %get-tuple-element.37.own_ref, f32[256,512]{1,0:T(8,128)S(1)} %collective-permute-done.1.other_ref, f32[16,512]{1,0:T(8,128)S(1)} %get-tuple-element.39.ratio_ref), custom_call_target="tpu_custom_call" | custom-call | tf_op jit(solution)/shard_map/plane_sum/pallas_call | solution.py:716
  88.9 6.8 %couple.1.own_ref = f32[256,512]{1,0:T(8,128)S(1)} custom-call(f32[256,512]{1,0:T(8,128)S(1)} %get-tuple-element.40.plane_ref.again_ref, f32[256,512]{1,0:T(8,128)S(1)} %get-tuple-element.40.plane_ref.again_ref, bf16[16,256]{1,0:T(8,128)(2,1)S(1)} %get-tuple-element.41.high_ref, bf16[16,256]{1,0:T(8,128)(2,1)S(1)} %get-tuple-element.42.low_ref, ...), custom_call_target="tpu_custom_call" | custom-call | flops 201326592 | bytes 4194304 | tf_op jit(solution)/shard_map/couple/pallas_call | solution.py:724
  95.6 1.5 %collective-permute-start.2 = (f32[256,512]{1,0:T(8,128)S(1)}, f32[256,512]{1,0:T(8,128)S(1)}, u32[]{:S(2)}, u32[]{:S(2)}) collective-permute-start(f32[256,512]{1,0:T(8,128)S(1)} %couple.1.own_ref), channel_id=1, source_target_pairs={{0,2},{1,3},{2,0},{3,1},{4,6},{5,7},{6,4},{7,5},{8,10},{9,11},{10,... | collective-permute-start | bytes 1572872 | tf_op jit(solution)/shard_map/ppermute | solution.py:636
  97.1 9.2 %collective-permute-done.2.other_ref = f32[256,512]{1,0:T(8,128)S(1)} collective-permute-done((f32[256,512]{1,0:T(8,128)S(1)}, f32[256,512]{1,0:T(8,128)S(1)}, u32[]{:S(2)}, u32[]{:S(2)}) %collective-permute-start.2) | collective-permute-done | bytes 524320 | tf_op jit(solution)/shard_map/ppermute | solution.py:636
  106.3 0.0 copy-done.2
  106.3 10.9 %plane_join.1 = (f32[256,1024]{1,0:T(8,128)S(1)}, f32[2,8,1024]{2,1,0:T(8,128)S(1)}) custom-call(f32[256,512]{1,0:T(8,128)S(1)} %couple.1.own_ref, f32[256,512]{1,0:T(8,128)S(1)} %collective-permute-done.2.other_ref, f32[8,1024]{1,0:T(8,128)S(1)} %copy-done.4, f32[8,1024]{1,0:T(8,128)S(1)} %get-tuple-element.44.weight_ref, f32[2,8,1024]{2,1,0:T(8,128)S(1)} %copy-done.2), custom_call_target="tpu_custom_call" | custom-call | tf_op jit(solution)/shard_map/plane_join/pallas_call | solution.py:744
  117.2 14.3 %from_modes.1 = (f32[1024,1024]{1,0:T(8,128)S(1)}, f32[1024,1024]{1,0:T(8,128)}) custom-call(f32[2048,1024]{1,0:T(8,128)} %get-tuple-element.33.modes_ref, f32[256,1024]{1,0:T(8,128)S(1)} %get-tuple-element.45.plane_ref, f32[8,1024]{1,0:T(8,128)S(1)} %get-tuple-element.44.weight_ref, bf16[256,256]{1,0:T(8,128)(2,1)S(1)} %get-tuple-element.46.high_ref, ...), custom_call_target="tpu_custom_call" | custom-call | flops 3221225472 | bytes 16777216 | tf_op jit(solution)/shard_map/from_modes/pallas_call | solution.py:757
  131.6 0.0 copy-start
  131.6 1.9 %copy-done = f32[1024,1024]{1,0:T(8,128)} copy-done((f32[1024,1024]{1,0:T(8,128)}, f32[1024,1024]{1,0:T(8,128)S(1)}, u32[]{:S(2)}) %copy-start) | copy-done | bytes 4194328
  133.5 11.3 %backward_x.1 = f32[256,4,2048]{2,1,0:T(4,128)} custom-call(f32[1024,1024]{1,0:T(8,128)} %copy-done, f32[1024,1024]{1,0:T(8,128)} %get-tuple-element.50.refs_1_, f32[8,256,256]{2,1,0:T(8,128)} %constant.8.clone.refs_2_), custom_call_target="tpu_custom_call" | custom-call | flops 3221225472 | bytes 16777216 | tf_op jit(solution)/shard_map/backward_x/pallas_call | solution.py:770
Async XLA Ops:
  0.0 14.0 %copy-start.5 = (f32[1,2048]{1,0:T(1,128)S(1)}, f32[1,2048]{1,0:T(1,128)}, u32[]{:S(2)}) copy-start(f32[1,2048]{1,0:T(1,128)} %constant.7.clone.eigen_ref) | copy-start | bytes 24580
  0.0 14.0 %copy-start.6 = (f32[17]{0:T(128)S(1)}, f32[17]{0:T(128)}, u32[]{:S(2)}) copy-start(f32[17]{0:T(128)} %couplings_ref.3) | copy-start | bytes 208
  13.6 15.1 %collective-permute-start = (f32[1024,1024]{1,0:T(8,128)}, f32[1024,1024]{1,0:T(8,128)S(1)}, u32[]{:S(2)}, u32[]{:S(2)}) collective-permute-start(f32[1024,1024]{1,0:T(8,128)} %get-tuple-element.29), channel_id=1, source_target_pairs={{0,1},{1,0},{2,3},{3,2},{4,5},{5,4},{6,7},{7,6},{8,9},{9,8},{10,11... | collective-permute-start | bytes 12582920 | tf_op jit(solution)/shard_map/ppermute | solution.py:633
  26.8 0.6 copy-start.3
  27.4 0.7 copy-start.7
  28.1 0.7 copy-start.8
  28.7 2.0 %copy-start.9 = (f32[1024,1024]{1,0:T(8,128)}, f32[1024,1024]{1,0:T(8,128)S(1)}, u32[]{:S(2)}) copy-start(f32[1024,1024]{1,0:T(8,128)S(1)} %collective-permute-done.refs_1_) | copy-start | bytes 12582916
  30.7 24.4 %copy-start.4 = (f32[8,1024]{1,0:T(8,128)S(1)}, f32[8,1024]{1,0:T(8,128)}, u32[]{:S(2)}) copy-start(f32[8,1024]{1,0:T(8,128)} %copy-done.3) | copy-start | bytes 98308
  55.1 0.8 copy-start.1
  55.9 50.4 %copy-start.2 = (f32[2,8,1024]{2,1,0:T(8,128)S(1)}, f32[2,8,1024]{2,1,0:T(8,128)}, u32[]{:S(2)}) copy-start(f32[2,8,1024]{2,1,0:T(8,128)} %get-tuple-element.36.edge_ref.known_ref) | copy-start | bytes 196612
  66.3 10.6 %collective-permute-start.1 = (f32[256,512]{1,0:T(8,128)S(1)}, f32[256,512]{1,0:T(8,128)S(1)}, u32[]{:S(2)}, u32[]{:S(2)}) collective-permute-start(f32[256,512]{1,0:T(8,128)S(1)} %get-tuple-element.38), channel_id=1, source_target_pairs={{0,2},{1,3},{2,0},{3,1},{4,6},{5,7},{6,4},{7,5},{8,10},{9,11},{10,... | collective-permute-start | bytes 1572872 | tf_op jit(solution)/shard_map/ppermute | solution.py:636
  95.6 10.7 %collective-permute-start.2 = (f32[256,512]{1,0:T(8,128)S(1)}, f32[256,512]{1,0:T(8,128)S(1)}, u32[]{:S(2)}, u32[]{:S(2)}) collective-permute-start(f32[256,512]{1,0:T(8,128)S(1)} %couple.1.own_ref), channel_id=1, source_target_pairs={{0,2},{1,3},{2,0},{3,1},{4,6},{5,7},{6,4},{7,5},{8,10},{9,11},{10,... | collective-permute-start | bytes 1572872 | tf_op jit(solution)/shard_map/ppermute | solution.py:636
  131.6 2.0 %copy-start = (f32[1024,1024]{1,0:T(8,128)}, f32[1024,1024]{1,0:T(8,128)S(1)}, u32[]{:S(2)}) copy-start(f32[1024,1024]{1,0:T(8,128)S(1)} %get-tuple-element.49.refs_0_) | copy-start | bytes 12582916

commit v6 on v5

--- a/solution.py
+++ b/solution.py
@@ -28,9 +28,8 @@
 
 
 def dot3(left, right):
-    left = jnp.concatenate([left[0], left[0], left[1]], 1)
-    right = jnp.concatenate([right[0], right[1], right[0]], 0)
-    return jnp.dot(left, right, preferred_element_type=f32)
+    dot = functools.partial(jnp.dot, preferred_element_type=f32)
+    return dot(left[0], right[0]) + (dot(left[0], right[1]) + dot(left[1], right[0]))
 
 
 @functools.lru_cache(None)
@@ -251,7 +250,7 @@
     all_modes, piece = full_ref.shape
     lanes = 128
     rows = to_high.shape[0]
-    chunk = edge_high.shape[0]
+    chunk = rows // modes
     levels = modes // group
     top = -(-(all_modes + 1) // 8) * 8
     low = -(-all_modes // 8) * 8
@@ -294,8 +293,11 @@
     to_high[...], to_low[...] = split(spread.T)
 
     edge = jnp.where(half == 0, vectors[modes - 1 : modes], vectors[0:1])
+    wide, wide_rows = edge_high.shape
+    column = iota((lanes, wide_rows), 1)
+    place = spot(iota((lanes, wide_rows), 0) == all_modes + lax.rem(column, modes))
     line = exact(jnp.broadcast_to(edge, (8, lanes)), place)[0:1]
-    at, to = iota((chunk, rows), 0), iota((chunk, rows), 1)
+    at, to = iota((wide, wide_rows), 0), iota((wide, wide_rows), 1)
     edge_high[...], edge_low[...] = split(jnp.where(at == to // modes, line, 0.0))
     jump = couplings_ref[modes] * (vectors[modes - 1 : modes] + vectors[modes : modes + 1])
     thin, plane_rows = jump_high.shape
@@ -658,23 +660,26 @@
     sections = [spectral[0]] + [passed(spectral[shift], shift) for shift in range(1, group)]
 
     chunk = max(BY, 256 // half_levels)
-    thin = max(BY, 256 // all_levels)
+    thin = min(row_count, max(BY, 512 // all_levels))
+    wide = min(row_count, max(BY, 512 // half_levels))
     rows = chunk * half_levels
     plane_rows = thin * all_levels
+    wide_rows = wide * half_levels
     in_smem = pl.BlockSpec(memory_space=pltpu.SMEM)
-    built = [(rows, rows)] * 4 + [(chunk, rows)] * 2 + [(thin, plane_rows)] * 2
+    built = [(rows, rows)] * 4 + [(wide, wide_rows)] * 2 + [(thin, plane_rows)] * 2
     *matrices, ratio, full_ratio, weight = pl.pallas_call(
         functools.partial(levels_kernel, group=group),
         in_specs=[in_smem, pl.BlockSpec(memory_space=pltpu.VMEM)],
         out_shape=[jax.ShapeDtypeStruct(each, bf16) for each in built]
         + [struct(half_levels, share), struct(all_levels, piece), struct(half_levels, share)],
-        compiler_params=params(),
+        compiler_params=params(room=ALL_VMEM_BYTES),
         name="levels",
     )(couplings, eigen_x[None, :])
     to_modes, from_modes, to_edge, to_jump = (matrices[2 * index : 2 * index + 2] for index in range(4))
 
     steps = row_count // chunk
     plane_steps = row_count // thin
+    wide_steps = row_count // wide
     shape = (half_levels, share)
     plane_shape = (all_levels, piece)
     modes_shape = struct(row_count * half_levels, share)
@@ -703,11 +708,11 @@
 
     kept, sent = pl.pallas_call(
         interface_kernel,
-        grid=(2 * steps,),
-        in_specs=[pl.BlockSpec((rows, share), ahead(steps))] + [whole((chunk, rows))] * 2 + [whole(shape), whole((2,) + shape)],
-        out_specs=[pl.BlockSpec((chunk, piece), behind(steps))] * 2,
+        grid=(2 * wide_steps,),
+        in_specs=[pl.BlockSpec((wide_rows, share), ahead(wide_steps))] + [whole((wide, wide_rows))] * 2 + [whole(shape), whole((2,) + shape)],
+        out_specs=[pl.BlockSpec((wide, piece), behind(wide_steps))] * 2,
         out_shape=[struct(row_count, piece)] * 2,
-        scratch_shapes=scratch(rows, shape) + [pltpu.VMEM((chunk, share), f32)],
+        scratch_shapes=scratch(wide_rows, shape) + [pltpu.VMEM((wide, share), f32)],
         compiler_params=params(),
         cost_estimate=cost(6 * size * chunk, 5 * size),
         name="interface",
@@ -763,7 +768,7 @@
         out_specs=[pl.BlockSpec((chunk * levels, share), behind(steps))] + [pl.BlockSpec(memory_space=pl.ANY)] * (group - 1),
         out_shape=[struct(row_count * levels, share)] * group,
         scratch_shapes=scratch(rows, shape) + (outgoing if group > 1 else []),
-        compiler_params=params(3 if group > 1 else None),
+        compiler_params=params(3 if group > 1 else None, ALL_VMEM_BYTES),
         cost_estimate=cost(6 * size * rows, 8 * size),
         name="from_modes",
     )(modes, joined, weight, *from_modes, ratio, edge)

time: 145 us -> 142 us (0.979)
  local copies, waits for them, and re-layouts: 6.68 us -> 2.45 us
  Pallas kernels: 116 us -> 118 us
    unnamed x20 -> x24, local copies, waits for them, and re-layouts: 6.68 us -> 2.45 us
    pallas_call x1, Pallas kernels: 12.8 us -> 16.1 us  [body(): pl.pallas_call(functools.partial(levels_kernel, group=group), in_specs=[i...]
    pallas_call x1, Pallas kernels: 10.4 us -> 8.45 us  [body(): pl.pallas_call(interface_kernel, grid=(2 * wide_steps,), in_specs=[pl.Blo...]
  transfers between devices with their start and end apart: 3 -> 3, of which waited for: 2 -> 2; matrix products, arithmetic and copies ran while one was open for 0% -> 0% of each run, Pallas kernels for 9% -> 11%
where the time goes in v6:
time: 142 us
  Pallas kernels  118 us (83%)
  waiting for transfers between devices  18.3 us (13%)
  starting transfers between devices  3.56 us (3%)
  local copies, waits for them, and re-layouts  2.45 us (2%)
    pallas_call x1, Pallas kernels, body(): pl.pallas_call(to_modes_kernel, grid=(steps,), in_specs=[section_spec] *...  24.5 us
    ppermute x2, waiting for transfers between devices, across_halves(): lax.ppermute(value, 'lev', [(place, (place + group) % lev_devices) for pl...  18.3 us
    pallas_call x1, Pallas kernels, body(): pl.pallas_call(functools.partial(levels_kernel, group=group), in_specs=[i...  16.1 us
    pallas_call x1, Pallas kernels, body(): pl.pallas_call(functools.partial(from_modes_kernel, group=group), grid=(2...  15.4 us
    pallas_call x1, Pallas kernels, body(): pl.pallas_call(forward_kernel, grid=(row_count // tile,), in_specs=[field...  13.3 us
    pallas_call x1, Pallas kernels, body(): pl.pallas_call(sum_kernel, out_shape=[struct(row_count, piece), struct(2,...  11.9 us
    pallas_call x1, Pallas kernels, body(): pl.pallas_call(join_kernel, out_shape=[struct(row_count, share), struct(2...  11.2 us
    pallas_call x1, Pallas kernels, body(): pl.pallas_call(backward_kernel, grid=(row_count // tile,), in_specs=[part...  11.1 us
  transfers between devices with their start and end apart: 3, of which 2 were waited for; matrix products, arithmetic and copies ran while one was open for 0% of the time, Pallas kernels for 11%

profile of v6, /device:TPU:0, one launch (start us, length us, event | category | flops | bytes accessed | tf_op | source)
XLA Modules:
  0.0 142.2 jit_solution(1784340877079108625)
XLA Ops:
  0.0 13.3 %forward_x.1 = (f32[1024,1024]{1,0:T(8,128)}, f32[1024,1024]{1,0:T(8,128)}) custom-call(f32[256,4,2048]{2,1,0:T(4,128)} %x_ref.1, s32[32,4,32]{2,1,0:T(4,128)} %solid_ref.1, f32[8,256,256]{2,1,0:T(8,128)} %constant.6.clone.table_ref), custom_call_target="tpu_custom_call" | custom-call | flops 3221225472 | bytes 16777216 | tf_op jit(solution)/shard_map/forward_x/pallas_call | solution.py:649
  13.3 0.4 collective-permute-start
  13.7 16.1 %levels.1 = (bf16[256,256]{1,0:T(8,128)(2,1)}, bf16[256,256]{1,0:T(8,128)(2,1)}, bf16[256,256]{1,0:T(8,128)(2,1)}, bf16[256,256]{1,0:T(8,128)(2,1)}, bf16[64,512...) custom-call(f32[17]{0:T(128)} %couplings_ref.3, ...), custom_call_target="tpu_custom_call" | custom-call | tf_op jit(solution)/shard_map/levels/pallas_call | solution.py:670
  29.8 0.0 collective-permute-done.refs_1_
  29.8 0.0 copy-start.2
  29.8 0.0 copy-start.4
  29.8 0.0 copy-start.5
  29.8 24.5 %to_modes.1 = (f32[2048,1024]{1,0:T(8,128)}, f32[2,8,1024]{2,1,0:T(8,128)}) custom-call(f32[1024,1024]{1,0:T(8,128)} %get-tuple-element.28.refs_0_, f32[1024,1024]{1,0:T(8,128)} %collective-permute-done.refs_1_, bf16[256,256]{1,0:T(8,128)(2,1)} %get-tuple-element.30.refs_2_, bf16[256,256]{1,0:T(8,128)(2,1)} %get-tuple-element.31.refs_3_, ...), custom_call_target="tpu_custom_call" | custom-call | flops 3221225472 | bytes 16777216 | tf_op jit(solution)/shard_map/to_modes/pallas_call | solution.py:697
  54.3 0.0 copy-done.2
  54.3 0.0 copy-done.4
  54.3 0.0 copy-done.5
  54.3 0.0 copy-start
  54.4 0.8 copy-done
  55.2 0.0 copy-start.3
  55.2 0.0 copy-start.7
  55.2 0.0 copy-start.8
  55.2 0.0 copy-start.9
  55.2 0.0 copy-start.1
  55.2 0.0 copy-start.6
  55.2 8.4 %interface.1 = (f32[256,512]{1,0:T(8,128)S(1)}, f32[256,512]{1,0:T(8,128)S(1)}) custom-call(f32[2048,1024]{1,0:T(8,128)} %get-tuple-element.33.modes_ref, bf16[64,512]{1,0:T(8,128)(2,1)S(1)} %copy-done.4, bf16[64,512]{1,0:T(8,128)(2,1)S(1)} %copy-done.5, f32[8,1024]{1,0:T(8,128)S(1)} %copy-done.2, f32[2,8,1024]{2,1,0:T(8,128)S(1)} %copy-done), custom_call_target="tpu_custom_call" | custom-call | flops 402653184 | bytes 10485760 | tf_op jit(solution)/shard_map/interface/pallas_call | solution.py:709
  63.7 1.6 %collective-permute-start.1 = (f32[256,512]{1,0:T(8,128)S(1)}, f32[256,512]{1,0:T(8,128)S(1)}, u32[]{:S(2)}, u32[]{:S(2)}) collective-permute-start(f32[256,512]{1,0:T(8,128)S(1)} %get-tuple-element.38), channel_id=1, source_target_pairs={{0,2},{1,3},{2,0},{3,1},{4,6},{5,7},{6,4},{7,5},{8,10},{9,11},{10,... | collective-permute-start | bytes 1572872 | tf_op jit(solution)/shard_map/ppermute | solution.py:638
  65.3 9.1 %collective-permute-done.1.other_ref = f32[256,512]{1,0:T(8,128)S(1)} collective-permute-done((f32[256,512]{1,0:T(8,128)S(1)}, f32[256,512]{1,0:T(8,128)S(1)}, u32[]{:S(2)}, u32[]{:S(2)}) %collective-permute-start.1) | collective-permute-done | bytes 524320 | tf_op jit(solution)/shard_map/ppermute | solution.py:638
  74.3 0.0 copy-done.3
  74.3 11.9 %plane_sum.1 = (f32[256,512]{1,0:T(8,128)S(1)}, f32[2,16,512]{2,1,0:T(8,128)S(1)}) custom-call(f32[256,512]{1,0:T(8,128)S(1)} %get-tuple-element.37.own_ref, f32[256,512]{1,0:T(8,128)S(1)} %collective-permute-done.1.other_ref, f32[16,512]{1,0:T(8,128)S(1)} %copy-done.3), custom_call_target="tpu_custom_call" | custom-call | tf_op jit(solution)/shard_map/plane_sum/pallas_call | solution.py:721
  86.2 0.0 copy-done.7
  86.3 0.0 copy-done.8
  86.3 0.0 copy-done.9
  86.3 5.8 %couple.1.own_ref = f32[256,512]{1,0:T(8,128)S(1)} custom-call(f32[256,512]{1,0:T(8,128)S(1)} %get-tuple-element.40.plane_ref.again_ref, f32[256,512]{1,0:T(8,128)S(1)} %get-tuple-element.40.plane_ref.again_ref, bf16[32,512]{1,0:T(8,128)(2,1)S(1)} %copy-done.7, bf16[32,512]{1,0:T(8,128)(2,1)S(1)} %copy-done.8, f32[16,512]{1,0:T(8,128)S(1)} %copy-done.3, ...), custom_call_target="tpu_custom_call" | custom-call | flops 402653184 | bytes 4194304 | tf_op jit(solution)/shard_map/couple/pallas_call | solution.py:729
  92.1 1.5 %collective-permute-start.2 = (f32[256,512]{1,0:T(8,128)S(1)}, f32[256,512]{1,0:T(8,128)S(1)}, u32[]{:S(2)}, u32[]{:S(2)}) collective-permute-start(f32[256,512]{1,0:T(8,128)S(1)} %couple.1.own_ref), channel_id=1, source_target_pairs={{0,2},{1,3},{2,0},{3,1},{4,6},{5,7},{6,4},{7,5},{8,10},{9,11},{10,... | collective-permute-start | bytes 1572872 | tf_op jit(solution)/shard_map/ppermute | solution.py:638
  93.6 9.2 %collective-permute-done.2.other_ref = f32[256,512]{1,0:T(8,128)S(1)} collective-permute-done((f32[256,512]{1,0:T(8,128)S(1)}, f32[256,512]{1,0:T(8,128)S(1)}, u32[]{:S(2)}, u32[]{:S(2)}) %collective-permute-start.2) | collective-permute-done | bytes 524320 | tf_op jit(solution)/shard_map/ppermute | solution.py:638
  102.8 0.0 copy-done.1
  102.8 0.0 copy-done.6
  102.8 11.2 %plane_join.1 = (f32[256,1024]{1,0:T(8,128)S(1)}, f32[2,8,1024]{2,1,0:T(8,128)S(1)}) custom-call(f32[256,512]{1,0:T(8,128)S(1)} %couple.1.own_ref, f32[256,512]{1,0:T(8,128)S(1)} %collective-permute-done.2.other_ref, f32[8,1024]{1,0:T(8,128)S(1)} %copy-done.2, f32[8,1024]{1,0:T(8,128)S(1)} %copy-done.6, f32[2,8,1024]{2,1,0:T(8,128)S(1)} %copy-done.1), custom_call_target="tpu_custom_call" | custom-call | tf_op jit(solution)/shard_map/plane_join/pallas_call | solution.py:749
  114.0 0.0 copy-start.10
  114.0 1.0 copy-done.10
  115.0 0.0 copy-start.11
  115.0 0.6 copy-done.11
  115.6 15.4 %from_modes.1 = (f32[1024,1024]{1,0:T(8,128)}, f32[1024,1024]{1,0:T(8,128)}) custom-call(f32[2048,1024]{1,0:T(8,128)} %get-tuple-element.33.modes_ref, f32[256,1024]{1,0:T(8,128)} %copy-done.10, f32[8,1024]{1,0:T(8,128)} %get-tuple-element.44.weight_ref, bf16[256,256]{1,0:T(8,128)(2,1)} %get-tuple-element.46.high_ref, ...), custom_call_target="tpu_custom_call" | custom-call | flops 3221225472 | bytes 16777216 | tf_op jit(solution)/shard_map/from_modes/pallas_call | solution.py:762
  131.0 11.1 %backward_x.1 = f32[256,4,2048]{2,1,0:T(4,128)} custom-call(f32[1024,1024]{1,0:T(8,128)} %get-tuple-element.49.refs_0_, f32[1024,1024]{1,0:T(8,128)} %get-tuple-element.50.refs_1_, f32[8,256,256]{2,1,0:T(8,128)} %constant.8.clone.refs_2_), custom_call_target="tpu_custom_call" | custom-call | flops 3221225472 | bytes 16777216 | tf_op jit(solution)/shard_map/backward_x/pallas_call | solution.py:775
Async XLA Ops:
  13.3 16.5 %collective-permute-start = (f32[1024,1024]{1,0:T(8,128)}, f32[1024,1024]{1,0:T(8,128)}, u32[]{:S(2)}, u32[]{:S(2)}) collective-permute-start(f32[1024,1024]{1,0:T(8,128)} %get-tuple-element.29), channel_id=1, source_target_pairs={{0,1},{1,0},{2,3},{3,2},{4,5},{5,4},{6,7},{7,6},{8,9},{9,8},{10,11... | collective-permute-start | bytes 12582920 | tf_op jit(solution)/shard_map/ppermute | solution.py:635
  29.8 24.6 %copy-start.2 = (f32[8,1024]{1,0:T(8,128)S(1)}, f32[8,1024]{1,0:T(8,128)}, u32[]{:S(2)}) copy-start(f32[8,1024]{1,0:T(8,128)} %get-tuple-element.32.refs_4_.ratio_ref) | copy-start | bytes 98308
  29.8 24.6 %copy-start.4 = (bf16[64,512]{1,0:T(8,128)(2,1)S(1)}, bf16[64,512]{1,0:T(8,128)(2,1)}, u32[]{:S(2)}) copy-start(bf16[64,512]{1,0:T(8,128)(2,1)} %get-tuple-element.34.high_ref) | copy-start | bytes 196612
  29.8 24.6 %copy-start.5 = (bf16[64,512]{1,0:T(8,128)(2,1)S(1)}, bf16[64,512]{1,0:T(8,128)(2,1)}, u32[]{:S(2)}) copy-start(bf16[64,512]{1,0:T(8,128)(2,1)} %get-tuple-element.35.low_ref) | copy-start | bytes 196612
  54.3 0.8 copy-start
  55.2 19.2 %copy-start.3 = (f32[16,512]{1,0:T(8,128)S(1)}, f32[16,512]{1,0:T(8,128)}, u32[]{:S(2)}) copy-start(f32[16,512]{1,0:T(8,128)} %get-tuple-element.39.ratio_ref) | copy-start | bytes 98308
  55.2 31.1 %copy-start.7 = (bf16[32,512]{1,0:T(8,128)(2,1)S(1)}, bf16[32,512]{1,0:T(8,128)(2,1)}, u32[]{:S(2)}) copy-start(bf16[32,512]{1,0:T(8,128)(2,1)} %get-tuple-element.41.high_ref) | copy-start | bytes 98308
  55.2 31.1 %copy-start.8 = (bf16[32,512]{1,0:T(8,128)(2,1)S(1)}, bf16[32,512]{1,0:T(8,128)(2,1)}, u32[]{:S(2)}) copy-start(bf16[32,512]{1,0:T(8,128)(2,1)} %get-tuple-element.42.low_ref) | copy-start | bytes 98308
  55.2 31.1 %copy-start.9 = (f32[17]{0:T(128)S(1)}, f32[17]{0:T(128)}, u32[]{:S(2)}) copy-start(f32[17]{0:T(128)} %couplings_ref.3) | copy-start | bytes 208
  55.2 47.7 %copy-start.1 = (f32[2,8,1024]{2,1,0:T(8,128)S(1)}, f32[2,8,1024]{2,1,0:T(8,128)}, u32[]{:S(2)}) copy-start(f32[2,8,1024]{2,1,0:T(8,128)} %get-tuple-element.36.edge_ref.known_ref) | copy-start | bytes 196612
  55.2 47.6 %copy-start.6 = (f32[8,1024]{1,0:T(8,128)S(1)}, f32[8,1024]{1,0:T(8,128)}, u32[]{:S(2)}) copy-start(f32[8,1024]{1,0:T(8,128)} %get-tuple-element.44.weight_ref) | copy-start | bytes 98308
  63.7 10.7 %collective-permute-start.1 = (f32[256,512]{1,0:T(8,128)S(1)}, f32[256,512]{1,0:T(8,128)S(1)}, u32[]{:S(2)}, u32[]{:S(2)}) collective-permute-start(f32[256,512]{1,0:T(8,128)S(1)} %get-tuple-element.38), channel_id=1, source_target_pairs={{0,2},{1,3},{2,0},{3,1},{4,6},{5,7},{6,4},{7,5},{8,10},{9,11},{10,... | collective-permute-start | bytes 1572872 | tf_op jit(solution)/shard_map/ppermute | solution.py:638
  92.1 10.8 %collective-permute-start.2 = (f32[256,512]{1,0:T(8,128)S(1)}, f32[256,512]{1,0:T(8,128)S(1)}, u32[]{:S(2)}, u32[]{:S(2)}) collective-permute-start(f32[256,512]{1,0:T(8,128)S(1)} %couple.1.own_ref), channel_id=1, source_target_pairs={{0,2},{1,3},{2,0},{3,1},{4,6},{5,7},{6,4},{7,5},{8,10},{9,11},{10,... | collective-permute-start | bytes 1572872 | tf_op jit(solution)/shard_map/ppermute | solution.py:638
  114.0 1.0 copy-start.10
  115.0 0.6 copy-start.11

commit v7 on v6

--- a/solution.py
+++ b/solution.py
@@ -402,8 +402,11 @@
         ends[...] = jnp.zeros(ends.shape, f32)
         scale_ref[...] = jnp.ones(scale_ref.shape, f32)
 
-    values = jnp.concatenate([x_ref[...] for x_ref in x_refs], 0)
-    modes_ref[...] = dot3((high_ref[...], low_ref[...]), split(values))
+    block = high_ref.shape[0]
+    each = block // len(x_refs)
+    for part in range(modes_ref.shape[0] // block):
+        values = jnp.concatenate([x_ref[part * each : (part + 1) * each] for x_ref in x_refs], 0)
+        modes_ref[part * block : (part + 1) * block] = dot3((high_ref[...], low_ref[...]), split(values))
     ratio = ratio_ref[...]
     first, last, scale = ends[0], ends[1], scale_ref[...]
     rows = modes_ref.shape[0] // modes
@@ -683,7 +686,6 @@
     shape = (half_levels, share)
     plane_shape = (all_levels, piece)
     modes_shape = struct(row_count * half_levels, share)
-    section_spec = pl.BlockSpec((chunk * levels, share), lambda i: (i, 0))
 
     def ahead(count):
         return lambda i: (jnp.minimum(i, count - 1), 0)
@@ -694,11 +696,12 @@
     def scratch(rows, shape):
         return [pltpu.VMEM((row_count * shape[0], shape[1]), f32), pltpu.VMEM((rows, shape[1]), f32), pltpu.VMEM(shape, f32)]
 
+    double = 2 if steps % 2 == 0 else 1
     modes, edge = pl.pallas_call(
         to_modes_kernel,
-        grid=(steps,),
-        in_specs=[section_spec] * group + [whole((rows, rows))] * 2 + [whole(shape)],
-        out_specs=[pl.BlockSpec((rows, share), lambda i: (i, 0)), whole((2,) + shape)],
+        grid=(steps // double,),
+        in_specs=[pl.BlockSpec((double * chunk * levels, share), lambda i: (i, 0))] * group + [whole((rows, rows))] * 2 + [whole(shape)],
+        out_specs=[pl.BlockSpec((double * rows, share), lambda i: (i, 0)), whole((2,) + shape)],
         out_shape=[modes_shape, struct(2, *shape)],
         scratch_shapes=[pltpu.VMEM(shape, f32)] + exchange_scratch(shape, row_devices),
         compiler_params=params(0, ALL_VMEM_BYTES),

time: 142 us -> 140 us (0.986); the launches traced: 142 us -> 139 us
  Pallas kernels: 118 us -> 114 us
    pallas_call x1, Pallas kernels: 16.1 us -> 13.8 us  [body(): pl.pallas_call(functools.partial(levels_kernel, group=group), in_specs=[i...]
  transfers between devices with their start and end apart: 3 -> 3, of which waited for: 2 -> 2; matrix products, arithmetic and copies ran while one was open for 0% -> 0% of each run, Pallas kernels for 11% -> 10%
where the time goes in v7:
time: 140 us; the launch traced here: 139 us
  Pallas kernels  114 us (81%)
  waiting for transfers between devices  18.4 us (13%)
  starting transfers between devices  3.49 us (2%)
  local copies, waits for them, and re-layouts  2.45 us (2%)
    pallas_call x1, Pallas kernels, body(): pl.pallas_call(to_modes_kernel, grid=(steps // double,), in_specs=[pl.Blo...  23.4 us
    ppermute x2, waiting for transfers between devices, across_halves(): lax.ppermute(value, 'lev', [(place, (place + group) % lev_devices) for pl...  18.4 us
    pallas_call x1, Pallas kernels, body(): pl.pallas_call(functools.partial(from_modes_kernel, group=group), grid=(2...  15.4 us
    pallas_call x1, Pallas kernels, body(): pl.pallas_call(functools.partial(levels_kernel, group=group), in_specs=[i...  13.8 us
    pallas_call x1, Pallas kernels, body(): pl.pallas_call(forward_kernel, grid=(row_count // tile,), in_specs=[field...  13.3 us
    pallas_call x1, Pallas kernels, body(): pl.pallas_call(sum_kernel, out_shape=[struct(row_count, piece), struct(2,...  12 us
    pallas_call x1, Pallas kernels, body(): pl.pallas_call(backward_kernel, grid=(row_count // tile,), in_specs=[part...  11.2 us
    pallas_call x1, Pallas kernels, body(): pl.pallas_call(join_kernel, out_shape=[struct(row_count, share), struct(2...  10.8 us
  transfers between devices with their start and end apart: 3, of which 2 were waited for; matrix products, arithmetic and copies ran while one was open for 0% of the time, Pallas kernels for 10%

profile of v7, /device:TPU:0, one launch (start us, length us, event | category | flops | bytes accessed | tf_op | source)
XLA Modules:
  0.0 138.5 jit_solution(4124822640664789905)
XLA Ops:
  0.0 13.3 %forward_x.1 = (f32[1024,1024]{1,0:T(8,128)}, f32[1024,1024]{1,0:T(8,128)}) custom-call(f32[256,4,2048]{2,1,0:T(4,128)} %x_ref.1, s32[32,4,32]{2,1,0:T(4,128)} %solid_ref.1, f32[8,256,256]{2,1,0:T(8,128)} %constant.6.clone.table_ref), custom_call_target="tpu_custom_call" | custom-call | flops 3221225472 | bytes 16777216 | tf_op jit(solution)/shard_map/forward_x/pallas_call | solution.py:652
  13.3 0.4 collective-permute-start
  13.7 13.8 %levels.1 = (bf16[256,256]{1,0:T(8,128)(2,1)}, bf16[256,256]{1,0:T(8,128)(2,1)}, bf16[256,256]{1,0:T(8,128)(2,1)}, bf16[256,256]{1,0:T(8,128)(2,1)}, bf16[64,512...) custom-call(f32[17]{0:T(128)} %couplings_ref.3, ...), custom_call_target="tpu_custom_call" | custom-call | tf_op jit(solution)/shard_map/levels/pallas_call | solution.py:673
  27.5 0.0 collective-permute-done.refs_1_
  27.5 0.0 copy-start.2
  27.5 0.0 copy-start.4
  27.5 0.0 copy-start.5
  27.5 23.4 %to_modes.1 = (f32[2048,1024]{1,0:T(8,128)}, f32[2,8,1024]{2,1,0:T(8,128)}) custom-call(f32[1024,1024]{1,0:T(8,128)} %get-tuple-element.28.refs_0_, f32[1024,1024]{1,0:T(8,128)} %collective-permute-done.refs_1_, bf16[256,256]{1,0:T(8,128)(2,1)} %get-tuple-element.30.refs_2_, bf16[256,256]{1,0:T(8,128)(2,1)} %get-tuple-element.31.refs_3_, ...), custom_call_target="tpu_custom_call" | custom-call | flops 3221225472 | bytes 16777216 | tf_op jit(solution)/shard_map/to_modes/pallas_call | solution.py:700
  51.0 0.0 copy-done.2
  51.0 0.0 copy-done.4
  51.0 0.0 copy-done.5
  51.0 0.0 copy-start
  51.0 0.8 copy-done
  51.9 0.0 copy-start.3
  51.9 0.0 copy-start.7
  51.9 0.0 copy-start.8
  51.9 0.0 copy-start.9
  51.9 0.0 copy-start.1
  51.9 0.0 copy-start.6
  51.9 8.4 %interface.1 = (f32[256,512]{1,0:T(8,128)S(1)}, f32[256,512]{1,0:T(8,128)S(1)}) custom-call(f32[2048,1024]{1,0:T(8,128)} %get-tuple-element.33.modes_ref, bf16[64,512]{1,0:T(8,128)(2,1)S(1)} %copy-done.4, bf16[64,512]{1,0:T(8,128)(2,1)S(1)} %copy-done.5, f32[8,1024]{1,0:T(8,128)S(1)} %copy-done.2, f32[2,8,1024]{2,1,0:T(8,128)S(1)} %copy-done), custom_call_target="tpu_custom_call" | custom-call | flops 402653184 | bytes 10485760 | tf_op jit(solution)/shard_map/interface/pallas_call | solution.py:712
  60.3 1.6 %collective-permute-start.1 = (f32[256,512]{1,0:T(8,128)S(1)}, f32[256,512]{1,0:T(8,128)S(1)}, u32[]{:S(2)}, u32[]{:S(2)}) collective-permute-start(f32[256,512]{1,0:T(8,128)S(1)} %get-tuple-element.38), channel_id=1, source_target_pairs={{0,2},{1,3},{2,0},{3,1},{4,6},{5,7},{6,4},{7,5},{8,10},{9,11},{10,... | collective-permute-start | bytes 1572872 | tf_op jit(solution)/shard_map/ppermute | solution.py:641
  61.9 9.1 %collective-permute-done.1.other_ref = f32[256,512]{1,0:T(8,128)S(1)} collective-permute-done((f32[256,512]{1,0:T(8,128)S(1)}, f32[256,512]{1,0:T(8,128)S(1)}, u32[]{:S(2)}, u32[]{:S(2)}) %collective-permute-start.1) | collective-permute-done | bytes 524320 | tf_op jit(solution)/shard_map/ppermute | solution.py:641
  71.0 0.0 copy-done.3
  71.0 12.0 %plane_sum.1 = (f32[256,512]{1,0:T(8,128)S(1)}, f32[2,16,512]{2,1,0:T(8,128)S(1)}) custom-call(f32[256,512]{1,0:T(8,128)S(1)} %get-tuple-element.37.own_ref, f32[256,512]{1,0:T(8,128)S(1)} %collective-permute-done.1.other_ref, f32[16,512]{1,0:T(8,128)S(1)} %copy-done.3), custom_call_target="tpu_custom_call" | custom-call | tf_op jit(solution)/shard_map/plane_sum/pallas_call | solution.py:724
  83.0 0.0 copy-done.7
  83.0 0.0 copy-done.8
  83.0 0.0 copy-done.9
  83.0 5.8 %couple.1.own_ref = f32[256,512]{1,0:T(8,128)S(1)} custom-call(f32[256,512]{1,0:T(8,128)S(1)} %get-tuple-element.40.plane_ref.again_ref, f32[256,512]{1,0:T(8,128)S(1)} %get-tuple-element.40.plane_ref.again_ref, bf16[32,512]{1,0:T(8,128)(2,1)S(1)} %copy-done.7, bf16[32,512]{1,0:T(8,128)(2,1)S(1)} %copy-done.8, f32[16,512]{1,0:T(8,128)S(1)} %copy-done.3, ...), custom_call_target="tpu_custom_call" | custom-call | flops 402653184 | bytes 4194304 | tf_op jit(solution)/shard_map/couple/pallas_call | solution.py:732
  88.8 1.5 %collective-permute-start.2 = (f32[256,512]{1,0:T(8,128)S(1)}, f32[256,512]{1,0:T(8,128)S(1)}, u32[]{:S(2)}, u32[]{:S(2)}) collective-permute-start(f32[256,512]{1,0:T(8,128)S(1)} %couple.1.own_ref), channel_id=1, source_target_pairs={{0,2},{1,3},{2,0},{3,1},{4,6},{5,7},{6,4},{7,5},{8,10},{9,11},{10,... | collective-permute-start | bytes 1572872 | tf_op jit(solution)/shard_map/ppermute | solution.py:641
  90.3 9.3 %collective-permute-done.2.other_ref = f32[256,512]{1,0:T(8,128)S(1)} collective-permute-done((f32[256,512]{1,0:T(8,128)S(1)}, f32[256,512]{1,0:T(8,128)S(1)}, u32[]{:S(2)}, u32[]{:S(2)}) %collective-permute-start.2) | collective-permute-done | bytes 524320 | tf_op jit(solution)/shard_map/ppermute | solution.py:641
  99.6 0.0 copy-done.1
  99.6 0.0 copy-done.6
  99.6 10.8 %plane_join.1 = (f32[256,1024]{1,0:T(8,128)S(1)}, f32[2,8,1024]{2,1,0:T(8,128)S(1)}) custom-call(f32[256,512]{1,0:T(8,128)S(1)} %couple.1.own_ref, f32[256,512]{1,0:T(8,128)S(1)} %collective-permute-done.2.other_ref, f32[8,1024]{1,0:T(8,128)S(1)} %copy-done.2, f32[8,1024]{1,0:T(8,128)S(1)} %copy-done.6, f32[2,8,1024]{2,1,0:T(8,128)S(1)} %copy-done.1), custom_call_target="tpu_custom_call" | custom-call | tf_op jit(solution)/shard_map/plane_join/pallas_call | solution.py:752
  110.4 0.0 copy-start.10
  110.4 1.0 copy-done.10
  111.3 0.0 copy-start.11
  111.3 0.6 copy-done.11
  112.0 15.4 %from_modes.1 = (f32[1024,1024]{1,0:T(8,128)}, f32[1024,1024]{1,0:T(8,128)}) custom-call(f32[2048,1024]{1,0:T(8,128)} %get-tuple-element.33.modes_ref, f32[256,1024]{1,0:T(8,128)} %copy-done.10, f32[8,1024]{1,0:T(8,128)} %get-tuple-element.44.weight_ref, bf16[256,256]{1,0:T(8,128)(2,1)} %get-tuple-element.46.high_ref, ...), custom_call_target="tpu_custom_call" | custom-call | flops 3221225472 | bytes 16777216 | tf_op jit(solution)/shard_map/from_modes/pallas_call | solution.py:765
  127.4 11.2 %backward_x.1 = f32[256,4,2048]{2,1,0:T(4,128)} custom-call(f32[1024,1024]{1,0:T(8,128)} %get-tuple-element.49.refs_0_, f32[1024,1024]{1,0:T(8,128)} %get-tuple-element.50.refs_1_, f32[8,256,256]{2,1,0:T(8,128)} %constant.8.clone.refs_2_), custom_call_target="tpu_custom_call" | custom-call | flops 3221225472 | bytes 16777216 | tf_op jit(solution)/shard_map/backward_x/pallas_call | solution.py:778
Async XLA Ops:
  13.3 14.3 %collective-permute-start = (f32[1024,1024]{1,0:T(8,128)}, f32[1024,1024]{1,0:T(8,128)}, u32[]{:S(2)}, u32[]{:S(2)}) collective-permute-start(f32[1024,1024]{1,0:T(8,128)} %get-tuple-element.29), channel_id=1, source_target_pairs={{0,1},{1,0},{2,3},{3,2},{4,5},{5,4},{6,7},{7,6},{8,9},{9,8},{10,11... | collective-permute-start | bytes 12582920 | tf_op jit(solution)/shard_map/ppermute | solution.py:638
  27.5 23.5 %copy-start.2 = (f32[8,1024]{1,0:T(8,128)S(1)}, f32[8,1024]{1,0:T(8,128)}, u32[]{:S(2)}) copy-start(f32[8,1024]{1,0:T(8,128)} %get-tuple-element.32.refs_4_.ratio_ref) | copy-start | bytes 98308
  27.5 23.5 %copy-start.4 = (bf16[64,512]{1,0:T(8,128)(2,1)S(1)}, bf16[64,512]{1,0:T(8,128)(2,1)}, u32[]{:S(2)}) copy-start(bf16[64,512]{1,0:T(8,128)(2,1)} %get-tuple-element.34.high_ref) | copy-start | bytes 196612
  27.5 23.5 %copy-start.5 = (bf16[64,512]{1,0:T(8,128)(2,1)S(1)}, bf16[64,512]{1,0:T(8,128)(2,1)}, u32[]{:S(2)}) copy-start(bf16[64,512]{1,0:T(8,128)(2,1)} %get-tuple-element.35.low_ref) | copy-start | bytes 196612
  51.0 0.8 copy-start
  51.9 19.2 %copy-start.3 = (f32[16,512]{1,0:T(8,128)S(1)}, f32[16,512]{1,0:T(8,128)}, u32[]{:S(2)}) copy-start(f32[16,512]{1,0:T(8,128)} %get-tuple-element.39.ratio_ref) | copy-start | bytes 98308
  51.9 31.1 %copy-start.7 = (bf16[32,512]{1,0:T(8,128)(2,1)S(1)}, bf16[32,512]{1,0:T(8,128)(2,1)}, u32[]{:S(2)}) copy-start(bf16[32,512]{1,0:T(8,128)(2,1)} %get-tuple-element.41.high_ref) | copy-start | bytes 98308
  51.9 31.1 %copy-start.8 = (bf16[32,512]{1,0:T(8,128)(2,1)S(1)}, bf16[32,512]{1,0:T(8,128)(2,1)}, u32[]{:S(2)}) copy-start(bf16[32,512]{1,0:T(8,128)(2,1)} %get-tuple-element.42.low_ref) | copy-start | bytes 98308
  51.9 31.2 %copy-start.9 = (f32[17]{0:T(128)S(1)}, f32[17]{0:T(128)}, u32[]{:S(2)}) copy-start(f32[17]{0:T(128)} %couplings_ref.3) | copy-start | bytes 208
  51.9 47.7 %copy-start.1 = (f32[2,8,1024]{2,1,0:T(8,128)S(1)}, f32[2,8,1024]{2,1,0:T(8,128)}, u32[]{:S(2)}) copy-start(f32[2,8,1024]{2,1,0:T(8,128)} %get-tuple-element.36.edge_ref.known_ref) | copy-start | bytes 196612
  51.9 47.7 %copy-start.6 = (f32[8,1024]{1,0:T(8,128)S(1)}, f32[8,1024]{1,0:T(8,128)}, u32[]{:S(2)}) copy-start(f32[8,1024]{1,0:T(8,128)} %get-tuple-element.44.weight_ref) | copy-start | bytes 98308
  60.3 10.7 %collective-permute-start.1 = (f32[256,512]{1,0:T(8,128)S(1)}, f32[256,512]{1,0:T(8,128)S(1)}, u32[]{:S(2)}, u32[]{:S(2)}) collective-permute-start(f32[256,512]{1,0:T(8,128)S(1)} %get-tuple-element.38), channel_id=1, source_target_pairs={{0,2},{1,3},{2,0},{3,1},{4,6},{5,7},{6,4},{7,5},{8,10},{9,11},{10,... | collective-permute-start | bytes 1572872 | tf_op jit(solution)/shard_map/ppermute | solution.py:641
  88.8 10.7 %collective-permute-start.2 = (f32[256,512]{1,0:T(8,128)S(1)}, f32[256,512]{1,0:T(8,128)S(1)}, u32[]{:S(2)}, u32[]{:S(2)}) collective-permute-start(f32[256,512]{1,0:T(8,128)S(1)} %couple.1.own_ref), channel_id=1, source_target_pairs={{0,2},{1,3},{2,0},{3,1},{4,6},{5,7},{6,4},{7,5},{8,10},{9,11},{10,... | collective-permute-start | bytes 1572872 | tf_op jit(solution)/shard_map/ppermute | solution.py:641
  110.4 1.0 copy-start.10
  111.3 0.6 copy-start.11
